TPU v7x, 32 devices: a whole 2x2x4 slice. The times are simulated.
32 devices in a mesh: dp: 8 (over y, x, core), tensor: 4 (over z).
Axes of the slice: x: 2, y: 2, z: 4, core: 2. Of those that a mesh axis runs over, the one named last changes fastest.
Arguments:
- tokens: bfloat16 [36928, 1024], P(('dp', 'tensor')), may hold values from -6 to 6
- cotangent: bfloat16 [36928, 1024], P(('dp', 'tensor')), may hold values from -14 to 14
- attn_master: float32 [1024, 4, 1024], P('dp', None, 'tensor'), may hold values from -2 to 2
- attn_first: float32 [1024, 4, 1024], P('dp', None, 'tensor'), may hold values from -0.00036621094 to 0.00036621094
- attn_second: float32 [1024, 4, 1024], P('dp', None, 'tensor'), may hold values from 2.9701488e-09 to 1.1768514e-08
- attn_ema: float32 [1024, 4, 1024], P('dp', None, 'tensor'), may hold values from -0.1875 to 0.1875
- mlp_master: float32 [1024, 2, 4096], P('dp', None, 'tensor'), may hold values from -0.1875 to 0.1875
- mlp_first: float32 [1024, 2, 4096], P('dp', None, 'tensor'), may hold values from -0.00036621094 to 0.00036621094
- mlp_second: float32 [1024, 2, 4096], P('dp', None, 'tensor'), may hold values from 2.9701488e-09 to 1.1768514e-08
- mlp_ema: float32 [1024, 2, 4096], P('dp', None, 'tensor'), may hold values from -0.1875 to 0.1875
- msg_master: float32 [1024, 5, 1024], P('dp'), may hold values from -0.1875 to 0.1875
- msg_first: float32 [1024, 5, 1024], P('dp'), may hold values from -4.5776367e-05 to 4.5776367e-05
- msg_second: float32 [1024, 5, 1024], P('dp'), may hold values from 4.1180573e-11 to 1.631683e-10
- msg_ema: float32 [1024, 5, 1024], P('dp'), may hold values from -0.1875 to 0.1875
- vec_master: float32 [1024, 18], P('dp'), may hold values from -3 to 3
- vec_first: float32 [1024, 18], P('dp'), may hold values from -0.0014648438 to 0.0014648438
- vec_second: float32 [1024, 18], P('dp'), may hold values from 4.7074057e-08 to 1.9053785e-07
- vec_ema: float32 [1024, 18], P('dp'), may hold values from 0.5 to 1.5
Outputs:
- block_output: float32 [36928, 1024], P(('dp', 'tensor'))
- input_grad: float32 [36928, 1024], P(('dp', 'tensor'))
- grad_norm: float32 [], replicated
- attn_grad: float32 [1024, 4, 1024], P('dp', None, 'tensor')
- attn_first_new: float32 [1024, 4, 1024], P('dp', None, 'tensor')
- attn_second_new: float32 [1024, 4, 1024], P('dp', None, 'tensor')
- attn_weight: float32 [1024, 4, 1024], P('dp', None, 'tensor')
- attn_average: float32 [1024, 4, 1024], P('dp', None, 'tensor')
- mlp_grad: float32 [1024, 2, 4096], P('dp', None, 'tensor')
- mlp_first_new: float32 [1024, 2, 4096], P('dp', None, 'tensor')
- mlp_second_new: float32 [1024, 2, 4096], P('dp', None, 'tensor')
- mlp_weight: float32 [1024, 2, 4096], P('dp', None, 'tensor')
- mlp_average: float32 [1024, 2, 4096], P('dp', None, 'tensor')
- msg_grad: float32 [1024, 5, 1024], P('dp')
- msg_first_new: float32 [1024, 5, 1024], P('dp')
- msg_second_new: float32 [1024, 5, 1024], P('dp')
- msg_weight: float32 [1024, 5, 1024], P('dp')
- msg_average: float32 [1024, 5, 1024], P('dp')
- vec_grad: float32 [1024, 18], P('dp')
- vec_first_new: float32 [1024, 18], P('dp')
- vec_second_new: float32 [1024, 18], P('dp')
- vec_weight: float32 [1024, 18], P('dp')
- vec_average: float32 [1024, 18], P('dp')
All inputs are finite; a program needn't handle non-finite values.
Results may differ from a plain program's by a relative error of at most 0.025.
The roundings to bfloat16 on the way count: a program that leaves them out, or rounds other values in their place, can miss the bound.
Values may be sent and summed in bfloat16 or wider, within the bound.
No kernel may reach another device: no remote copies, remote signals or barrier semaphores. Data moves between devices by JAX's collectives and lax.ppermute only.
A program may use at most 320 MiB of HBM per device.

v0:
```python
import jax
import jax.numpy as jnp
from jax import lax
from jax.sharding import PartitionSpec as P

D = 1024
HEADS = 16
HEAD = 64
FF = 4096
PATCHES = 577
FRAMES = 8
STEP = 10


norm_eps = 1e-05
beta_one = 0.9
beta_two = 0.95
adam_eps = 1e-08
decay_mat = 0.05
ema_keep = 0.7
clip_limit = 1.0
rate_mat = 0.02
rate_vec = 0.4
highest = lax.Precision.HIGHEST


def norm_rows(values, gain_row, shift_row):
    centre = values - jnp.mean(values, -1, keepdims=True)
    spread = jnp.mean(centre * centre, -1, keepdims=True)
    inverse = lax.rsqrt(spread + norm_eps)
    scaled = centre * inverse
    return (scaled * gain_row + shift_row, scaled, inverse)


def norm_back(gradient, scaled, inverse, gain_row):
    inner = gradient * gain_row
    return inverse * (
        inner
        - jnp.mean(inner, -1, keepdims=True)
        - scaled * jnp.mean(inner * scaled, -1, keepdims=True)
    )


def gelu_slope(hidden_pre):
    sigma = jax.nn.sigmoid(1.702 * hidden_pre)
    return sigma + 1.702 * hidden_pre * sigma * (1.0 - sigma)


def dot_plain(left_side, right_side):
    return jnp.dot(left_side, right_side, preferred_element_type=jnp.float32)


def dot_rows(left_side, right_side):
    return lax.dot_general(
        left_side, right_side, (((1,), (1,)), ((), ())), preferred_element_type=jnp.float32
    )


def dot_cols(left_side, right_side):
    return lax.dot_general(
        left_side, right_side, (((0,), (0,)), ((), ())), preferred_element_type=jnp.float32
    )


def to_heads(rows_in, head_count):
    shaped = rows_in.reshape(rows_in.shape[:-1] + (head_count, HEAD))
    return jnp.moveaxis(shaped, -2, -3)


def from_heads(values):
    moved_axes = jnp.moveaxis(values, -3, -2)
    return moved_axes.reshape(moved_axes.shape[:-2] + (moved_axes.shape[-2] * HEAD,))


def attend_forward(queries, key_rows, value_rows):
    scores = jnp.einsum(
        "...qe,...ke->...qk", queries, key_rows, preferred_element_type=jnp.float32
    ) * HEAD ** (-0.5)
    highest_score = jnp.max(scores, -1, keepdims=True)
    shifted = jnp.exp(scores - highest_score)
    row_total = jnp.sum(shifted, -1, keepdims=True)
    probability = (shifted / row_total).astype(jnp.bfloat16)
    output = jnp.einsum(
        "...qk,...ke->...qe", probability, value_rows, preferred_element_type=jnp.float32
    )
    return (output, highest_score + jnp.log(row_total))


def attend_backward(queries, key_rows, value_rows, log_total, grad_out):
    scores = jnp.einsum(
        "...qe,...ke->...qk", queries, key_rows, preferred_element_type=jnp.float32
    ) * HEAD ** (-0.5)
    probability = jnp.exp(scores - log_total)
    grad_prob = jnp.einsum(
        "...qe,...ke->...qk", grad_out, value_rows, preferred_element_type=jnp.float32
    )
    grad_scores = (
        probability * (grad_prob - jnp.sum(grad_prob * probability, -1, keepdims=True))
    ).astype(jnp.bfloat16)
    grad_query = jnp.einsum(
        "...qk,...ke->...qe", grad_scores, key_rows, preferred_element_type=jnp.float32
    ) * HEAD ** (-0.5)
    grad_keys = jnp.einsum(
        "...qk,...qe->...ke", grad_scores, queries, preferred_element_type=jnp.float32
    ) * HEAD ** (-0.5)
    grad_values = jnp.einsum(
        "...qk,...qe->...ke",
        probability.astype(jnp.bfloat16),
        grad_out,
        preferred_element_type=jnp.float32,
    )
    return (grad_query, grad_keys, grad_values)


def adam_step(weight, first_moment, second_moment, gradient, factor, step_rate, decay_rate):
    clipped = gradient * factor
    first_new = beta_one * first_moment + (1.0 - beta_one) * clipped
    second_new = beta_two * second_moment + (1.0 - beta_two) * clipped * clipped
    update = (
        first_new
        / (1.0 - beta_one**STEP)
        / (jnp.sqrt(second_new / (1.0 - beta_two**STEP)) + adam_eps)
    )
    weight_new = weight - step_rate * (update + decay_rate * weight)
    return (first_new, second_new, weight_new)


def forward_frame(inputs):
    return attend_forward(inputs[0], inputs[1], inputs[2])


def backward_frame(inputs):
    return attend_backward(inputs[0], inputs[1], inputs[2], inputs[3], inputs[4])


def on_device(
    tokens,
    cotangent,
    attn_master,
    attn_first,
    attn_second,
    attn_ema,
    mlp_master,
    mlp_first,
    mlp_second,
    mlp_ema,
    msg_master,
    msg_first,
    msg_second,
    msg_ema,
    vec_master,
    vec_first,
    vec_second,
    vec_ema,
):
    tensor_index = lax.axis_index("tensor")
    tensor_count = lax.axis_size("tensor")
    attn_w, mlp_w, msg_w, vec_low = (
        lax.all_gather(attn_master.astype(jnp.bfloat16), "dp", axis=0, tiled=True),
        lax.all_gather(mlp_master.astype(jnp.bfloat16), "dp", axis=0, tiled=True),
        lax.all_gather(msg_master.astype(jnp.bfloat16), "dp", axis=0, tiled=True),
        lax.all_gather(vec_master.astype(jnp.bfloat16), "dp", axis=0, tiled=True),
    )
    vectors = vec_low.astype(jnp.float32)
    local_ff = mlp_w.shape[2]
    own_rows = tokens.shape[0]
    row_start = tensor_index * own_rows
    ff_bias = vectors[:, 14:].T.reshape(FF)
    work_rows = lax.all_gather(tokens, "tensor", axis=0, tiled=True)
    class_rows = work_rows.reshape(work_rows.shape[0] // PATCHES, PATCHES, D)[:, 0]
    column_start = tensor_index * attn_w.shape[2]
    local_width = attn_w.shape[2]
    local_heads = local_width // HEAD
    work_count = work_rows.shape[0]
    work_frames = work_count // PATCHES
    frame_count = class_rows.shape[0]
    video_count = frame_count // FRAMES
    query_bias = lax.dynamic_slice_in_dim(vectors[:, 10], column_start, local_width)
    value_bias = lax.dynamic_slice_in_dim(vectors[:, 11], column_start, local_width)
    first_msg = dot_plain(class_rows, msg_w[:, 0]) + vectors[:, 6]
    normed_msg, scaled_msg, inverse_msg = norm_rows(first_msg, vectors[:, 4], vectors[:, 5])
    normed_msg = normed_msg.astype(jnp.bfloat16)
    msg_query = (dot_plain(normed_msg, msg_w[:, 1]) + vectors[:, 7]).astype(jnp.bfloat16)
    msg_keys = dot_plain(normed_msg, msg_w[:, 2]).astype(jnp.bfloat16)
    msg_values = (dot_plain(normed_msg, msg_w[:, 3]) + vectors[:, 8]).astype(jnp.bfloat16)
    query_heads = to_heads(msg_query.reshape(video_count, FRAMES, D), HEADS)
    keys_heads = to_heads(msg_keys.reshape(video_count, FRAMES, D), HEADS)
    values_heads = to_heads(msg_values.reshape(video_count, FRAMES, D), HEADS)
    msg_out, msg_total = attend_forward(query_heads, keys_heads, values_heads)
    msg_mixed = from_heads(msg_out).reshape(frame_count, D).astype(jnp.bfloat16)
    message = first_msg + dot_plain(msg_mixed, msg_w[:, 4]) + vectors[:, 9]
    normed_rows, scaled_rows, inverse_rows = norm_rows(
        work_rows.astype(jnp.float32), vectors[:, 0], vectors[:, 1]
    )
    normed_rows = normed_rows.astype(jnp.bfloat16)
    normed_tok, scaled_tok, inverse_tok = norm_rows(message, vectors[:, 0], vectors[:, 1])
    normed_tok = normed_tok.astype(jnp.bfloat16)
    proj_w = attn_w[:, :3].reshape(D, 3 * local_width)
    proj_bias = jnp.concatenate([query_bias, jnp.zeros_like(query_bias), value_bias])
    qkv_rows = (dot_plain(normed_rows, proj_w) + proj_bias).astype(jnp.bfloat16)
    qkv_tok = (dot_plain(normed_tok, proj_w) + proj_bias).astype(jnp.bfloat16)

    def frame_split(source, slot_index, length):
        part_rows = source[:, slot_index * local_width : (slot_index + 1) * local_width]
        return to_heads(part_rows.reshape(work_frames, length, local_width), local_heads)

    queries = frame_split(qkv_rows, 0, PATCHES)
    key_rows = jnp.concatenate(
        [frame_split(qkv_rows, 1, PATCHES), frame_split(qkv_tok, 1, 1)], axis=2
    )
    value_rows = jnp.concatenate(
        [frame_split(qkv_rows, 2, PATCHES), frame_split(qkv_tok, 2, 1)], axis=2
    )
    attended, log_totals = lax.map(forward_frame, (queries, key_rows, value_rows))
    attended_rows = from_heads(attended).reshape(work_count, local_width).astype(jnp.bfloat16)
    out_w = attn_w[:, 3]
    attention_out = lax.psum_scatter(
        dot_rows(attended_rows, out_w), "tensor", scatter_dimension=0, tiled=True
    )
    middle = tokens.astype(jnp.float32) + attention_out + vectors[:, 12]
    middle_low = middle.astype(jnp.bfloat16)
    fc_w = mlp_w[:, 0]
    down_w = mlp_w[:, 1]
    fc_bias = lax.dynamic_slice_in_dim(ff_bias, tensor_index * local_ff, local_ff)
    mid_rows = lax.all_gather(middle_low, "tensor", axis=0, tiled=True)
    normed_mid, scaled_mid, inverse_mid = norm_rows(
        mid_rows.astype(jnp.float32), vectors[:, 2], vectors[:, 3]
    )
    normed_mid = normed_mid.astype(jnp.bfloat16)
    hidden_pre = dot_plain(normed_mid, fc_w) + fc_bias
    hidden_act = (hidden_pre * jax.nn.sigmoid(1.702 * hidden_pre)).astype(jnp.bfloat16)
    block_output = (
        middle
        + lax.psum_scatter(
            dot_rows(hidden_act, down_w).astype(jnp.bfloat16),
            "tensor",
            scatter_dimension=0,
            tiled=True,
        ).astype(jnp.float32)
        + vectors[:, 13]
    )
    grad_rows = lax.all_gather(cotangent, "tensor", axis=0, tiled=True)
    grad_act = dot_plain(grad_rows, down_w)
    grad_down = dot_cols(grad_rows, hidden_act)
    grad_pre = (grad_act * gelu_slope(hidden_pre)).astype(jnp.bfloat16)
    grad_fc = dot_cols(normed_mid, grad_pre)
    fc_bias_grad = lax.dynamic_update_slice_in_dim(
        jnp.zeros((FF,), jnp.float32),
        jnp.sum(grad_pre.astype(jnp.float32), 0),
        tensor_index * local_ff,
        0,
    )
    grad_mid_in = lax.psum_scatter(
        dot_rows(grad_pre, fc_w), "tensor", scatter_dimension=0, tiled=True
    )
    mlp_grad_local = jnp.stack([grad_fc, grad_down], 1)
    own_scaled = lax.dynamic_slice_in_dim(scaled_mid, row_start, own_rows, 0)
    own_inverse = lax.dynamic_slice_in_dim(inverse_mid, row_start, own_rows, 0)
    back_mid = norm_back(grad_mid_in, own_scaled, own_inverse, vectors[:, 2])
    gain_two = jnp.sum(grad_mid_in * own_scaled, 0)
    shift_two = jnp.sum(grad_mid_in, 0)
    middle_grad = (cotangent.astype(jnp.float32) + back_mid).astype(jnp.bfloat16)
    grad_mid_rows = lax.all_gather(middle_grad, "tensor", axis=0, tiled=True)
    grad_attended = dot_plain(grad_mid_rows, out_w).astype(jnp.bfloat16)
    grad_out_w = dot_cols(grad_mid_rows, attended_rows)
    out_bias_grad = jnp.sum(middle_grad.astype(jnp.float32), 0)
    grad_frames = to_heads(grad_attended.reshape(work_frames, PATCHES, local_width), local_heads)
    grad_query, grad_keys, grad_values = lax.map(
        backward_frame, (queries, key_rows, value_rows, log_totals, grad_frames)
    )
    grad_qkv = (
        jnp.concatenate(
            [
                from_heads(grad_query),
                from_heads(grad_keys[:, :, :PATCHES]),
                from_heads(grad_values[:, :, :PATCHES]),
            ],
            -1,
        )
        .reshape(work_count, 3 * local_width)
        .astype(jnp.bfloat16)
    )
    grad_tok = jnp.concatenate(
        [
            jnp.zeros((work_frames, local_width), jnp.float32),
            from_heads(grad_keys[:, :, PATCHES:]).reshape(work_frames, local_width),
            from_heads(grad_values[:, :, PATCHES:]).reshape(work_frames, local_width),
        ],
        -1,
    ).astype(jnp.bfloat16)
    grad_proj = dot_cols(normed_rows, grad_qkv) + dot_cols(normed_tok, grad_tok)
    query_bias_grad = jnp.sum(grad_qkv[:, :local_width].astype(jnp.float32), 0)
    value_bias_grad = jnp.sum(grad_qkv[:, 2 * local_width :].astype(jnp.float32), 0) + jnp.sum(
        grad_tok[:, 2 * local_width :].astype(jnp.float32), 0
    )
    grad_norm_rows = dot_rows(grad_qkv, proj_w)
    grad_norm_tok = dot_rows(grad_tok, proj_w)
    gain_one = jnp.sum(grad_norm_rows * scaled_rows, 0) + jnp.sum(grad_norm_tok * scaled_tok, 0)
    shift_one = jnp.sum(grad_norm_rows, 0) + jnp.sum(grad_norm_tok, 0)
    back_rows = norm_back(grad_norm_rows, scaled_rows, inverse_rows, vectors[:, 0])
    back_tok = norm_back(grad_norm_tok, scaled_tok, inverse_tok, vectors[:, 0])
    zero_row = jnp.zeros((D,), jnp.float32)
    placed_query = lax.dynamic_update_slice_in_dim(zero_row, query_bias_grad, column_start, 0)
    placed_value = lax.dynamic_update_slice_in_dim(zero_row, value_bias_grad, column_start, 0)
    vector_part = jnp.concatenate(
        [
            jnp.stack(
                [
                    gain_one,
                    shift_one,
                    gain_two,
                    shift_two,
                    zero_row,
                    zero_row,
                    zero_row,
                    zero_row,
                    zero_row,
                    zero_row,
                    placed_query,
                    placed_value,
                    out_bias_grad,
                    jnp.sum(cotangent.astype(jnp.float32), 0),
                ]
            ),
            fc_bias_grad.reshape(FF // D, D),
        ],
        0,
    )
    vector_count = vector_part.shape[0]
    attn_grad_full = jnp.concatenate([grad_proj.reshape(D, 3, local_width), grad_out_w[:, None]], 1)
    extended = jnp.concatenate(
        [
            back_rows.reshape(tensor_count, own_rows, D),
            jnp.broadcast_to(back_tok[None], (tensor_count, frame_count, D)),
            jnp.broadcast_to(vector_part[None], (tensor_count, vector_count, D)),
        ],
        1,
    ).reshape(-1, D)
    summed = lax.psum_scatter(extended, "tensor", scatter_dimension=0, tiled=True)
    own_back = summed[:own_rows]
    message_grad = summed[own_rows : own_rows + frame_count]
    vector_sum = summed[own_rows + frame_count :]
    msg_grad_low = message_grad.astype(jnp.bfloat16)
    grad_mixed = dot_rows(msg_grad_low, msg_w[:, 4]).astype(jnp.bfloat16)
    grad_msg_out = dot_cols(msg_mixed, msg_grad_low)
    grad_mixed_heads = to_heads(grad_mixed.reshape(video_count, FRAMES, D), HEADS)
    msg_dq, msg_dk, msg_dv = attend_backward(
        query_heads, keys_heads, values_heads, msg_total, grad_mixed_heads
    )
    msg_dq = from_heads(msg_dq).reshape(frame_count, D).astype(jnp.bfloat16)
    msg_dk = from_heads(msg_dk).reshape(frame_count, D).astype(jnp.bfloat16)
    msg_dv = from_heads(msg_dv).reshape(frame_count, D).astype(jnp.bfloat16)
    grad_msg_query = dot_cols(normed_msg, msg_dq)
    grad_msg_keys = dot_cols(normed_msg, msg_dk)
    grad_msg_values = dot_cols(normed_msg, msg_dv)
    grad_normed_msg = (
        dot_rows(msg_dq, msg_w[:, 1])
        + dot_rows(msg_dk, msg_w[:, 2])
        + dot_rows(msg_dv, msg_w[:, 3])
    )
    back_first = norm_back(grad_normed_msg, scaled_msg, inverse_msg, vectors[:, 4])
    grad_first = (msg_grad_low.astype(jnp.float32) + back_first).astype(jnp.bfloat16)
    grad_msg_fc = dot_cols(class_rows, grad_first)
    grad_class = dot_rows(grad_first, msg_w[:, 0])
    message_rows = jnp.stack(
        [
            jnp.sum(grad_normed_msg * scaled_msg, 0),
            jnp.sum(grad_normed_msg, 0),
            jnp.sum(grad_first.astype(jnp.float32), 0),
            jnp.sum(msg_dq.astype(jnp.float32), 0),
            jnp.sum(msg_dv.astype(jnp.float32), 0),
            jnp.sum(msg_grad_low.astype(jnp.float32), 0),
        ]
    )
    message_table = jnp.concatenate(
        [
            jnp.zeros((4, D), jnp.float32),
            message_rows,
            jnp.zeros((vector_count - 10, D), jnp.float32),
        ],
        0,
    )
    positions = row_start + lax.iota(jnp.int32, own_rows)
    marks = (
        (positions % PATCHES == 0)[:, None]
        & ((positions // PATCHES)[:, None] == lax.iota(jnp.int32, frame_count)[None, :])
    ).astype(jnp.float32)
    input_grad = (
        middle_grad.astype(jnp.float32) + own_back + jnp.dot(marks, grad_class, precision=highest)
    )
    msg_grad_local = jnp.stack(
        [grad_msg_fc, grad_msg_query, grad_msg_keys, grad_msg_values, grad_msg_out], 1
    )
    vec_grad_local = (vector_sum + message_table).T
    attn_grad, mlp_grad, msg_grad, vec_grad = (
        lax.psum_scatter(
            attn_grad_full.astype(jnp.bfloat16), "dp", scatter_dimension=0, tiled=True
        ).astype(jnp.float32),
        lax.psum_scatter(
            mlp_grad_local.astype(jnp.bfloat16), "dp", scatter_dimension=0, tiled=True
        ).astype(jnp.float32),
        lax.psum_scatter(
            msg_grad_local.astype(jnp.bfloat16), "dp", scatter_dimension=0, tiled=True
        ).astype(jnp.float32),
        lax.psum_scatter(
            vec_grad_local.astype(jnp.bfloat16), "dp", scatter_dimension=0, tiled=True
        ).astype(jnp.float32),
    )
    keep_share = (tensor_index == 0).astype(jnp.float32)
    squares = (
        jnp.sum(attn_grad * attn_grad)
        + jnp.sum(mlp_grad * mlp_grad)
        + keep_share * (jnp.sum(msg_grad * msg_grad) + jnp.sum(vec_grad * vec_grad))
    )
    grad_norm = jnp.sqrt(lax.psum(squares, ("dp", "tensor")))
    factor = clip_limit / jnp.maximum(grad_norm, clip_limit)
    attn_m, attn_s, attn_new = adam_step(
        attn_master, attn_first, attn_second, attn_grad, factor, rate_mat, decay_mat
    )
    mlp_m, mlp_s, mlp_new = adam_step(
        mlp_master, mlp_first, mlp_second, mlp_grad, factor, rate_mat, decay_mat
    )
    msg_m, msg_s, msg_new = adam_step(
        msg_master, msg_first, msg_second, msg_grad, factor, rate_mat, decay_mat
    )
    vec_m, vec_s, vec_new = adam_step(
        vec_master, vec_first, vec_second, vec_grad, factor, rate_vec, 0.0
    )
    attn_avg = ema_keep * attn_ema + (1.0 - ema_keep) * attn_new
    mlp_avg = ema_keep * mlp_ema + (1.0 - ema_keep) * mlp_new
    msg_avg = ema_keep * msg_ema + (1.0 - ema_keep) * msg_new
    vec_avg = ema_keep * vec_ema + (1.0 - ema_keep) * vec_new
    return (
        block_output,
        input_grad,
        grad_norm,
        attn_grad,
        attn_m,
        attn_s,
        attn_new,
        attn_avg,
        mlp_grad,
        mlp_m,
        mlp_s,
        mlp_new,
        mlp_avg,
        msg_grad,
        msg_m,
        msg_s,
        msg_new,
        msg_avg,
        vec_grad,
        vec_m,
        vec_s,
        vec_new,
        vec_avg,
    )


def solution(mesh):
    in_specs = (
        P(("dp", "tensor"), None),
        P(("dp", "tensor"), None),
        P("dp", None, "tensor"),
        P("dp", None, "tensor"),
        P("dp", None, "tensor"),
        P("dp", None, "tensor"),
        P("dp", None, "tensor"),
        P("dp", None, "tensor"),
        P("dp", None, "tensor"),
        P("dp", None, "tensor"),
        P("dp", None, None),
        P("dp", None, None),
        P("dp", None, None),
        P("dp", None, None),
        P("dp", None),
        P("dp", None),
        P("dp", None),
        P("dp", None),
    )
    out_specs = (
        P(("dp", "tensor"), None),
        P(("dp", "tensor"), None),
        P(),
        P("dp", None, "tensor"),
        P("dp", None, "tensor"),
        P("dp", None, "tensor"),
        P("dp", None, "tensor"),
        P("dp", None, "tensor"),
        P("dp", None, "tensor"),
        P("dp", None, "tensor"),
        P("dp", None, "tensor"),
        P("dp", None, "tensor"),
        P("dp", None, "tensor"),
        P("dp", None, None),
        P("dp", None, None),
        P("dp", None, None),
        P("dp", None, None),
        P("dp", None, None),
        P("dp", None),
        P("dp", None),
        P("dp", None),
        P("dp", None),
        P("dp", None),
    )
    return jax.shard_map(
        on_device, mesh=mesh, in_specs=in_specs, out_specs=out_specs, check_vma=False
    )
```

profile of v0, /device:TPU:0, one launch (start us, length us, event | category | flops | bytes accessed | tf_op | source)
XLA Modules:
  0.0 2887.7 jit_solution(4785251948555952834)
XLA Ops:
  12.1 10.4 all_gather.25
  23.7 17.7 all-gather.12.cloned.1.call-done
  43.0 167.9 %all-gather.18.cloned.1.call-done = bf16[4,1154,1024]{2,1,0:T(8,128)(2,1)} async-done(((bf16[1,1154,1024]{2,1,0:T(8,128)(2,1)}), bf16[4,1154,1024]{2,1,0:T(8,128)(2,1)}) %all-gather.18.cloned.1.call-update) | async-done | bytes 9453584 | tf_op jit(solution)/shard_map/all_gather | solution.py:169
  210.9 5.0 convert_reduce_fusion.5
  216.0 13.1 reshape.394
  229.1 8.5 multiply_reduce_fusion.5
  237.6 9.8 add_convert_fusion.1
  247.4 3.7 copy-done.19
  251.1 8.1 add_convert_fusion.2
  265.5 4.2 reshape_reshape.29
  271.9 8.4 reshape.373
  281.2 4.4 copy.139
  285.6 6.4 reshape_reshape.30
  292.0 4.3 copy.146
  296.3 6.7 reshape_reshape.34
  329.3 60.8 %while.26 = (s32[]{:T(128)}, bf16[8,4,577,64]{2,3,1,0:T(8,128)(2,1)}, f32[8,4,577,1]{2,1,3,0:T(4,128)}, bf16[8,4,577,64]{2,3,1,0:T(8,128)(2,1)S(1)}, bf16[8,4,57...) while((s32[]{:T(128)}, bf16[8,4,577,64]{2,3,1,0:T(8,128)(2,1)}, ...), condition=%wide.region_11.12_spmd, body=%wide.region_8.11_spmd.sunk | while | flops 353514048 | bytes 17723688 | solution.py:214
  390.1 5.7 copy.151
  395.8 5.7 convert_element_type.254
  401.5 10.9 fusion.97
  412.4 339.3 %fusion = f32[1160,1024]{1,0:T(8,128)} fusion(f32[4616,1024]{1,0:T(8,128)} %fusion.97), kind=kCustom, calls=%all-reduce-scatter | all-reduce-scatter fusion | flops 4751361 | bytes 23659008
  756.2 13.4 concatenate.53
  769.7 4.8 fusion.60
  775.8 10.5 reshape.388
  786.4 156.7 %all-gather.20.cloned.1.call-done = bf16[4,1154,1024]{2,1,0:T(8,128)(2,1)} async-done(((bf16[1,1154,1024]{2,1,0:T(8,128)(2,1)}), bf16[4,1154,1024]{2,1,0:T(8,128)(2,1)}) %all-gather.20.cloned.1.call-update) | async-done | bytes 9453584 | tf_op jit(solution)/shard_map/all_gather | solution.py:225
  943.1 5.1 convert_reduce_fusion.6
  948.3 12.6 reshape.391
  960.9 9.1 multiply_reduce_fusion.4
  970.0 15.7 subtract_multiply_fusion.1
  985.7 22.6 multiply_convert_fusion.2
  1008.3 25.1 convert_reduce_fusion
  1033.4 17.1 fusion.71
  1050.5 317.4 %fusion.2 = f32[1160,1024]{1,0:T(8,128)} fusion(f32[4616,1024]{1,0:T(8,128)} %fusion.71), kind=kCustom, calls=%all-reduce-scatter.2 | all-reduce-scatter fusion | flops 4751361 | bytes 23659008
  1368.9 4.0 collective-permute-start.2
  1375.0 13.4 concatenate.55
  1388.5 6.6 multiply_reduce_fusion.7
  1395.1 6.2 convert_reduce_fusion.1
  1403.1 166.4 %all-gather.24.cloned.1.call-done = bf16[4,1154,1024]{2,1,0:T(8,128)(2,1)} async-done(((bf16[1,1154,1024]{2,1,0:T(8,128)(2,1)}), bf16[4,1154,1024]{2,1,0:T(8,128)(2,1)}) %all-gather.24.cloned.1.call-update) | async-done | bytes 9453584 | tf_op jit(solution)/shard_map/all_gather | solution.py:263
  1569.5 9.8 reshape.390
  1579.3 7.8 convolution_convert_fusion.1
  1590.3 4.2 reshape_reshape.35
  1598.5 119.6 %while.27 = (s32[]{:T(128)}, bf16[8,4,577,64]{2,3,1,0:T(8,128)(2,1)}, bf16[8,4,578,64]{2,3,1,0:T(8,128)(2,1)}, bf16[8,4,578,64]{2,3,1,0:T(8,128)(2,1)}, bf16[8,4...) while((s32[]{:T(128)}, ...), condition=%wide.region_21.22_spmd, body=%wide.region_19.21_spmd.sunk | while | flops 870076928 | bytes 45640560 | solution.py:268
  1728.7 4.4 concatenate.43
  1738.8 5.5 concatenate.44
  1747.3 4.4 concatenate.45
  1757.0 22.5 multiply_reduce_fusion.2
  1779.5 20.5 subtract_multiply_fusion
  1800.0 15.1 reshape.378
  1816.5 51.4 %concatenate.50 = f32[4,1180,1024]{2,1,0:T(8,128)} concatenate(f32[4,1154,1024]{2,1,0:T(8,128)} %reshape.378, f32[4,8,1024]{2,1,0:T(8,128)S(1)} %broadcast_in_dim.41, f32[4,18,1024]{2,1,0:T(8,128)S(1)} %broadcast_in_dim.44), dimensions={1} | concatenate | bytes 38666240 | tf_op jit(solution)/shard_map/concatenate | solution.py:331
  1867.8 16.8 reshape.380
  1885.3 18.5 convert_bitcast_fusion.3
  1903.8 15.8 convert_bitcast_fusion.2
  1923.3 6.5 fusion.72
  1930.6 12.7 fusion.156
  1951.6 575.9 %all-reduce.11.cloned.1.call-done = f32[4720,1024]{1,0:T(8,128)} async-done(((f32[4720,1024]{1,0:T(8,128)}), f32[4720,1024]{1,0:T(8,128)}) %all-reduce.11.cloned.1.call-update) | async-done | bytes 19333136
  2551.6 13.8 copy.205
  2565.4 16.7 convolution_convert_fusion
  2582.1 164.5 %fusion.1 = bf16[1160,1024]{1,0:T(8,128)(2,1)} fusion(bf16[4616,1024]{1,0:T(8,128)(2,1)} %convolution_convert_fusion), kind=kCustom, calls=%all-reduce-scatter.1 | all-reduce-scatter fusion | flops 4751361 | bytes 11829760
  2761.5 12.7 concatenate.54
  2774.2 6.9 add_add_fusion
  2791.8 6.2 convolution_add_fusion
  2805.8 40.0 %psum.7 = f32[]{:T(128)} all-reduce(f32[]{:T(128)S(6)} %add.475), channel_id=1, replica_groups=mesh['dp'=8,'tensor'=4] {'dp','tensor'}, use_global_device_ids=true, to_apply=%region_56.57 | all-reduce | flops 1 | bytes 8 | tf_op jit(solution)/shard_map/psum | solution.py:415
  2846.6 3.9 fusion.92
  2857.7 5.2 multiply_add_fusion
  2874.9 3.7 multiply_add_fusion.2
  (468 shorter events, 352.0 us)
Async XLA Ops:
  7.2 34.2 %all-gather.12.cloned.1.call-start = ((), (), s32[]{:S(2)}) async-start(), calls=%async_computation.3 | async-start | bytes 2359296 | tf_op jit(solution)/shard_map/all_gather | solution.py:159
  9.3 201.6 %all-gather.18.cloned.1.call-start = ((), (), s32[]{:S(2)}) async-start(), calls=%async_computation.7 | async-start | bytes 11878400 | tf_op jit(solution)/shard_map/all_gather | solution.py:169
  10.1 292.9 %all-gather.14.cloned.1.call-start = ((), (), s32[]{:S(2)}) async-start(), calls=%async_computation.4 | async-start | bytes 11796480 | tf_op jit(solution)/shard_map/all_gather | solution.py:161
  11.4 764.4 %all-gather.22.cloned.1.call-start = ((), (), s32[]{:S(2)}) async-start(), calls=%async_computation.9 | async-start | bytes 11878400 | tf_op jit(solution)/shard_map/all_gather | solution.py:242
  12.0 931.1 %all-gather.20.cloned.1.call-start = ((), (), s32[]{:S(2)}) async-start(), calls=%async_computation.8 | async-start | bytes 11878400 | tf_op jit(solution)/shard_map/all_gather | solution.py:225
  23.7 281.7 %copy-start.56 = (f32[1024,1]{0,1:T(1,128)}, f32[1024,1]{0,1:T(1,128)S(1)}, u32[]{:S(2)}) copy-start(f32[1024,1]{0,1:T(1,128)S(1)} %get-tuple-element.296) | copy-start | bytes 12292
  23.7 292.2 %copy-start.42 = (f32[1024,1]{0,1:T(1,128)}, f32[1024,1]{0,1:T(1,128)S(1)}, u32[]{:S(2)}) copy-start(f32[1024,1]{0,1:T(1,128)S(1)} %get-tuple-element.301) | copy-start | bytes 12292
  23.7 292.2 %copy-start.54 = (f32[1024,1]{0,1:T(1,128)}, f32[1024,1]{0,1:T(1,128)S(1)}, u32[]{:S(2)}) copy-start(f32[1024,1]{0,1:T(1,128)S(1)} %get-tuple-element.302) | copy-start | bytes 12292
  23.7 746.0 %copy-start.62 = (f32[1024,1]{0,1:T(1,128)}, f32[1024,1]{0,1:T(1,128)S(1)}, u32[]{:S(2)}) copy-start(f32[1024,1]{0,1:T(1,128)S(1)} %get-tuple-element.292) | copy-start | bytes 12292
  42.9 204.5 %copy-start.6 = (bf16[1024,3,256]{0,2,1:T(8,128)(2,1)}, bf16[1024,3,256]{0,2,1:T(8,128)(2,1)S(1)}, u32[]{:S(2)}) copy-start(bf16[1024,3,256]{0,2,1:T(8,128)(2,1)S(1)} %slice.169) | copy-start | bytes 4718596
  216.0 21.6 copy-start.36
  237.6 9.8 copy-start.44
  281.2 21.8 copy-start.50
  305.1 10.7 copy-start.28
  305.4 12.7 copy-start.32
  307.5 10.6 copy-start.40
  309.7 8.5 copy-start.38
  390.1 11.4 copy-start.1
  412.4 341.5 %copy-start.87 = (u32[32]{0:T(128)S(1)}, u32[32]{0:T(128)}, u32[]{:S(2)}) copy-start(u32[32]{0:T(128)} %constant.193) | copy-start | bytes 388
  752.6 3.6 collective-permute-start
  755.2 14.5 copy-start.2
  774.5 211.2 %all-gather.16.cloned.1.call-start = ((), (), s32[]{:S(2)}) async-start(), calls=%async_computation.5 | async-start | bytes 4718592 | tf_op jit(solution)/shard_map/all_gather | solution.py:160
  775.7 793.8 %all-gather.24.cloned.1.call-start = ((), (), s32[]{:S(2)}) async-start(), calls=%async_computation.10 | async-start | bytes 11878400 | tf_op jit(solution)/shard_map/all_gather | solution.py:263
  970.0 15.7 copy-start.64
  970.0 15.7 copy-start.85
  1368.9 6.2 collective-permute-start.2
  1401.3 1126.2 %all-reduce.11.cloned.1.call-start = ((), (), s32[]{:S(2)}) async-start(), calls=%async_computation.13 | async-start | bytes 38666240
  1735.8 8.5 copy-start.15
  1799.9 15.4 copy-start.7
  1799.9 15.4 copy-start.31
  1799.9 15.4 copy-start.68
  1799.9 15.4 copy-start.75
  1799.9 15.4 copy-start.80
  1800.0 16.1 copy-start.58
  1800.0 16.1 copy-start.70
  1800.0 16.1 copy-start.71
  1800.0 16.1 copy-start.72
  1800.0 16.1 copy-start.73
  1884.7 896.5 %reduce-scatter.14.cloned.1.call-start = ((), (), s32[]{:S(2)}) async-start(), calls=%async_computation.6 | async-start | bytes 4718592 | tf_op jit(solution)/shard_map/reduce_scatter | solution.py:399
  1922.1 863.6 %all-reduce.13.cloned.1.call-start = ((), (), s32[]{:S(2)}) async-start(), calls=%async_computation.14 | async-start | bytes 4194304
  1930.6 12.7 copy-start.55
  1948.1 582.7 %copy-start.27 = (f32[16,8,8]{1,2,0:T(8,128)S(1)}, f32[16,8,8]{1,2,0:T(8,128)}, u32[]{:S(2)}) copy-start(f32[16,8,8]{1,2,0:T(8,128)} %copy-done.26) | copy-start | bytes 12292
  1948.1 582.7 %copy-start.49 = (bf16[1,8,16,64]{3,2,1,0:T(8,128)(2,1)S(1)}, bf16[1,8,16,64]{3,2,1,0:T(8,128)(2,1)}, u32[]{:S(2)}) copy-start(bf16[1,8,16,64]{3,2,1,0:T(8,128)(2,1)} %copy-done.48) | copy-start | bytes 49156
  1948.1 582.9 %copy-start.41 = (bf16[1,8,16,64]{3,2,1,0:T(8,128)(2,1)S(1)}, bf16[1,8,16,64]{3,2,1,0:T(8,128)(2,1)}, u32[]{:S(2)}) copy-start(bf16[1,8,16,64]{3,2,1,0:T(8,128)(2,1)} %copy-done.40) | copy-start | bytes 49156
  1948.1 583.1 %copy-start.39 = (bf16[1,8,16,64]{3,2,1,0:T(8,128)(2,1)S(1)}, bf16[1,8,16,64]{3,2,1,0:T(8,128)(2,1)}, u32[]{:S(2)}) copy-start(bf16[1,8,16,64]{3,2,1,0:T(8,128)(2,1)} %copy-done.38) | copy-start | bytes 49156
  1951.4 585.0 %copy-start.29 = (f32[8,1024]{1,0:T(8,128)S(1)}, f32[8,1024]{1,0:T(8,128)}, u32[]{:S(2)}) copy-start(f32[8,1024]{1,0:T(8,128)} %copy-done.28) | copy-start | bytes 98308
  1951.4 585.0 %copy-start.57 = (f32[1024,1]{0,1:T(1,128)S(1)}, f32[1024,1]{0,1:T(1,128)}, u32[]{:S(2)}) copy-start(f32[1024,1]{0,1:T(1,128)} %copy-done.56) | copy-start | bytes 12292
  1951.4 585.0 %copy-start.82 = (f32[8]{0:T(128)S(1)}, f32[8]{0:T(128)}, u32[]{:S(2)}) copy-start(f32[8]{0:T(128)} %copy-done.81) | copy-start | bytes 100
  1951.4 585.0 %copy-start.84 = (f32[8]{0:T(128)S(1)}, f32[8]{0:T(128)}, u32[]{:S(2)}) copy-start(f32[8]{0:T(128)} %copy-done.83) | copy-start | bytes 100
  1951.4 846.6 %reduce-scatter.18.cloned.1.call-start = ((), (), s32[]{:S(2)}) async-start(), calls=%async_computation.12 | async-start | bytes 294912
  2530.6 10.5 copy-start.51
  2531.9 11.3 copy-start.33
  2540.2 9.3 copy-start.47
  2549.4 250.2 %reduce-scatter.16.cloned.1.call-start = ((), (), s32[]{:S(2)}) async-start(), calls=%async_computation.11 | async-start | bytes 11796480
  2582.1 166.9 %copy-start.14 = (f32[128,5,1024]{2,0,1:T(8,128)S(1)}, f32[128,5,1024]{2,0,1:T(8,128)}, u32[]{:S(2)}) copy-start(f32[128,5,1024]{2,0,1:T(8,128)} %param.32) | copy-start | bytes 7864324
  2747.5 14.0 collective-permute-start.1
  2757.4 16.7 copy-start.3
  2757.4 16.7 copy-start.63
  2757.4 16.7 copy-start.69
  2781.1 10.7 copy-start.4
  2798.0 48.5 %copy-start.20 = (bf16[128,2,1024]{2,0,1:T(8,128)(2,1)S(1)}, bf16[128,2,1024]{2,0,1:T(8,128)(2,1)}, u32[]{:S(2)}) copy-start(bf16[128,2,1024]{2,0,1:T(8,128)(2,1)} %reduce-scatter.14.cloned.1.call-done) | copy-start | bytes 1572868
  2798.0 48.6 %copy-start.22 = (f32[128,2,1024]{2,1,0:T(2,128)S(1)}, f32[128,2,1024]{2,1,0:T(2,128)}, u32[]{:S(2)}) copy-start(f32[128,2,1024]{2,1,0:T(2,128)} %param.28) | copy-start | bytes 3145732
  2799.6 79.0 %copy-start.61 = (f32[128,18]{0,1:T(8,128)}, f32[128,18]{0,1:T(8,128)S(1)}, u32[]{:S(2)}) copy-start(f32[128,18]{0,1:T(8,128)S(1)} %get-tuple-element.272) | copy-start | bytes 27652
  2846.6 11.1 copy-start.11
  (40 other events, 159.7 us)
Sparse Core Ops, SparseCore 0:
  10.5 30.8 all-gather.11
  43.0 167.8 all-gather.17
  213.3 61.4 all-gather.13
  276.3 193.3 all-gather.21
  774.6 168.3 all-gather.19
  945.4 34.8 all-gather.15
  1401.4 168.0 all-gather.23
  1884.8 642.7 all-reduce.10
  2531.8 50.2 reduce-scatter.13
  2585.2 61.4 all-reduce.12
  2650.3 32.8 reduce-scatter.17
  2686.9 81.5 reduce-scatter.15
where the time goes:
time: 2900 us; the launch traced here: 2890 us
  waiting for transfers between devices  1090 us (38%)
  blocking collectives  872 us (30%)
  matrix products  373 us (13%)
  local copies, waits for them, and re-layouts  361 us (12%)
  other arithmetic  161 us (6%)
    unnamed x3, blocking collectives  821 us
    unnamed x19, waiting for transfers between devices  580 us
    all_gather x1, waiting for transfers between devices, on_device(): work_rows = lax.all_gather(tokens, 'tensor', axis=0, tiled=True)  168 us
    all_gather x1, waiting for transfers between devices, on_device(): grad_mid_rows = lax.all_gather(middle_grad, 'tensor', axis=0, tiled=True)  166 us
    all_gather x1, waiting for transfers between devices, on_device(): mid_rows = lax.all_gather(middle_low, 'tensor', axis=0, tiled=True)  157 us
    unnamed x212, local copies, waits for them, and re-layouts  131 us
    dot_general x10, matrix products, dot_rows(): lax.dot_general(left_side, right_side, (((1,), (1,)), ((), ())), preferre...  79.1 us
    dot_general x10, matrix products, dot_plain(): return jnp.dot(left_side, right_side, preferred_element_type=jnp.float32)  75.7 us
  transfers between devices with their start and end apart: 15, of which 7 were waited for; matrix products, arithmetic and copies ran while one was open for 33% of the time, Pallas kernels for 0%

commit v1 on v0

v1 whole, which is shorter than its diff:
```python
import functools

import jax
import jax.numpy as jnp
from jax import lax
from jax.experimental import pallas as pl
from jax.experimental.pallas import tpu as pltpu
from jax.sharding import PartitionSpec as P

D = 1024
HEADS = 16
HEAD = 64
FF = 4096
PATCHES = 577
FRAMES = 8
STEP = 10
ROWS = 592


norm_eps = 1e-05
beta_one = 0.9
beta_two = 0.95
adam_eps = 1e-08
decay_mat = 0.05
ema_keep = 0.7
clip_limit = 1.0
rate_mat = 0.02
rate_vec = 0.4
far_below = -1e30
bf16 = jnp.bfloat16
f32 = jnp.float32
NN = (((1,), (0,)), ((), ()))
NT = (((1,), (1,)), ((), ()))
TN = (((0,), (0,)), ((), ()))


def dot(left_side, right_side, dims=NN):
    return lax.dot_general(left_side, right_side, dims, preferred_element_type=f32)


def norm_rows(values, gain_row, shift_row):
    centre = values - jnp.mean(values, -1, keepdims=True)
    spread = jnp.mean(centre * centre, -1, keepdims=True)
    inverse = lax.rsqrt(spread + norm_eps)
    scaled = centre * inverse
    return (scaled * gain_row + shift_row, scaled, inverse)


def norm_back(gradient, scaled, inverse, gain_row):
    inner = gradient * gain_row
    return inverse * (
        inner
        - jnp.mean(inner, -1, keepdims=True)
        - scaled * jnp.mean(inner * scaled, -1, keepdims=True)
    )


def pad_rows(values, count):
    if values.shape[0] == count:
        return values
    extra = jnp.zeros((count - values.shape[0],) + values.shape[1:], values.dtype)
    return jnp.concatenate([values, extra], 0)


def head_pair(queries, key_rows, head):
    lane = lax.broadcasted_iota(jnp.int32, queries.shape, 1)
    key_lane = lax.broadcasted_iota(jnp.int32, key_rows.shape, 1)
    key_row = lax.broadcasted_iota(jnp.int32, key_rows.shape, 0)
    spare = HEAD * (1 - head)
    mask = jnp.where(
        (key_lane == spare) & (key_row > PATCHES), jnp.asarray(far_below, bf16), jnp.asarray(0, bf16)
    )
    keys_one = jnp.where((key_lane // HEAD) == head, key_rows, mask)
    queries_one = jnp.where(lane == spare, jnp.asarray(1, bf16), queries)
    return queries_one, keys_one


def attend_forward_kernel(q_ref, k_ref, v_ref, out_ref, total_ref):
    rows = q_ref.shape[1]
    key_count = -(-rows // 128) * 128
    queries = q_ref[0] * jnp.asarray(HEAD**-0.5, bf16)
    key_rows = pad_rows(k_ref[0], key_count)
    value_rows = pad_rows(v_ref[0], key_count)
    lane = lax.broadcasted_iota(jnp.int32, (rows, 128), 1)
    outs, totals = [], []
    for head in range(2):
        queries_one, keys_one = head_pair(queries, key_rows, head)
        scores = dot(queries_one, keys_one, NT)
        highest = jnp.max(scores, 1, keepdims=True)
        shifted = jnp.exp(scores - highest)
        total = jnp.sum(shifted, 1, keepdims=True)
        probability = (shifted * (1.0 / total)).astype(bf16)
        outs.append(dot(probability, value_rows))
        totals.append(highest + jnp.log(total))
    out_ref[0] = jnp.where(lane < HEAD, outs[0], outs[1]).astype(bf16)
    both = jnp.where(lane < HEAD, totals[0], totals[1]).T
    total_ref[0, 0] = jnp.concatenate([both[0:1], both[HEAD : HEAD + 1]], 0)


def attend_backward_kernel(q_ref, k_ref, v_ref, total_ref, grad_ref, dq_ref, dk_ref, dv_ref):
    rows = q_ref.shape[1]
    query_count = -(-rows // 128) * 128
    queries = pad_rows(q_ref[0], query_count) * jnp.asarray(HEAD**-0.5, bf16)
    grads = pad_rows(grad_ref[0], query_count)
    key_rows = k_ref[0]
    value_rows = v_ref[0]
    keys_t = pad_rows(key_rows, query_count).astype(f32).T.astype(bf16)
    lane = lax.broadcasted_iota(jnp.int32, (rows, 128), 1)
    grad_q, grad_k, grad_v = [], [], []
    for head in range(2):
        queries_one, keys_one = head_pair(queries, key_rows, head)
        total = total_ref[0, 0, head : head + 1, :]
        if query_count > rows:
            total = jnp.concatenate([total, jnp.zeros((1, query_count - rows), f32)], 1)
        probability = jnp.exp(dot(keys_one, queries_one, NT) - total)
        values_one = jnp.where((lane // HEAD) == head, value_rows, jnp.asarray(0, bf16))
        grad_prob = dot(values_one, grads, NT)
        inner = jnp.sum(grad_prob * probability, 0, keepdims=True)
        grad_scores = (probability * (grad_prob - inner)).astype(bf16)
        grad_v.append(dot(probability.astype(bf16), grads))
        grad_k.append(dot(grad_scores, queries))
        grad_q.append(dot(keys_t[HEAD * head : HEAD * (head + 1)], pad_rows(grad_scores, query_count)))
    grad_q = jnp.concatenate(grad_q, 0) * HEAD**-0.5
    dq_ref[0] = grad_q.T[:rows].astype(bf16)
    dk_ref[0] = jnp.where(lane < HEAD, grad_k[0], grad_k[1]).astype(bf16)
    dv_ref[0] = jnp.where(lane < HEAD, grad_v[0], grad_v[1]).astype(bf16)


def attend_cost(frames, rows, width, matmuls):
    return pl.CostEstimate(
        flops=2 * matmuls * frames * rows * rows * width,
        bytes_accessed=2 * matmuls * frames * rows * width * 2,
        transcendentals=frames * rows * rows * width // HEAD,
    )


def attend_forward(queries, key_rows, value_rows):
    frames, rows, width = queries.shape
    spec = pl.BlockSpec((1, rows, 128), lambda f, h: (f, 0, h))
    return pl.pallas_call(
        attend_forward_kernel,
        grid=(frames, width // 128),
        in_specs=[spec] * 3,
        out_specs=[spec, pl.BlockSpec((1, 1, 2, rows), lambda f, h: (f, h, 0, 0))],
        out_shape=[
            jax.ShapeDtypeStruct((frames, rows, width), bf16),
            jax.ShapeDtypeStruct((frames, width // 128, 2, rows), f32),
        ],
        compiler_params=pltpu.CompilerParams(vmem_limit_bytes=48 << 20),
        cost_estimate=attend_cost(frames, rows, width, 4),
        name="attend_forward",
    )(queries, key_rows, value_rows)


def attend_backward(queries, key_rows, value_rows, totals, grads):
    frames, rows, width = queries.shape
    spec = pl.BlockSpec((1, rows, 128), lambda f, h: (f, 0, h))
    return pl.pallas_call(
        attend_backward_kernel,
        grid=(frames, width // 128),
        in_specs=[spec] * 3 + [pl.BlockSpec((1, 1, 2, rows), lambda f, h: (f, h, 0, 0)), spec],
        out_specs=[spec] * 3,
        out_shape=[jax.ShapeDtypeStruct((frames, rows, width), bf16)] * 3,
        compiler_params=pltpu.CompilerParams(vmem_limit_bytes=48 << 20),
        cost_estimate=attend_cost(frames, rows, width, 8),
        name="attend_backward",
    )(queries, key_rows, value_rows, totals, grads)


def feed_kernel(
    n2_ref,
    n2t_ref,
    g_ref,
    gt_ref,
    bias_ref,
    up_own_ref,
    up_other_ref,
    down_own_ref,
    down_other_ref,
    out_ref,
    dn2_ref,
    dup_own_ref,
    dup_other_ref,
    ddown_own_ref,
    ddown_other_ref,
    db_ref,
    act_ref,
    dpre_ref,
):
    frames, rows = n2_ref.shape[:2]
    blocks, _, part, chunk = up_own_ref.shape
    half = blocks * part

    @pl.when(pl.program_id(0) == 0)
    def _():
        out_ref[...] = jnp.zeros_like(out_ref)
        dn2_ref[...] = jnp.zeros_like(dn2_ref)
        act_ref[...] = jnp.zeros_like(act_ref)
        dpre_ref[...] = jnp.zeros_like(dpre_ref)

    def whole(own_ref, other_ref):
        return jnp.concatenate(
            [own_ref[:, 0].reshape(half, chunk), other_ref[:, 0].reshape(half, chunk)], 0
        )

    first = whole(up_own_ref, up_other_ref)
    second = whole(down_own_ref, down_other_ref)
    bias_sum = jnp.zeros((1, chunk), f32)
    for frame in range(frames):
        place = pl.ds(frame * rows, rows)
        pre = dot(n2_ref[frame], first) + bias_ref[0]
        sigma = 1.0 / (1.0 + jnp.exp(-1.702 * pre))
        act = (pre * sigma).astype(bf16)
        act_ref[place] = act
        out_ref[frame] += dot(act, second, NT)
        grad_act = dot(g_ref[frame], second)
        grad_pre = grad_act * (sigma + 1.702 * pre * sigma * (1.0 - sigma))
        grad_low = grad_pre.astype(bf16)
        dpre_ref[place] = grad_low
        bias_sum += jnp.sum(grad_low.astype(f32), 0, keepdims=True)
        dn2_ref[frame] += dot(grad_low, first, NT)
    db_ref[0] = bias_sum

    def place_grad(left_ref, right_ref, own_ref, other_ref):
        for at, ref in ((0, own_ref), (half, other_ref)):
            grad = dot(left_ref[at : at + half], right_ref[...]).astype(bf16)
            ref[:, 0] = grad.reshape(blocks, part, chunk)

    place_grad(n2t_ref, dpre_ref, dup_own_ref, dup_other_ref)
    place_grad(gt_ref, act_ref, ddown_own_ref, ddown_other_ref)


def feed_forward(n2, n2t, grads, grads_t, bias, weights):
    frames, rows, _ = n2.shape
    blocks, ff_blocks, part, local = weights[0].shape
    chunk = min(512, local)
    per = local // chunk
    steps = ff_blocks * per
    deep = n2t.shape[1]
    whole3 = lambda n: (0, 0, 0)
    whole2 = lambda n: (0, 0)
    once = pl.Buffered(1)
    w_spec = pl.BlockSpec((blocks, 1, part, chunk), lambda n: (0, n // per, 0, n % per))
    return pl.pallas_call(
        feed_kernel,
        grid=(steps,),
        in_specs=[
            pl.BlockSpec((frames, rows, D), whole3, pipeline_mode=once),
            pl.BlockSpec((D, deep), whole2, pipeline_mode=once),
            pl.BlockSpec((frames, rows, D), whole3, pipeline_mode=once),
            pl.BlockSpec((D, deep), whole2, pipeline_mode=once),
            pl.BlockSpec((1, 1, chunk), lambda n: (n, 0, 0)),
        ]
        + [w_spec] * 4,
        out_specs=[pl.BlockSpec((frames, rows, D), whole3)] * 2
        + [w_spec] * 4
        + [pl.BlockSpec((1, 1, chunk), lambda n: (n, 0, 0))],
        out_shape=[jax.ShapeDtypeStruct((frames, rows, D), f32)] * 2
        + [jax.ShapeDtypeStruct(weights[0].shape, bf16)] * 4
        + [jax.ShapeDtypeStruct((steps, 1, chunk), f32)],
        scratch_shapes=[pltpu.VMEM((deep, chunk), bf16), pltpu.VMEM((deep, chunk), bf16)],
        compiler_params=pltpu.CompilerParams(vmem_limit_bytes=60 << 20),
        cost_estimate=pl.CostEstimate(
            flops=12 * frames * rows * D * ff_blocks * local,
            bytes_accessed=8 * D * ff_blocks * local + 16 * frames * rows * D,
            transcendentals=frames * rows * ff_blocks * local,
        ),
        name="feed_forward",
    )(n2, n2t, grads, grads_t, bias.reshape(steps, 1, chunk), *weights)


def swap(values, axis, bit):
    pairs = [(i, i ^ bit) for i in range(lax.axis_size(axis))]
    return lax.ppermute(values, axis, pairs)


def bits_of(axis):
    size = lax.axis_size(axis)
    return [1 << i for i in range(size.bit_length() - 1)]


def chip_orders():
    bits = bits_of("dp")[1:]
    middle = len(bits) // 2
    return bits[::-1], (bits, bits[middle:] + bits[:middle])


def gather_chips(values, which):
    high_first, orders = chip_orders()
    done = []
    for bit in orders[which]:
        at = sum(b > bit for b in done)
        values = jnp.stack([values, swap(values, "dp", bit)], at)
        done.append(bit)
    return values.reshape((-1,) + values.shape[len(done) :])


def gather_small(values):
    chips = gather_chips(values, 0)
    return jnp.concatenate([chips, swap(chips, "dp", 1)], 0)


def add_low(left_side, right_side):
    return (left_side.astype(f32) + right_side.astype(f32)).astype(bf16)


def scatter_chips(kept, sent, which):
    high_first, orders = chip_orders()
    left = list(high_first)
    shape = (2,) * len(left) + kept.shape[1:]
    kept, received = kept.reshape(shape), swap(sent, "dp", 1).reshape(shape)
    for bit in orders[which][::-1]:
        at = left.index(bit)
        left.remove(bit)
        take = lambda v, i: lax.index_in_dim(v, i, at, keepdims=False)
        going = add_low(take(kept, 1), take(received, 1))
        kept = add_low(take(kept, 0), take(received, 0))
        received = swap(going, "dp", bit)
    return add_low(kept, received)


def scatter_videos(values, earlier):
    if earlier:
        values, _ = lax.optimization_barrier((values, earlier[-1]))
    return lax.psum_scatter(values, "tensor", scatter_dimension=0, tiled=False)


def sum_everywhere(values):
    for axis in ("dp", "tensor"):
        for bit in bits_of(axis):
            values = values + swap(values, axis, bit)
    return values


def gather_videos(values):
    values = values[None]
    for bit in bits_of("tensor"):
        values = jnp.concatenate([values, swap(values, "tensor", bit)], 0)
    order = lax.iota(jnp.int32, values.shape[0]) ^ lax.axis_index("tensor")
    return jnp.take(values, order, axis=0, mode="clip").reshape(-1, values.shape[-1])


def relative_places():
    count = lax.axis_size("dp")
    return [
        lax.axis_index("dp") ^ (2 * (r % (count // 2)) + r // (count // 2)) for r in range(count)
    ]


def absolute_places():
    differs = lax.iota(jnp.int32, lax.axis_size("dp")) ^ lax.axis_index("dp")
    return (differs & 1) * (lax.axis_size("dp") // 2) + (differs >> 1)


def to_relative(values):
    part = D // lax.axis_size("dp")
    return jnp.concatenate(
        [
            lax.dynamic_slice_in_dim(values, place * part, part, values.ndim - 1)
            for place in relative_places()
        ],
        -1,
    )


def to_absolute(values):
    part = D // lax.axis_size("dp")
    places = absolute_places()
    return jnp.concatenate(
        [
            lax.dynamic_slice_in_dim(values, places[i] * part, part, values.ndim - 1)
            for i in range(lax.axis_size("dp"))
        ],
        -1,
    )


def to_heads(rows_in):
    return jnp.moveaxis(rows_in.reshape(rows_in.shape[0], HEADS, HEAD), 1, 0)


def from_heads(values):
    return jnp.moveaxis(values, 0, 1).reshape(values.shape[1], D)


def message_attend(queries, key_rows, value_rows):
    scores = jnp.einsum("hqe,hke->hqk", queries, key_rows, preferred_element_type=f32) * HEAD**-0.5
    highest = jnp.max(scores, -1, keepdims=True)
    shifted = jnp.exp(scores - highest)
    probability = shifted / jnp.sum(shifted, -1, keepdims=True)
    out = jnp.einsum(
        "hqk,hke->hqe", probability.astype(bf16), value_rows, preferred_element_type=f32
    )
    return out, probability


def message_attend_back(queries, key_rows, value_rows, probability, grads):
    grad_prob = jnp.einsum("hqe,hke->hqk", grads, value_rows, preferred_element_type=f32)
    grad_scores = (
        probability * (grad_prob - jnp.sum(grad_prob * probability, -1, keepdims=True))
    ).astype(bf16)
    scale = HEAD**-0.5
    grad_q = jnp.einsum("hqk,hke->hqe", grad_scores, key_rows, preferred_element_type=f32) * scale
    grad_k = jnp.einsum("hqk,hqe->hke", grad_scores, queries, preferred_element_type=f32) * scale
    grad_v = jnp.einsum("hqk,hqe->hke", probability.astype(bf16), grads, preferred_element_type=f32)
    return grad_q, grad_k, grad_v


def adam_step(weight, first_moment, second_moment, gradient, factor, step_rate, decay_rate):
    clipped = gradient * factor
    first_new = beta_one * first_moment + (1.0 - beta_one) * clipped
    second_new = beta_two * second_moment + (1.0 - beta_two) * clipped * clipped
    update = (
        first_new
        / (1.0 - beta_one**STEP)
        / (jnp.sqrt(second_new / (1.0 - beta_two**STEP)) + adam_eps)
    )
    weight_new = weight - step_rate * (update + decay_rate * weight)
    return (first_new, second_new, weight_new)


def on_device(
    tokens,
    cotangent,
    attn_master,
    attn_first,
    attn_second,
    attn_ema,
    mlp_master,
    mlp_first,
    mlp_second,
    mlp_ema,
    msg_master,
    msg_first,
    msg_second,
    msg_ema,
    vec_master,
    vec_first,
    vec_second,
    vec_ema,
):
    z_index = lax.axis_index("tensor")
    z_count = lax.axis_size("tensor")
    dp_index = lax.axis_index("dp")
    dp_count = lax.axis_size("dp")
    part = attn_master.shape[0]
    local_width = attn_master.shape[2]
    local_ff = mlp_master.shape[2]
    frames = tokens.shape[0] // PATCHES
    half_ff = local_ff // 2

    attn_z = lax.all_gather(jnp.swapaxes(attn_master, 0, 1).astype(bf16), "tensor", axis=0)
    mlp_z = lax.all_gather(jnp.swapaxes(mlp_master, 0, 1).astype(bf16), "tensor", axis=0)
    vec_all = gather_small(vec_master.astype(bf16).T)
    class_own = tokens.reshape(frames, PATCHES, D)[:, 0]
    class_rows = gather_videos(class_own)

    def both_cores(values):
        return [values, swap(values, "dp", 1)]

    msg_low = jnp.swapaxes(msg_master, 0, 1).astype(bf16)
    msg_half = [
        both_cores(gather_chips(msg_low[..., i * D // 2 : (i + 1) * D // 2], i)) for i in range(2)
    ]
    attn_half = [both_cores(gather_chips(attn_z[:, 2 * i : 2 * i + 2], i)) for i in range(2)]
    mlp_parts = [
        [
            side
            for i in range(2)
            for side in both_cores(gather_chips(mlp_z[:, i, :, j * half_ff : (j + 1) * half_ff], i))
        ]
        for j in range(2)
    ]
    vec_rel = jnp.moveaxis(vec_all, 0, 1).reshape(-1, D).astype(f32)
    vectors = to_absolute(vec_rel)
    ff_bias = vectors[14:].reshape(z_count, 2, half_ff)
    msg_w = [
        jnp.concatenate(
            [
                jnp.concatenate([side[:, i].reshape(D // 2, D // 2) for side in sides], 0)
                for sides in msg_half
            ],
            1,
        )
        for i in range(5)
    ]
    attn_w = [
        jnp.concatenate(
            [
                jnp.swapaxes(side[:, :, i % 2], 1, 2).reshape(D // 2, z_count * local_width)
                for side in attn_half[i // 2]
            ],
            0,
        )
        for i in range(4)
    ]

    first_msg = dot(to_relative(class_rows), msg_w[0]) + vectors[6]
    normed_msg, scaled_msg, inverse_msg = norm_rows(first_msg, vectors[4], vectors[5])
    normed_msg = normed_msg.astype(bf16)
    normed_rel = to_relative(normed_msg)
    msg_q = to_heads((dot(normed_rel, msg_w[1]) + vectors[7]).astype(bf16))
    msg_k = to_heads(dot(normed_rel, msg_w[2]).astype(bf16))
    msg_v = to_heads((dot(normed_rel, msg_w[3]) + vectors[8]).astype(bf16))
    msg_out, msg_prob = message_attend(msg_q, msg_k, msg_v)
    msg_mixed = from_heads(msg_out).astype(bf16)
    message = first_msg + dot(to_relative(msg_mixed), msg_w[4]) + vectors[9]
    own_message = to_relative(lax.dynamic_slice_in_dim(message, z_index * frames, frames, 0))

    token_rows = to_relative(tokens).reshape(frames, PATCHES, D)
    zero_rows = jnp.zeros((frames, ROWS - PATCHES - 1, D), f32)
    full_rows = jnp.concatenate(
        [token_rows.astype(f32), own_message[:, None], zero_rows], axis=1
    )
    normed, scaled, inverse = norm_rows(full_rows, vec_rel[0], vec_rel[1])
    normed = normed.astype(bf16).reshape(frames * ROWS, D)
    queries = (dot(normed, attn_w[0]) + vectors[10]).astype(bf16).reshape(frames, ROWS, D)
    key_rows = dot(normed, attn_w[1]).astype(bf16).reshape(frames, ROWS, D)
    value_rows = (dot(normed, attn_w[2]) + vectors[11]).astype(bf16).reshape(frames, ROWS, D)
    attended, totals = attend_forward(queries, key_rows, value_rows)
    attended_flat = attended.reshape(frames * ROWS, D)
    middle = (
        full_rows + dot(attended_flat, attn_w[3], NT).reshape(frames, ROWS, D) + vec_rel[12]
    )

    scaled_gain, scaled_mid, inverse_mid = norm_rows(
        middle.astype(bf16).astype(f32), vec_rel[2], vec_rel[3]
    )
    normed_mid = scaled_gain.astype(bf16)
    grads = jnp.concatenate(
        [
            to_relative(cotangent).reshape(frames, PATCHES, D),
            jnp.zeros((frames, ROWS - PATCHES, D), bf16),
        ],
        1,
    )
    deep = -(-frames * ROWS // 128) * 128
    normed_mid_t = pad_rows(normed_mid.reshape(frames * ROWS, D), deep).T
    grads_t = pad_rows(grads.reshape(frames * ROWS, D), deep).T
    mlp_out, grad_mid_in, mlp_grads, bias_grads = 0.0, 0.0, [], []
    for j in range(2):
        out_j, dn2_j, *dw_j, db_j = feed_forward(
            normed_mid, normed_mid_t, grads, grads_t, ff_bias[:, j], mlp_parts[j]
        )
        mlp_out += out_j
        grad_mid_in += dn2_j
        sums = [scatter_chips(dw_j[2 * i], dw_j[2 * i + 1], i) for i in range(2)]
        mlp_grads.append(scatter_videos(jnp.stack(sums, 1), mlp_grads))
        bias_grads.append(db_j.reshape(z_count, half_ff))
    block_output = to_absolute(
        (middle + mlp_out + vec_rel[13])[:, :PATCHES].reshape(-1, D)
    )
    ff_bias_grad = jnp.stack(bias_grads, 1).reshape(FF // D, D)

    back_mid = norm_back(grad_mid_in, scaled_mid, inverse_mid, vec_rel[2])
    middle_grad = (grads.astype(f32) + back_mid).astype(bf16)
    middle_flat = middle_grad.reshape(frames * ROWS, D)
    grad_attended = dot(middle_flat, attn_w[3]).astype(bf16).reshape(frames, ROWS, D)
    grad_out_w = dot(middle_flat, attended_flat, TN).astype(bf16)
    grad_q, grad_k, grad_v = attend_backward(queries, key_rows, value_rows, totals, grad_attended)
    flat = [g.reshape(frames * ROWS, D) for g in (grad_q, grad_k, grad_v)]
    attn_full = [dot(normed, g, TN).astype(bf16) for g in flat] + [grad_out_w]
    attn_sums = []
    for i in range(2):
        sides = []
        for side in range(2):
            rows = [
                g[side * D // 2 : (side + 1) * D // 2].reshape(-1, part, z_count, local_width)
                for g in attn_full[2 * i : 2 * i + 2]
            ]
            sides.append(jnp.stack([jnp.swapaxes(g, 1, 2) for g in rows], 2))
        attn_sums.append(scatter_chips(sides[0], sides[1], i))
    attn_grad = scatter_videos(jnp.concatenate(attn_sums, 1), mlp_grads)
    attn_grad = jnp.swapaxes(attn_grad, 0, 1).astype(f32)
    grad_normed = (
        dot(flat[0], attn_w[0], NT) + dot(flat[1], attn_w[1], NT) + dot(flat[2], attn_w[2], NT)
    ).reshape(frames, ROWS, D)
    back_rows = norm_back(grad_normed, scaled, inverse, vec_rel[0])
    input_grad = middle_grad.astype(f32) + back_rows

    msg_grad_own = to_absolute(back_rows[:, PATCHES].astype(bf16))
    msg_grad_low = gather_videos(msg_grad_own)
    grad_mixed = to_absolute(dot(msg_grad_low, msg_w[4], NT).astype(bf16))
    msg_dq, msg_dk, msg_dv = message_attend_back(
        msg_q, msg_k, msg_v, msg_prob, to_heads(grad_mixed)
    )
    msg_dq, msg_dk, msg_dv = (from_heads(g).astype(bf16) for g in (msg_dq, msg_dk, msg_dv))
    grad_normed_msg = to_absolute(
        dot(msg_dq, msg_w[1], NT) + dot(msg_dk, msg_w[2], NT) + dot(msg_dv, msg_w[3], NT)
    )
    back_first = norm_back(grad_normed_msg, scaled_msg, inverse_msg, vectors[4])
    grad_first = (msg_grad_low.astype(f32) + back_first).astype(bf16)
    grad_class = dot(grad_first, msg_w[0], NT)
    own_class = lax.dynamic_slice_in_dim(grad_class, z_index * frames, frames, 0)
    class_mark = (lax.iota(jnp.int32, PATCHES) == 0)[None, :, None]
    input_grad = to_absolute(
        (input_grad[:, :PATCHES] + jnp.where(class_mark, own_class[:, None], 0.0)).reshape(-1, D)
    )
    sent = jnp.stack(
        [class_rows, normed_msg, msg_mixed, grad_first, msg_dq, msg_dk, msg_dv, msg_grad_low], 0
    )
    everyone = jnp.moveaxis(gather_small(sent), 0, 1).reshape(8, -1, D)
    mine = lax.dynamic_slice_in_dim(everyone[:3], dp_index * part, part, 2)
    msg_grad = jnp.stack(
        [
            dot(mine[0], everyone[3], TN),
            dot(mine[1], everyone[4], TN),
            dot(mine[1], everyone[5], TN),
            dot(mine[1], everyone[6], TN),
            dot(mine[2], everyone[7], TN),
        ],
        1,
    )

    def over_rows(values):
        return jnp.sum(values.astype(f32), (0, 1))

    def over_messages(values):
        return jnp.where(z_index == 0, jnp.sum(values.astype(f32), 0), 0.0)

    relative = to_absolute(
        jnp.stack(
            [
                over_rows(grad_normed * scaled),
                over_rows(grad_normed),
                over_rows(grad_mid_in * scaled_mid),
                over_rows(grad_mid_in),
                over_rows(middle_grad),
                over_rows(grads),
            ]
        )
    )
    straight = jnp.stack(
        [
            over_messages(grad_normed_msg * scaled_msg),
            over_messages(grad_normed_msg),
            over_messages(grad_first),
            over_messages(msg_dq),
            over_messages(msg_dv),
            over_messages(msg_grad_low),
            over_rows(grad_q),
            over_rows(grad_v),
        ]
    )
    table = sum_everywhere(
        jnp.concatenate([relative[:4], straight, relative[4:], ff_bias_grad], 0)
    )
    vec_grad = lax.dynamic_slice_in_dim(table, dp_index * part, part, 1).T

    mlp_grad = jnp.swapaxes(jnp.concatenate(mlp_grads, 2), 0, 1).astype(f32)

    keep_share = (z_index == 0).astype(f32)
    squares = (
        jnp.sum(attn_grad * attn_grad)
        + jnp.sum(mlp_grad * mlp_grad)
        + keep_share * (jnp.sum(msg_grad * msg_grad) + jnp.sum(vec_grad * vec_grad))
    )
    squares = sum_everywhere(jnp.broadcast_to(squares, (8, 128)))[0, 0]
    grad_norm = jnp.sqrt(squares)
    factor = clip_limit / jnp.maximum(grad_norm, clip_limit)

    def update(master, first, second, ema, grad, rate, decay):
        first_new, second_new, weight = adam_step(master, first, second, grad, factor, rate, decay)
        return grad, first_new, second_new, weight, ema_keep * ema + (1.0 - ema_keep) * weight

    return (
        block_output,
        input_grad,
        grad_norm,
        *update(attn_master, attn_first, attn_second, attn_ema, attn_grad, rate_mat, decay_mat),
        *update(mlp_master, mlp_first, mlp_second, mlp_ema, mlp_grad, rate_mat, decay_mat),
        *update(msg_master, msg_first, msg_second, msg_ema, msg_grad, rate_mat, decay_mat),
        *update(vec_master, vec_first, vec_second, vec_ema, vec_grad, rate_vec, 0.0),
    )


def solution(mesh):
    rows = P(("dp", "tensor"), None)
    split = P("dp", None, "tensor")
    copied = P("dp", None, None)
    table = P("dp", None)
    in_specs = (rows,) * 2 + (split,) * 8 + (copied,) * 4 + (table,) * 4
    out_specs = (rows,) * 2 + (P(),) + (split,) * 10 + (copied,) * 5 + (table,) * 5
    return jax.shard_map(
        on_device, mesh=mesh, in_specs=in_specs, out_specs=out_specs, check_vma=False
    )
```

time: 2900 us -> 974 us (0.34)
  blocking collectives: 872 us -> 0 us
  waiting for transfers between devices: 1090 us -> 319 us
  matrix products: 373 us -> 70.4 us
  local copies, waits for them, and re-layouts: 361 us -> 197 us
  Pallas kernels: 0 us -> 160 us
  starting transfers between devices: 7.83 us -> 62.9 us
  other arithmetic: 161 us -> 131 us
    unnamed x3 -> x0, blocking collectives: 821 us -> none
    all_gather x7 -> x2, waiting for transfers between devices: 509 us -> 0.01 us  [the longest x1 0.01 us: on_device(): lax.all_gather(jnp.swapaxes(attn_master, 0, 1).astype(bf16), 'tensor', ax...]
    unnamed x19 -> x8, waiting for transfers between devices: 580 us -> 124 us
    dot_general x93 -> x32, matrix products: 373 us -> 69.6 us  [the longest x27 68.5 us: dot(): lax.dot_general(left_side, right_side, dims, preferred_element_type=f32)]
    ppermute x0 -> x62, waiting for transfers between devices: none -> 194 us  [swap(): return lax.ppermute(values, axis, pairs)]
    pallas_call x0 -> x4, Pallas kernels: none -> 160 us  [the longest x2 81.3 us: feed_forward(): pl.pallas_call(feed_kernel, grid=(steps,), in_specs=[pl.BlockSpec((frames...]
    ppermute x0 -> x62, starting transfers between devices: none -> 62.4 us  [swap(): return lax.ppermute(values, axis, pairs)]
    concatenate x9 -> x20, local copies, waits for them, and re-layouts: 68.4 us -> 10.4 us  [the longest x7 4.48 us: to_absolute(): jnp.concatenate([lax.dynamic_slice_in_dim(values, places[i] * part, part,...]
  transfers between devices with their start and end apart: 15 -> 67, of which waited for: 7 -> 25; matrix products, arithmetic and copies ran while one was open for 33% -> 31% of each run, Pallas kernels for 0% -> 8%
where the time goes in v1:
time: 974 us; the launch traced here: 967 us
  waiting for transfers between devices  319 us (33%)
  local copies, waits for them, and re-layouts  197 us (20%)
  Pallas kernels  160 us (16%)
  other arithmetic  131 us (13%)
  matrix products  70.4 us (7%)
  starting transfers between devices  62.9 us (6%)
  between operations  26.5 us (3%)
    ppermute x62, waiting for transfers between devices, swap(): return lax.ppermute(values, axis, pairs)  194 us
    unnamed x8, waiting for transfers between devices  124 us
    pallas_call x2, Pallas kernels, feed_forward(): pl.pallas_call(feed_kernel, grid=(steps,), in_specs=[pl.BlockSpec((frames...  81.3 us
    unnamed x425, local copies, waits for them, and re-layouts  74.7 us
    dot_general x27, matrix products, dot(): lax.dot_general(left_side, right_side, dims, preferred_element_type=f32)  68.5 us
    ppermute x62, starting transfers between devices, swap(): return lax.ppermute(values, axis, pairs)  62.4 us
    pallas_call x1, Pallas kernels, attend_backward(): pl.pallas_call(attend_backward_kernel, grid=(frames, width // 128), in_sp...  45.7 us
    pallas_call x1, Pallas kernels, attend_forward(): pl.pallas_call(attend_forward_kernel, grid=(frames, width // 128), in_spe...  33 us
  transfers between devices with their start and end apart: 67, of which 25 were waited for; matrix products, arithmetic and copies ran while one was open for 31% of the time, Pallas kernels for 8%

profile of v1, /device:TPU:0, one launch (start us, length us, event | category | flops | bytes accessed | tf_op | source)
XLA Modules:
  0.0 966.8 jit_solution(15293199836856540171)
XLA Ops:
  9.8 2.9 collective-permute-start.8
  54.9 3.1 copy.300
  65.6 4.3 reshape.700
  70.6 2.7 collective-permute-start.1
  82.1 2.7 fusion.158
  94.2 30.2 %collective-permute-done.14 = bf16[4,2,128,256]{3,2,1,0:T(8,128)(2,1)S(1)} collective-permute-done((bf16[4,2,128,256]{3,2,1,0:T(8,128)(2,1)S(1)}, bf16[4,2,128,256]{3,2,1,0:T(8,128)(2,1)S(1)}, u32[]{:S(2)}, u32[]{:S(2)}) %collective-permute-start.14) | collective-permute-done | bytes 524320 | tf_op jit(solution)/shard_map/ppermute | solution.py:274
  130.2 3.2 pad_maximum_fusion
  135.5 3.2 fusion.170
  140.3 9.3 collective-permute-done.15
  149.8 2.9 copy.298
  154.3 3.6 fusion.179
  177.0 4.9 collective-permute-done.17
  183.4 7.5 collective-permute-done.23
  195.6 2.9 fusion.171
  199.5 2.9 fusion.173
  212.8 5.1 maximum_maximum_fusion
  219.7 22.4 %collective-permute-done.27 = bf16[2,4,128,512]{3,2,1,0:T(8,128)(2,1)S(1)} collective-permute-done((bf16[2,4,128,512]{3,2,1,0:T(8,128)(2,1)}, bf16[2,4,128,512]{3,2,1,0:T(8,128)(2,1)S(1)}, u32[]{:S(2)}, u32[]{:S(2)}) %collective-permute-start.27) | collective-permute-done | bytes 1048608 | tf_op jit(solution)/shard_map/ppermute | solution.py:274
  243.8 4.5 add_convert_fusion.3
  249.8 16.8 %collective-permute-done.18 = bf16[2,4,128,512]{3,2,1,0:T(8,128)(2,1)S(1)} collective-permute-done((bf16[2,4,128,512]{3,2,1,0:T(8,128)(2,1)S(1)}, bf16[2,4,128,512]{3,2,1,0:T(8,128)(2,1)S(1)}, u32[]{:S(2)}, u32[]{:S(2)}) %collective-permute-start.18) | collective-permute-done | bytes 1048608 | tf_op jit(solution)/shard_map/ppermute | solution.py:274
  268.6 2.8 pad_maximum_fusion.5
  271.5 2.7 pad_maximum_fusion.6
  285.5 3.9 convolution_convert_fusion.1
  289.4 3.9 add_convert_fusion.1
  293.4 3.1 add_convert_fusion.2
  296.4 33.0 %attend_forward.1 = (bf16[2,592,1024]{2,1,0:T(8,128)(2,1)S(1)}, f32[2,8,2,592]{3,2,1,0:T(2,128)S(1)}) custom-call(bf16[2,592,1024]{2,1,0:T(8,128)(2,1)S(1)} %bitcast.644, bf16[2,592,1024]{2,1,0:T(8,128)(2,1)} %bitcast.808, bf16[2,592,1024]{2,1,0:T(8,128)(2,1)} %bitcast.810), custom_call_target="tpu_custom_call" | custom-call | flops 5742002176 | bytes 19398656 | tf_op jit(solution)/shard_map/attend_forward/pallas_call | solution.py:140
  329.4 5.0 convert_reduce_fusion.1
  337.5 4.3 copy.299
  341.9 3.5 pad_bitcast_fusion.1.n2t_ref
  345.3 40.4 %feed_forward.3 = (f32[2,592,1024]{2,1,0:T(8,128)}, f32[2,592,1024]{2,1,0:T(8,128)}, bf16[4,4,128,512]{3,2,1,0:T(8,128)(2,1)}, bf16[4,4,128,512]{3,2,1,0:T(8,128...) custom-call(bf16[2,592,1024]{2,1,0:T(8,128)(2,1)} %fusion.8.n2_ref, ...), custom_call_target="tpu_custom_call" | custom-call | flops 29796335616 | bytes 36175872 | tf_op jit(solution)/shard_map/feed_forward/pallas_call | solution.py:244
  385.8 40.9 %feed_forward.2 = (f32[2,592,1024]{2,1,0:T(8,128)}, f32[2,592,1024]{2,1,0:T(8,128)}, bf16[4,4,128,512]{3,2,1,0:T(8,128)(2,1)}, bf16[4,4,128,512]{3,2,1,0:T(8,128...) custom-call(bf16[2,592,1024]{2,1,0:T(8,128)(2,1)} %fusion.8.n2_ref, ...), custom_call_target="tpu_custom_call" | custom-call | flops 29796335616 | bytes 36175872 | tf_op jit(solution)/shard_map/feed_forward/pallas_call | solution.py:244
  426.7 6.7 fusion.12
  433.4 3.1 convert_reduce_fusion.4
  436.5 3.1 bitcast_convert_fusion
  439.7 3.9 convolution_convert_fusion
  443.6 45.7 %attend_backward.1 = (bf16[2,592,1024]{2,1,0:T(8,128)(2,1)S(1)}, bf16[2,592,1024]{2,1,0:T(8,128)(2,1)S(1)}, bf16[2,592,1024]{2,1,0:T(8,128)(2,1)}) custom-call(bf16[2,592,1024]{2,1,0:T(8,128)(2,1)} %bitcast.645, bf16[2,592,1024]{2,1,0:T(8,128)(2,1)} %bitcast.809, bf16[2,592,1024]{2,1,0:T(8,128)(2,1)} %bitcast.811, ...), custom_call_target="tpu_custom_call" | custom-call | flops 11484004352 | bytes 38797312 | tf_op jit(solution)/shard_map/attend_backward/pallas_call | solution.py:158
  489.3 4.9 bitcast_convert_fusion.3
  495.9 4.9 bitcast_convert_fusion.1
  503.7 6.6 bitcast_convert_fusion.2
  515.0 3.0 fusion.174
  523.3 3.0 fusion.176
  532.9 2.7 fusion.194
  535.7 2.8 fusion.195
  539.4 6.0 multiply_reduce_fusion
  545.6 5.3 subtract_multiply_fusion
  555.6 4.4 pad_maximum_fusion.9
  560.1 9.8 %fusion.17 = f32[2,577,1024]{2,1,0:T(8,128)} fusion(f32[2,592,1024]{2,1,0:T(8,128)} %get-tuple-element.345, f32[2,592,1024]{2,1,0:T(8,128)} %get-tuple-element.46, f32[2,592,1024]{2,1,0:T(8,128)} %get-tuple-element.45, f32[1024]{0:T(1024)S(1)} %bitcast.798), kind=kLoop, calls=%fused_computation.39 | loop fusion | flops 3545088 | bytes 18911232 | tf_op jit(solution)/shard_map/add | solution.py:551
  569.9 3.4 collective-permute-start.30
  573.3 2.7 convert_element_type.646
  576.0 5.0 reshape.675
  604.7 6.5 fusion.16
  611.2 5.0 reshape.684
  630.4 3.2 collective-permute-done.54
  634.2 4.0 collective-permute-done.55
  638.6 6.2 collective-permute-done.56
  672.0 9.1 collective-permute-done.35
  683.5 46.0 %collective-permute-done.44 = bf16[2,4,128,512]{3,2,1,0:T(8,128)(2,1)S(1)} collective-permute-done((bf16[2,4,128,512]{3,2,1,0:T(8,128)(2,1)S(1)}, bf16[2,4,128,512]{3,2,1,0:T(8,128)(2,1)S(1)}, u32[]{:S(2)}, u32[]{:S(2)}) %collective-permute-start.44) | collective-permute-done | bytes 1048608 | tf_op jit(solution)/shard_map/ppermute | solution.py:274
  734.1 9.9 %collective-permute-done.45 = bf16[4,128,512]{2,1,0:T(8,128)(2,1)S(1)} collective-permute-done((bf16[4,128,512]{2,1,0:T(8,128)(2,1)S(1)}, bf16[4,128,512]{2,1,0:T(8,128)(2,1)S(1)}, u32[]{:S(2)}, u32[]{:S(2)}) %collective-permute-start.45) | collective-permute-done | bytes 524320 | tf_op jit(solution)/shard_map/ppermute | solution.py:274
  745.8 8.4 collective-permute-done.48
  763.1 6.3 collective-permute-done.42
  771.7 34.3 %all-reduce.10.cloned.1.call-done = bf16[4,2,128,512]{3,2,0,1:T(8,128)(2,1)} async-done(((bf16[4,2,128,512]{3,2,0,1:T(8,128)(2,1)}), bf16[4,2,128,512]{3,2,0,1:T(8,128)(2,1)}) %all-reduce.10.cloned.1.call-update) | async-done | bytes 1048592
  814.3 45.9 %all-reduce.12.cloned.1.call-done = bf16[4,2,128,512]{3,2,0,1:T(8,128)(2,1)} async-done(((bf16[4,2,128,512]{3,2,0,1:T(8,128)(2,1)}), bf16[4,2,128,512]{3,2,0,1:T(8,128)(2,1)}) %all-reduce.12.cloned.1.call-update) | async-done | bytes 1048592
  870.0 44.2 %all-reduce.14.cloned.1.call-done = bf16[4,4,128,256]{3,2,0,1:T(8,128)(2,1)} async-done(((bf16[4,4,128,256]{3,2,0,1:T(8,128)(2,1)}), bf16[4,4,128,256]{3,2,0,1:T(8,128)(2,1)}) %all-reduce.14.cloned.1.call-update) | async-done | bytes 1048592
  936.5 2.9 fusion.78
  953.1 5.2 multiply_add_fusion
  (766 shorter events, 297.7 us)
Async XLA Ops:
  7.2 79.1 %all-gather.5.cloned.1.call-start = ((), (), s32[]{:S(2)}) async-start(), calls=%async_computation | async-start | bytes 1310720 | tf_op jit(solution)/shard_map/all_gather | solution.py:452
  9.1 148.8 %all-gather.7.cloned.1.call-start = ((), (), s32[]{:S(2)}) async-start(), calls=%async_computation.1 | async-start | bytes 2621440 | tf_op jit(solution)/shard_map/all_gather | solution.py:453
  9.8 63.5 %collective-permute-start.8 = (bf16[18,128]{1,0:T(8,128)(2,1)S(1)}, bf16[18,128]{1,0:T(8,128)(2,1)S(1)}, u32[]{:S(2)}, u32[]{:S(2)}) collective-permute-start(bf16[18,128]{1,0:T(8,128)(2,1)S(1)} %get-tuple-element.324), channel_id=1, source_target_pairs={{0,8},{4,12},{8,0},{12,4},{16,24},{20,28},{24,16},{28,20},{1,9},{5... | collective-permute-start | bytes 13832 | tf_op jit(solution)/shard_map/ppermute | solution.py:274
  16.3 65.8 %collective-permute-start.5 = (bf16[5,128,512]{2,1,0:T(8,128)(2,1)}, bf16[5,128,512]{2,1,0:T(8,128)(2,1)}, u32[]{:S(2)}, u32[]{:S(2)}) collective-permute-start(bf16[5,128,512]{2,1,0:T(8,128)(2,1)} %get-tuple-element.282), channel_id=1, source_target_pairs={{0,16},{4,20},{8,24},{12,28},{16,0},{20,4},{24,8},{28,12},{1,17},{... | collective-permute-start | bytes 1966088 | tf_op jit(solution)/shard_map/ppermute | solution.py:274
  17.9 61.9 %collective-permute-start.2 = (bf16[5,128,512]{2,1,0:T(8,128)(2,1)}, bf16[5,128,512]{2,1,0:T(8,128)(2,1)}, u32[]{:S(2)}, u32[]{:S(2)}) collective-permute-start(bf16[5,128,512]{2,1,0:T(8,128)(2,1)} %get-tuple-element.283), channel_id=1, source_target_pairs={{0,8},{4,12},{8,0},{12,4},{16,24},{20,28},{24,16},{28,20},{1,9},{5... | collective-permute-start | bytes 1966088 | tf_op jit(solution)/shard_map/ppermute | solution.py:274
  21.1 49.6 %collective-permute-start = (bf16[1,2,1024]{2,1,0:T(2,128)(2,1)S(1)}, bf16[1,2,1024]{2,1,0:T(2,128)(2,1)S(1)}, u32[]{:S(2)}, u32[]{:S(2)}) collective-permute-start(bf16[1,2,1024]{2,1,0:T(2,128)(2,1)S(1)} %bitcast.773), channel_id=1, source_target_pairs={{0,1},{1,0},{2,3},{3,2},{4,5},{5,4},{6,7},{7,6},{8,9},{9,8},{10,11... | collective-permute-start | bytes 12296 | tf_op jit(solution)/shard_map/ppermute | solution.py:274
  23.8 782.2 %all-reduce.10.cloned.1.call-start = ((), (), s32[]{:S(2)}) async-start(), calls=%async_computation.2 | async-start | bytes 2097152
  70.6 5.7 collective-permute-start.1
  73.3 4.4 collective-permute-start.9
  82.1 48.1 %collective-permute-start.3 = (bf16[2,5,128,512]{3,2,1,0:T(8,128)(2,1)}, bf16[2,5,128,512]{3,2,1,0:T(8,128)(2,1)}, u32[]{:S(2)}, u32[]{:S(2)}) collective-permute-start(bf16[2,5,128,512]{3,2,1,0:T(8,128)(2,1)} %get-tuple-element.279), channel_id=1, source_target_pairs={{0,16},{4,20},{8,24},{12,28},{16,0},{20,4},{24,8},{28,12},{1,17},{... | collective-permute-start | bytes 3932168 | tf_op jit(solution)/shard_map/ppermute | solution.py:274
  84.9 48.5 %collective-permute-start.6 = (bf16[2,5,128,512]{3,2,1,0:T(8,128)(2,1)}, bf16[2,5,128,512]{3,2,1,0:T(8,128)(2,1)}, u32[]{:S(2)}, u32[]{:S(2)}) collective-permute-start(bf16[2,5,128,512]{3,2,1,0:T(8,128)(2,1)} %get-tuple-element.285), channel_id=1, source_target_pairs={{0,8},{4,12},{8,0},{12,4},{16,24},{20,28},{24,16},{28,20},{1,9},{5... | collective-permute-start | bytes 3932168 | tf_op jit(solution)/shard_map/ppermute | solution.py:274
  88.4 36.0 %collective-permute-start.14 = (bf16[4,2,128,256]{3,2,1,0:T(8,128)(2,1)S(1)}, bf16[4,2,128,256]{3,2,1,0:T(8,128)(2,1)S(1)}, u32[]{:S(2)}, u32[]{:S(2)}) collective-permute-start(bf16[4,2,128,256]{3,2,1,0:T(8,128)(2,1)S(1)} %get-tuple-element.297), channel_id=1, source_target_pairs={{0,16},{4,20},{8,24},{12,28},{16,0},{20,4},{24,8},{28,12},{1,17},{... | collective-permute-start | bytes 1572872 | tf_op jit(solution)/shard_map/ppermute | solution.py:274
  92.0 35.7 %collective-permute-start.11 = (bf16[4,2,128,256]{3,2,0,1:T(8,128)(2,1)S(1)}, bf16[4,2,128,256]{3,2,0,1:T(8,128)(2,1)S(1)}, u32[]{:S(2)}, u32[]{:S(2)}) collective-permute-start(bf16[4,2,128,256]{3,2,0,1:T(8,128)(2,1)S(1)} %copy.516), channel_id=1, source_target_pairs={{0,8},{4,12},{8,0},{12,4},{16,24},{20,28},{24,16},{28,20},{1,9},{5... | collective-permute-start | bytes 1572872 | tf_op jit(solution)/shard_map/ppermute | solution.py:274
  124.5 25.1 %collective-permute-start.15 = (bf16[2,4,2,128,256]{4,3,2,1,0:T(8,128)(2,1)S(1)}, bf16[2,4,2,128,256]{4,3,2,1,0:T(8,128)(2,1)S(1)}, u32[]{:S(2)}, u32[]{:S(2)}) collective-permute-start(bf16[2,4,2,128,256]{4,3,2,1,0:T(8,128)(2,1)S(1)} %get-tuple-element.295), channel_id=1, source_target_pairs={{0,8},{4,12},{8,0},{12,4},{16,24},{20,28},{24,16},{28,20},{1,9},{5... | collective-permute-start | bytes 3145736 | tf_op jit(solution)/shard_map/ppermute | solution.py:274
  127.8 24.9 %collective-permute-start.12 = (bf16[2,4,2,128,256]{4,3,1,0,2:T(8,128)(2,1)S(1)}, bf16[2,4,2,128,256]{4,3,1,0,2:T(8,128)(2,1)S(1)}, u32[]{:S(2)}, u32[]{:S(2)}) collective-permute-start(bf16[2,4,2,128,256]{4,3,1,0,2:T(8,128)(2,1)S(1)} %get-tuple-element.300), channel_id=1, source_target_pairs={{0,16},{4,20},{8,24},{12,28},{16,0},{20,4},{24,8},{28,12},{1,17},{... | collective-permute-start | bytes 3145736 | tf_op jit(solution)/shard_map/ppermute | solution.py:274
  133.4 60.8 %collective-permute-start.4 = (bf16[4,5,128,512]{3,2,1,0:T(8,128)(2,1)}, bf16[4,5,128,512]{3,2,1,0:T(8,128)(2,1)}, u32[]{:S(2)}, u32[]{:S(2)}) collective-permute-start(bf16[4,5,128,512]{3,2,1,0:T(8,128)(2,1)} %bitcast.6), channel_id=1, source_target_pairs={{0,4},{4,0},{8,12},{12,8},{16,20},{20,16},{24,28},{28,24},{1,5},{5... | collective-permute-start | bytes 7864328 | tf_op jit(solution)/shard_map/ppermute | solution.py:274
  134.9 63.6 %collective-permute-start.7 = (bf16[4,5,128,512]{3,2,1,0:T(8,128)(2,1)S(1)}, bf16[4,5,128,512]{3,2,1,0:T(8,128)(2,1)}, u32[]{:S(2)}, u32[]{:S(2)}) collective-permute-start(bf16[4,5,128,512]{3,2,1,0:T(8,128)(2,1)S(1)} %bitcast.658), channel_id=1, source_target_pairs={{0,4},{4,0},{8,12},{12,8},{16,20},{20,16},{24,28},{28,24},{1,5},{5... | collective-permute-start | bytes 7864328 | tf_op jit(solution)/shard_map/ppermute | solution.py:274
  159.9 12.9 %collective-permute-start.26 = (bf16[4,128,512]{2,1,0:T(8,128)(2,1)S(1)}, bf16[4,128,512]{2,1,0:T(8,128)(2,1)S(1)}, u32[]{:S(2)}, u32[]{:S(2)}) collective-permute-start(bf16[4,128,512]{2,1,0:T(8,128)(2,1)S(1)} %get-tuple-element.269), channel_id=1, source_target_pairs={{0,16},{4,20},{8,24},{12,28},{16,0},{20,4},{24,8},{28,12},{1,17},{... | collective-permute-start | bytes 1572872 | tf_op jit(solution)/shard_map/ppermute | solution.py:274
  167.1 14.9 %collective-permute-start.17 = (bf16[4,128,512]{2,1,0:T(8,128)(2,1)S(1)}, bf16[4,128,512]{2,1,0:T(8,128)(2,1)S(1)}, u32[]{:S(2)}, u32[]{:S(2)}) collective-permute-start(bf16[4,128,512]{2,1,0:T(8,128)(2,1)S(1)} %get-tuple-element.268), channel_id=1, source_target_pairs={{0,8},{4,12},{8,0},{12,4},{16,24},{20,28},{24,16},{28,20},{1,9},{5... | collective-permute-start | bytes 1572872 | tf_op jit(solution)/shard_map/ppermute | solution.py:274
  169.6 21.3 %collective-permute-start.23 = (bf16[4,128,512]{2,1,0:T(8,128)(2,1)S(1)}, bf16[4,128,512]{2,1,0:T(8,128)(2,1)S(1)}, u32[]{:S(2)}, u32[]{:S(2)}) collective-permute-start(bf16[4,128,512]{2,1,0:T(8,128)(2,1)S(1)} %get-tuple-element.266), channel_id=1, source_target_pairs={{0,8},{4,12},{8,0},{12,4},{16,24},{20,28},{24,16},{28,20},{1,9},{5... | collective-permute-start | bytes 1572872 | tf_op jit(solution)/shard_map/ppermute | solution.py:274
  172.8 19.5 %collective-permute-start.20 = (bf16[4,128,512]{2,1,0:T(8,128)(2,1)S(1)}, bf16[4,128,512]{2,1,0:T(8,128)(2,1)S(1)}, u32[]{:S(2)}, u32[]{:S(2)}) collective-permute-start(bf16[4,128,512]{2,1,0:T(8,128)(2,1)S(1)} %get-tuple-element.267), channel_id=1, source_target_pairs={{0,16},{4,20},{8,24},{12,28},{16,0},{20,4},{24,8},{28,12},{1,17},{... | collective-permute-start | bytes 1572872 | tf_op jit(solution)/shard_map/ppermute | solution.py:274
  181.9 92.3 %collective-permute-start.16 = (bf16[4,4,2,128,256]{4,1,3,0,2:T(4,128)(2,1)}, bf16[4,4,2,128,256]{4,1,3,0,2:T(4,128)(2,1)}, u32[]{:S(2)}, u32[]{:S(2)}) collective-permute-start(bf16[4,4,2,128,256]{4,1,3,0,2:T(4,128)(2,1)} %bitcast.85), channel_id=1, source_target_pairs={{0,4},{4,0},{8,12},{12,8},{16,20},{20,16},{24,28},{28,24},{1,5},{5... | collective-permute-start | bytes 6291464 | tf_op jit(solution)/shard_map/ppermute | solution.py:274
  190.9 86.5 %collective-permute-start.13 = (bf16[4,4,2,128,256]{4,3,1,0,2:T(8,128)(2,1)}, bf16[4,4,2,128,256]{4,3,1,0,2:T(8,128)(2,1)}, u32[]{:S(2)}, u32[]{:S(2)}) collective-permute-start(bf16[4,4,2,128,256]{4,3,1,0,2:T(8,128)(2,1)} %bitcast.69), channel_id=1, source_target_pairs={{0,4},{4,0},{8,12},{12,8},{16,20},{20,16},{24,28},{28,24},{1,5},{5... | collective-permute-start | bytes 6291464 | tf_op jit(solution)/shard_map/ppermute | solution.py:274
  192.3 79.1 %collective-permute-start.24 = (bf16[2,4,128,512]{3,2,1,0:T(8,128)(2,1)}, bf16[2,4,128,512]{3,2,1,0:T(8,128)(2,1)}, u32[]{:S(2)}, u32[]{:S(2)}) collective-permute-start(bf16[2,4,128,512]{3,2,1,0:T(8,128)(2,1)} %get-tuple-element.293), channel_id=1, source_target_pairs={{0,16},{4,20},{8,24},{12,28},{16,0},{20,4},{24,8},{28,12},{1,17},{... | collective-permute-start | bytes 3145736 | tf_op jit(solution)/shard_map/ppermute | solution.py:274
  194.1 74.0 %collective-permute-start.21 = (bf16[2,4,128,512]{3,2,1,0:T(8,128)(2,1)}, bf16[2,4,128,512]{3,2,1,0:T(8,128)(2,1)}, u32[]{:S(2)}, u32[]{:S(2)}) collective-permute-start(bf16[2,4,128,512]{3,2,1,0:T(8,128)(2,1)} %get-tuple-element.287), channel_id=1, source_target_pairs={{0,8},{4,12},{8,0},{12,4},{16,24},{20,28},{24,16},{28,20},{1,9},{5... | collective-permute-start | bytes 3145736 | tf_op jit(solution)/shard_map/ppermute | solution.py:274
  198.5 43.6 %collective-permute-start.27 = (bf16[2,4,128,512]{3,2,1,0:T(8,128)(2,1)}, bf16[2,4,128,512]{3,2,1,0:T(8,128)(2,1)S(1)}, u32[]{:S(2)}, u32[]{:S(2)}) collective-permute-start(bf16[2,4,128,512]{3,2,1,0:T(8,128)(2,1)} %get-tuple-element.291), channel_id=1, source_target_pairs={{0,8},{4,12},{8,0},{12,4},{16,24},{20,28},{24,16},{28,20},{1,9},{5... | collective-permute-start | bytes 3145736 | tf_op jit(solution)/shard_map/ppermute | solution.py:274
  242.1 24.5 %collective-permute-start.18 = (bf16[2,4,128,512]{3,2,1,0:T(8,128)(2,1)S(1)}, bf16[2,4,128,512]{3,2,1,0:T(8,128)(2,1)S(1)}, u32[]{:S(2)}, u32[]{:S(2)}) collective-permute-start(bf16[2,4,128,512]{3,2,1,0:T(8,128)(2,1)S(1)} %copy-done.46), channel_id=1, source_target_pairs={{0,16},{4,20},{8,24},{12,28},{16,0},{20,4},{24,8},{28,12},{1,17},{... | collective-permute-start | bytes 3145736 | tf_op jit(solution)/shard_map/ppermute | solution.py:274
  266.6 78.7 %collective-permute-start.28 = (bf16[4,4,128,512]{3,2,1,0:T(8,128)(2,1)}, bf16[4,4,128,512]{3,2,1,0:T(8,128)(2,1)}, u32[]{:S(2)}, u32[]{:S(2)}) collective-permute-start(bf16[4,4,128,512]{3,2,1,0:T(8,128)(2,1)} %bitcast.131.down_own_ref), channel_id=1, source_target_pairs={{0,4},{4,0},{8,12},{12,8},{16,20},{20,16},{24,28},{28,24},{1,5},{5... | collective-permute-start | bytes 6291464 | tf_op jit(solution)/shard_map/ppermute | solution.py:274
  268.1 117.7 %collective-permute-start.19 = (bf16[4,4,128,512]{3,2,1,0:T(8,128)(2,1)}, bf16[4,4,128,512]{3,2,1,0:T(8,128)(2,1)}, u32[]{:S(2)}, u32[]{:S(2)}) collective-permute-start(bf16[4,4,128,512]{3,2,1,0:T(8,128)(2,1)} %bitcast.111.up_own_ref), channel_id=1, source_target_pairs={{0,4},{4,0},{8,12},{12,8},{16,20},{20,16},{24,28},{28,24},{1,5},{5... | collective-permute-start | bytes 6291464 | tf_op jit(solution)/shard_map/ppermute | solution.py:274
  271.4 114.4 %collective-permute-start.22 = (bf16[4,4,128,512]{3,2,1,0:T(8,128)(2,1)}, bf16[4,4,128,512]{3,2,1,0:T(8,128)(2,1)}, u32[]{:S(2)}, u32[]{:S(2)}) collective-permute-start(bf16[4,4,128,512]{3,2,1,0:T(8,128)(2,1)} %bitcast.118.down_own_ref), channel_id=1, source_target_pairs={{0,4},{4,0},{8,12},{12,8},{16,20},{20,16},{24,28},{28,24},{1,5},{5... | collective-permute-start | bytes 6291464 | tf_op jit(solution)/shard_map/ppermute | solution.py:274
  274.2 71.1 %collective-permute-start.25 = (bf16[4,4,128,512]{3,2,1,0:T(8,128)(2,1)}, bf16[4,4,128,512]{3,2,1,0:T(8,128)(2,1)}, u32[]{:S(2)}, u32[]{:S(2)}) collective-permute-start(bf16[4,4,128,512]{3,2,1,0:T(8,128)(2,1)} %bitcast.124.up_own_ref), channel_id=1, source_target_pairs={{0,4},{4,0},{8,12},{12,8},{16,20},{20,16},{24,28},{28,24},{1,5},{5... | collective-permute-start | bytes 6291464 | tf_op jit(solution)/shard_map/ppermute | solution.py:274
  532.0 123.0 %collective-permute-start.31 = (bf16[4,4,2,128,256]{4,3,1,2,0:T(8,128)(2,1)}, bf16[4,4,2,128,256]{4,3,1,2,0:T(8,128)(2,1)}, u32[]{:S(2)}, u32[]{:S(2)}) collective-permute-start(bf16[4,4,2,128,256]{4,3,1,2,0:T(8,128)(2,1)} %pad_maximum_fusion.8), channel_id=1, source_target_pairs={{0,4},{4,0},{8,12},{12,8},{16,20},{20,16},{24,28},{28,24},{1,5},{5... | collective-permute-start | bytes 6291464 | tf_op jit(solution)/shard_map/ppermute | solution.py:274
  553.2 16.7 %collective-permute-start.29 = (bf16[1,2,1024]{2,1,0:T(2,128)(2,1)S(1)}, bf16[1,2,1024]{2,1,0:T(2,128)(2,1)S(1)}, u32[]{:S(2)}, u32[]{:S(2)}) collective-permute-start(bf16[1,2,1024]{2,1,0:T(2,128)(2,1)S(1)} %bitcast.790), channel_id=1, source_target_pairs={{0,1},{1,0},{2,3},{3,2},{4,5},{5,4},{6,7},{7,6},{8,9},{9,8},{10,11... | collective-permute-start | bytes 12296 | tf_op jit(solution)/shard_map/ppermute | solution.py:274
  569.9 21.7 %collective-permute-start.30 = (bf16[2,2,1024]{2,1,0:T(2,128)(2,1)S(1)}, bf16[2,2,1024]{2,1,0:T(2,128)(2,1)S(1)}, u32[]{:S(2)}, u32[]{:S(2)}) collective-permute-start(bf16[2,2,1024]{2,1,0:T(2,128)(2,1)S(1)} %pad_maximum_fusion.31), channel_id=1, source_target_pairs={{0,2},{1,3},{2,0},{3,1},{4,6},{5,7},{6,4},{7,5},{8,10},{9,11},{10,... | collective-permute-start | bytes 24584 | tf_op jit(solution)/shard_map/ppermute | solution.py:274
  591.0 56.8 %collective-permute-start.34 = (bf16[4,4,2,128,256]{4,1,3,0,2:T(4,128)(2,1)}, bf16[4,4,2,128,256]{4,1,3,0,2:T(4,128)(2,1)}, u32[]{:S(2)}, u32[]{:S(2)}) collective-permute-start(bf16[4,4,2,128,256]{4,1,3,0,2:T(4,128)(2,1)} %pad_maximum_fusion.9), channel_id=1, source_target_pairs={{0,4},{4,0},{8,12},{12,8},{16,20},{20,16},{24,28},{28,24},{1,5},{5... | collective-permute-start | bytes 6291464 | tf_op jit(solution)/shard_map/ppermute | solution.py:274
  591.0 68.0 %collective-permute-start.37 = (bf16[4,4,128,512]{3,2,1,0:T(8,128)(2,1)}, bf16[4,4,128,512]{3,2,1,0:T(8,128)(2,1)}, u32[]{:S(2)}, u32[]{:S(2)}) collective-permute-start(bf16[4,4,128,512]{3,2,1,0:T(8,128)(2,1)} %get-tuple-element.54), channel_id=1, source_target_pairs={{0,4},{4,0},{8,12},{12,8},{16,20},{20,16},{24,28},{28,24},{1,5},{5... | collective-permute-start | bytes 6291464 | tf_op jit(solution)/shard_map/ppermute | solution.py:274
  603.1 19.4 %collective-permute-start.52 = (f32[18,1024]{1,0:T(8,128)S(1)}, f32[18,1024]{1,0:T(8,128)S(1)}, u32[]{:S(2)}, u32[]{:S(2)}) collective-permute-start(f32[18,1024]{1,0:T(8,128)S(1)} %concatenate.185), channel_id=1, source_target_pairs={{0,4},{4,0},{8,12},{12,8},{16,20},{20,16},{24,28},{28,24},{1,5},{5... | collective-permute-start | bytes 221192 | tf_op jit(solution)/shard_map/ppermute | solution.py:274
  603.3 19.9 %collective-permute-start.49 = (bf16[8,8,1024]{2,1,0:T(8,128)(2,1)S(1)}, bf16[8,8,1024]{2,1,0:T(8,128)(2,1)S(1)}, u32[]{:S(2)}, u32[]{:S(2)}) collective-permute-start(bf16[8,8,1024]{2,1,0:T(8,128)(2,1)S(1)} %constant_dynamic-update-slice_fusion.72), channel_id=1, source_target_pairs={{0,8},{4,12},{8,0},{12,4},{16,24},{20,28},{24,16},{28,20},{1,9},{5... | collective-permute-start | bytes 393224 | tf_op jit(solution)/shard_map/ppermute | solution.py:274
  622.5 5.0 collective-permute-start.53
  623.2 15.1 %collective-permute-start.50 = (bf16[2,8,8,1024]{3,2,1,0:T(8,128)(2,1)S(1)}, bf16[2,8,8,1024]{3,2,1,0:T(8,128)(2,1)S(1)}, u32[]{:S(2)}, u32[]{:S(2)}) collective-permute-start(bf16[2,8,8,1024]{3,2,1,0:T(8,128)(2,1)S(1)} %get-tuple-element.304), channel_id=1, source_target_pairs={{0,16},{4,20},{8,24},{12,28},{16,0},{20,4},{24,8},{28,12},{1,17},{... | collective-permute-start | bytes 786440 | tf_op jit(solution)/shard_map/ppermute | solution.py:274
  627.5 6.0 collective-permute-start.54
  633.5 4.7 collective-permute-start.55
  638.2 6.6 collective-permute-start.56
  638.5 8.7 collective-permute-start.51
  644.9 17.9 %collective-permute-start.43 = (bf16[4,4,128,512]{3,2,1,0:T(8,128)(2,1)S(1)}, bf16[4,4,128,512]{3,2,1,0:T(8,128)(2,1)S(1)}, u32[]{:S(2)}, u32[]{:S(2)}) collective-permute-start(bf16[4,4,128,512]{3,2,1,0:T(8,128)(2,1)S(1)} %copy-done.138), channel_id=1, source_target_pairs={{0,4},{4,0},{8,12},{12,8},{16,20},{20,16},{24,28},{28,24},{1,5},{5... | collective-permute-start | bytes 6291464 | tf_op jit(solution)/shard_map/ppermute | solution.py:274
  647.2 17.1 %collective-permute-start.46 = (bf16[4,4,128,512]{3,2,1,0:T(8,128)(2,1)S(1)}, bf16[4,4,128,512]{3,2,1,0:T(8,128)(2,1)S(1)}, u32[]{:S(2)}, u32[]{:S(2)}) collective-permute-start(bf16[4,4,128,512]{3,2,1,0:T(8,128)(2,1)S(1)} %copy-done.137), channel_id=1, source_target_pairs={{0,4},{4,0},{8,12},{12,8},{16,20},{20,16},{24,28},{28,24},{1,5},{5... | collective-permute-start | bytes 6291464 | tf_op jit(solution)/shard_map/ppermute | solution.py:274
  647.9 18.6 %collective-permute-start.40 = (bf16[4,4,128,512]{3,2,1,0:T(8,128)(2,1)S(1)}, bf16[4,4,128,512]{3,2,1,0:T(8,128)(2,1)S(1)}, u32[]{:S(2)}, u32[]{:S(2)}) collective-permute-start(bf16[4,4,128,512]{3,2,1,0:T(8,128)(2,1)S(1)} %copy-done.136), channel_id=1, source_target_pairs={{0,4},{4,0},{8,12},{12,8},{16,20},{20,16},{24,28},{28,24},{1,5},{5... | collective-permute-start | bytes 6291464 | tf_op jit(solution)/shard_map/ppermute | solution.py:274
  655.1 26.0 %collective-permute-start.35 = (bf16[2,4,2,128,256]{4,3,1,2,0:T(8,128)(2,1)S(1)}, bf16[2,4,2,128,256]{4,3,1,2,0:T(8,128)(2,1)S(1)}, u32[]{:S(2)}, u32[]{:S(2)}) collective-permute-start(bf16[2,4,2,128,256]{4,3,1,2,0:T(8,128)(2,1)S(1)} %get-tuple-element.232), channel_id=1, source_target_pairs={{0,8},{4,12},{8,0},{12,4},{16,24},{20,28},{24,16},{28,20},{1,9},{5... | collective-permute-start | bytes 3145736 | tf_op jit(solution)/shard_map/ppermute | solution.py:274
  659.1 99.3 %collective-permute-start.32 = (bf16[2,4,2,128,256]{4,3,1,0,2:T(8,128)(2,1)}, bf16[2,4,2,128,256]{4,3,1,0,2:T(8,128)(2,1)}, u32[]{:S(2)}, u32[]{:S(2)}) collective-permute-start(bf16[2,4,2,128,256]{4,3,1,0,2:T(8,128)(2,1)} %fusion.21), channel_id=1, source_target_pairs={{0,16},{4,20},{8,24},{12,28},{16,0},{20,4},{24,8},{28,12},{1,17},{... | collective-permute-start | bytes 3145736 | tf_op jit(solution)/shard_map/ppermute | solution.py:274
  662.8 69.6 %collective-permute-start.38 = (bf16[2,4,128,512]{3,2,1,0:T(8,128)(2,1)S(1)}, bf16[2,4,128,512]{3,2,1,0:T(8,128)(2,1)S(1)}, u32[]{:S(2)}, u32[]{:S(2)}) collective-permute-start(bf16[2,4,128,512]{3,2,1,0:T(8,128)(2,1)S(1)} %get-tuple-element.228), channel_id=1, source_target_pairs={{0,16},{4,20},{8,24},{12,28},{16,0},{20,4},{24,8},{28,12},{1,17},{... | collective-permute-start | bytes 3145736 | tf_op jit(solution)/shard_map/ppermute | solution.py:274
  664.3 65.2 %collective-permute-start.44 = (bf16[2,4,128,512]{3,2,1,0:T(8,128)(2,1)S(1)}, bf16[2,4,128,512]{3,2,1,0:T(8,128)(2,1)S(1)}, u32[]{:S(2)}, u32[]{:S(2)}) collective-permute-start(bf16[2,4,128,512]{3,2,1,0:T(8,128)(2,1)S(1)} %get-tuple-element.224), channel_id=1, source_target_pairs={{0,16},{4,20},{8,24},{12,28},{16,0},{20,4},{24,8},{28,12},{1,17},{... | collective-permute-start | bytes 3145736 | tf_op jit(solution)/shard_map/ppermute | solution.py:274
  666.5 64.5 %collective-permute-start.47 = (bf16[2,4,128,512]{3,2,1,0:T(8,128)(2,1)S(1)}, bf16[2,4,128,512]{3,2,1,0:T(8,128)(2,1)S(1)}, u32[]{:S(2)}, u32[]{:S(2)}) collective-permute-start(bf16[2,4,128,512]{3,2,1,0:T(8,128)(2,1)S(1)} %get-tuple-element.226), channel_id=1, source_target_pairs={{0,8},{4,12},{8,0},{12,4},{16,24},{20,28},{24,16},{28,20},{1,9},{5... | collective-permute-start | bytes 3145736 | tf_op jit(solution)/shard_map/ppermute | solution.py:274
  681.1 74.5 %collective-permute-start.41 = (bf16[2,4,128,512]{3,2,1,0:T(8,128)(2,1)}, bf16[2,4,128,512]{3,2,1,0:T(8,128)(2,1)}, u32[]{:S(2)}, u32[]{:S(2)}) collective-permute-start(bf16[2,4,128,512]{3,2,1,0:T(8,128)(2,1)} %get-tuple-element.230), channel_id=1, source_target_pairs={{0,8},{4,12},{8,0},{12,4},{16,24},{20,28},{24,16},{28,20},{1,9},{5... | collective-permute-start | bytes 3145736 | tf_op jit(solution)/shard_map/ppermute | solution.py:274
  729.5 80.6 %collective-permute-start.36 = (bf16[4,2,128,256]{3,2,0,1:T(8,128)(2,1)}, bf16[4,2,128,256]{3,2,0,1:T(8,128)(2,1)}, u32[]{:S(2)}, u32[]{:S(2)}) collective-permute-start(bf16[4,2,128,256]{3,2,0,1:T(8,128)(2,1)} %fusion.69), channel_id=1, source_target_pairs={{0,16},{4,20},{8,24},{12,28},{16,0},{20,4},{24,8},{28,12},{1,17},{... | collective-permute-start | bytes 1572872 | tf_op jit(solution)/shard_map/ppermute | solution.py:274
  731.0 13.0 %collective-permute-start.45 = (bf16[4,128,512]{2,1,0:T(8,128)(2,1)S(1)}, bf16[4,128,512]{2,1,0:T(8,128)(2,1)S(1)}, u32[]{:S(2)}, u32[]{:S(2)}) collective-permute-start(bf16[4,128,512]{2,1,0:T(8,128)(2,1)S(1)} %fusion.66), channel_id=1, source_target_pairs={{0,8},{4,12},{8,0},{12,4},{16,24},{20,28},{24,16},{28,20},{1,9},{5... | collective-permute-start | bytes 1572872 | tf_op jit(solution)/shard_map/ppermute | solution.py:274
  732.5 21.7 %collective-permute-start.48 = (bf16[4,128,512]{2,1,0:T(8,128)(2,1)S(1)}, bf16[4,128,512]{2,1,0:T(8,128)(2,1)S(1)}, u32[]{:S(2)}, u32[]{:S(2)}) collective-permute-start(bf16[4,128,512]{2,1,0:T(8,128)(2,1)S(1)} %fusion.77), channel_id=1, source_target_pairs={{0,16},{4,20},{8,24},{12,28},{16,0},{20,4},{24,8},{28,12},{1,17},{... | collective-permute-start | bytes 1572872 | tf_op jit(solution)/shard_map/ppermute | solution.py:274
  744.0 17.8 %collective-permute-start.39 = (bf16[4,128,512]{2,1,0:T(8,128)(2,1)}, bf16[4,128,512]{2,1,0:T(8,128)(2,1)}, u32[]{:S(2)}, u32[]{:S(2)}) collective-permute-start(bf16[4,128,512]{2,1,0:T(8,128)(2,1)} %fusion.64), channel_id=1, source_target_pairs={{0,8},{4,12},{8,0},{12,4},{16,24},{20,28},{24,16},{28,20},{1,9},{5... | collective-permute-start | bytes 1572872 | tf_op jit(solution)/shard_map/ppermute | solution.py:274
  755.5 104.7 %all-reduce.12.cloned.1.call-start = ((), (), s32[]{:S(2)}) async-start(), calls=%async_computation.3 | async-start | bytes 2097152
  756.9 12.5 %collective-permute-start.42 = (bf16[4,128,512]{2,1,0:T(8,128)(2,1)S(1)}, bf16[4,128,512]{2,1,0:T(8,128)(2,1)S(1)}, u32[]{:S(2)}, u32[]{:S(2)}) collective-permute-start(bf16[4,128,512]{2,1,0:T(8,128)(2,1)S(1)} %fusion.73), channel_id=1, source_target_pairs={{0,16},{4,20},{8,24},{12,28},{16,0},{20,4},{24,8},{28,12},{1,17},{... | collective-permute-start | bytes 1572872 | tf_op jit(solution)/shard_map/ppermute | solution.py:274
  760.3 51.4 %collective-permute-start.33 = (bf16[4,2,128,256]{3,2,0,1:T(8,128)(2,1)}, bf16[4,2,128,256]{3,2,0,1:T(8,128)(2,1)}, u32[]{:S(2)}, u32[]{:S(2)}) collective-permute-start(bf16[4,2,128,256]{3,2,0,1:T(8,128)(2,1)} %fusion.67), channel_id=1, source_target_pairs={{0,8},{4,12},{8,0},{12,4},{16,24},{20,28},{24,16},{28,20},{1,9},{5... | collective-permute-start | bytes 1572872 | tf_op jit(solution)/shard_map/ppermute | solution.py:274
  807.7 106.6 %all-reduce.14.cloned.1.call-start = ((), (), s32[]{:S(2)}) async-start(), calls=%async_computation.4 | async-start | bytes 2097152
  919.9 3.6 collective-permute-start.58
  923.5 3.6 collective-permute-start.59
  930.8 4.5 collective-permute-start.61
  (153 other events, 3748.6 us)
Sparse Core Ops, SparseCore 0:
  10.2 30.5 all-gather.4
  42.9 45.8 all-gather.6
  755.6 50.3 all-reduce.9
  809.0 51.1 all-reduce.11
  863.0 51.1 all-reduce.13

commit v2 on v1

v2 whole, which is shorter than its diff:
```python
import jax
import jax.numpy as jnp
from jax import lax
from jax.experimental import pallas as pl
from jax.experimental.pallas import tpu as pltpu
from jax.sharding import PartitionSpec as P

D = 1024
HEADS = 16
HEAD = 64
FF = 4096
PATCHES = 577
FRAMES = 8
STEP = 10
ROWS = 592


norm_eps = 1e-05
beta_one = 0.9
beta_two = 0.95
adam_eps = 1e-08
decay_mat = 0.05
ema_keep = 0.7
clip_limit = 1.0
rate_mat = 0.02
rate_vec = 0.4
far_below = -1e30
bf16 = jnp.bfloat16
f32 = jnp.float32
NN = (((1,), (0,)), ((), ()))
NT = (((1,), (1,)), ((), ()))
TN = (((0,), (0,)), ((), ()))


def dot(left_side, right_side, dims=NN):
    return lax.dot_general(left_side, right_side, dims, preferred_element_type=f32)


def norm_rows(values, gain_row, shift_row):
    centre = values - jnp.mean(values, -1, keepdims=True)
    spread = jnp.mean(centre * centre, -1, keepdims=True)
    inverse = lax.rsqrt(spread + norm_eps)
    scaled = centre * inverse
    return (scaled * gain_row + shift_row, scaled, inverse)


def norm_back(gradient, scaled, inverse, gain_row):
    inner = gradient * gain_row
    return inverse * (
        inner
        - jnp.mean(inner, -1, keepdims=True)
        - scaled * jnp.mean(inner * scaled, -1, keepdims=True)
    )


def pad_rows(values, count):
    if values.shape[0] == count:
        return values
    extra = jnp.zeros((count - values.shape[0],) + values.shape[1:], values.dtype)
    return jnp.concatenate([values, extra], 0)


def head_pair(queries, key_rows, head):
    lane = lax.broadcasted_iota(jnp.int32, queries.shape, 1)
    key_lane = lax.broadcasted_iota(jnp.int32, key_rows.shape, 1)
    key_row = lax.broadcasted_iota(jnp.int32, key_rows.shape, 0)
    spare = HEAD * (1 - head)
    mask = jnp.where(
        (key_lane == spare) & (key_row > PATCHES), jnp.asarray(far_below, bf16), jnp.asarray(0, bf16)
    )
    keys_one = jnp.where((key_lane // HEAD) == head, key_rows, mask)
    queries_one = jnp.where(lane == spare, jnp.asarray(1, bf16), queries)
    return queries_one, keys_one


def attend_forward_kernel(q_ref, k_ref, v_ref, out_ref, total_ref):
    rows = q_ref.shape[1]
    key_count = -(-rows // 128) * 128
    queries = q_ref[0] * jnp.asarray(HEAD**-0.5, bf16)
    key_rows = pad_rows(k_ref[0], key_count)
    value_rows = pad_rows(v_ref[0], key_count)
    lane = lax.broadcasted_iota(jnp.int32, (rows, 128), 1)
    outs, totals = [], []
    for head in range(2):
        queries_one, keys_one = head_pair(queries, key_rows, head)
        scores = dot(queries_one, keys_one, NT)
        highest = jnp.max(scores, 1, keepdims=True)
        shifted = jnp.exp(scores - highest)
        total = jnp.sum(shifted, 1, keepdims=True)
        probability = (shifted * (1.0 / total)).astype(bf16)
        outs.append(dot(probability, value_rows))
        totals.append(highest + jnp.log(total))
    out_ref[0] = jnp.where(lane < HEAD, outs[0], outs[1]).astype(bf16)
    both = jnp.where(lane < HEAD, totals[0], totals[1]).T
    total_ref[0, 0] = jnp.concatenate([both[0:1], both[HEAD : HEAD + 1]], 0)


def attend_backward_kernel(q_ref, k_ref, v_ref, total_ref, grad_ref, *rest):
    dq_ref, dk_ref, dv_ref = rest[-3:]
    rows = q_ref.shape[1]
    query_count = -(-rows // 128) * 128
    queries = pad_rows(q_ref[0], query_count) * jnp.asarray(HEAD**-0.5, bf16)
    grads = pad_rows(grad_ref[0], query_count)
    key_rows = k_ref[0]
    value_rows = v_ref[0]
    keys_t = pad_rows(key_rows, query_count).astype(f32).T.astype(bf16)
    lane = lax.broadcasted_iota(jnp.int32, (rows, 128), 1)
    grad_q, grad_k, grad_v = [], [], []
    for head in range(2):
        queries_one, keys_one = head_pair(queries, key_rows, head)
        total = total_ref[0, 0, head : head + 1, :]
        if query_count > rows:
            total = jnp.concatenate([total, jnp.zeros((1, query_count - rows), f32)], 1)
        probability = jnp.exp(dot(keys_one, queries_one, NT) - total)
        values_one = jnp.where((lane // HEAD) == head, value_rows, jnp.asarray(0, bf16))
        grad_prob = dot(values_one, grads, NT)
        inner = jnp.sum(grad_prob * probability, 0, keepdims=True)
        grad_scores = (probability * (grad_prob - inner)).astype(bf16)
        grad_v.append(dot(probability.astype(bf16), grads))
        grad_k.append(dot(grad_scores, queries))
        grad_q.append(dot(keys_t[HEAD * head : HEAD * (head + 1)], pad_rows(grad_scores, query_count)))
    grad_q = jnp.concatenate(grad_q, 0) * HEAD**-0.5
    dq_ref[0] = grad_q.T[:rows].astype(bf16)
    dk_ref[0] = jnp.where(lane < HEAD, grad_k[0], grad_k[1]).astype(bf16)
    dv_ref[0] = jnp.where(lane < HEAD, grad_v[0], grad_v[1]).astype(bf16)


def attend_cost(frames, rows, width, matmuls):
    return pl.CostEstimate(
        flops=2 * matmuls * frames * rows * rows * width,
        bytes_accessed=2 * matmuls * frames * rows * width * 2,
        transcendentals=frames * rows * rows * width // HEAD,
    )


def attend_forward(queries, key_rows, value_rows):
    frames, rows, width = queries.shape
    spec = pl.BlockSpec((1, rows, 128), lambda f, h: (f, 0, h))
    return pl.pallas_call(
        attend_forward_kernel,
        grid=(frames, width // 128),
        in_specs=[spec] * 3,
        out_specs=[spec, pl.BlockSpec((1, 1, 2, rows), lambda f, h: (f, h, 0, 0))],
        out_shape=[
            jax.ShapeDtypeStruct((frames, rows, width), bf16),
            jax.ShapeDtypeStruct((frames, width // 128, 2, rows), f32),
        ],
        compiler_params=pltpu.CompilerParams(vmem_limit_bytes=48 << 20),
        cost_estimate=attend_cost(frames, rows, width, 4),
        name="attend_forward",
    )(queries, key_rows, value_rows)


def attend_backward(queries, key_rows, value_rows, totals, grads, begin, count, earlier=()):
    frames, rows, width = queries.shape
    spec = pl.BlockSpec((1, rows, 128), lambda f, h: (f, 0, h + begin))
    total_spec = pl.BlockSpec((1, 1, 2, rows), lambda f, h: (f, h + begin, 0, 0))
    return pl.pallas_call(
        attend_backward_kernel,
        grid=(frames, count),
        in_specs=[spec] * 3 + [total_spec, spec] + [pl.BlockSpec(memory_space=pl.ANY)] * len(earlier),
        out_specs=[spec] * 3,
        out_shape=[jax.ShapeDtypeStruct((frames, rows, width), bf16)] * 3,
        input_output_aliases={5 + i: i for i in range(len(earlier))},
        compiler_params=pltpu.CompilerParams(vmem_limit_bytes=48 << 20),
        cost_estimate=attend_cost(frames, rows, count * 128, 8),
        name="attend_backward",
    )(queries, key_rows, value_rows, totals, grads, *earlier)


def feed_kernel(
    n2_ref,
    n2t_ref,
    g_ref,
    gt_ref,
    bias_ref,
    up_own_ref,
    up_other_ref,
    down_own_ref,
    down_other_ref,
    out_ref,
    dn2_ref,
    dup_own_ref,
    dup_other_ref,
    ddown_own_ref,
    ddown_other_ref,
    db_ref,
    act_ref,
    dpre_ref,
):
    frames, rows = n2_ref.shape[:2]
    blocks, _, part, chunk = up_own_ref.shape
    half = blocks * part

    @pl.when(pl.program_id(0) == 0)
    def _():
        out_ref[...] = jnp.zeros_like(out_ref)
        dn2_ref[...] = jnp.zeros_like(dn2_ref)
        act_ref[...] = jnp.zeros_like(act_ref)
        dpre_ref[...] = jnp.zeros_like(dpre_ref)

    def whole(own_ref, other_ref):
        return jnp.concatenate(
            [own_ref[:, 0].reshape(half, chunk), other_ref[:, 0].reshape(half, chunk)], 0
        )

    first = whole(up_own_ref, up_other_ref)
    second = whole(down_own_ref, down_other_ref)
    bias_sum = jnp.zeros((1, chunk), f32)
    for frame in range(frames):
        place = pl.ds(frame * rows, rows)
        pre = dot(n2_ref[frame], first) + bias_ref[0]
        sigma = 1.0 / (1.0 + jnp.exp(-1.702 * pre))
        act = (pre * sigma).astype(bf16)
        act_ref[place] = act
        out_ref[frame] += dot(act, second, NT)
        grad_act = dot(g_ref[frame], second)
        grad_pre = grad_act * (sigma + 1.702 * pre * sigma * (1.0 - sigma))
        grad_low = grad_pre.astype(bf16)
        dpre_ref[place] = grad_low
        bias_sum += jnp.sum(grad_low.astype(f32), 0, keepdims=True)
        dn2_ref[frame] += dot(grad_low, first, NT)
    db_ref[0] = bias_sum

    def place_grad(left_ref, right_ref, own_ref, other_ref):
        for at, ref in ((0, own_ref), (half, other_ref)):
            grad = dot(left_ref[at : at + half], right_ref[...]).astype(bf16)
            ref[:, 0] = grad.reshape(blocks, part, chunk)

    place_grad(n2t_ref, dpre_ref, dup_own_ref, dup_other_ref)
    place_grad(gt_ref, act_ref, ddown_own_ref, ddown_other_ref)


def feed_forward(n2, n2t, grads, grads_t, bias, weights):
    frames, rows, _ = n2.shape
    blocks, ff_blocks, part, local = weights[0].shape
    chunk = min(512, local)
    per = local // chunk
    steps = ff_blocks * per
    deep = n2t.shape[1]
    whole3 = lambda n: (0, 0, 0)
    whole2 = lambda n: (0, 0)
    single = pl.Buffered(1)
    w_spec = pl.BlockSpec((blocks, 1, part, chunk), lambda n: (0, n // per, 0, n % per))
    return pl.pallas_call(
        feed_kernel,
        grid=(steps,),
        in_specs=[
            pl.BlockSpec((frames, rows, D), whole3, pipeline_mode=single),
            pl.BlockSpec((D, deep), whole2, pipeline_mode=single),
            pl.BlockSpec((frames, rows, D), whole3, pipeline_mode=single),
            pl.BlockSpec((D, deep), whole2, pipeline_mode=single),
            pl.BlockSpec((1, 1, chunk), lambda n: (n, 0, 0)),
        ]
        + [w_spec] * 4,
        out_specs=[pl.BlockSpec((frames, rows, D), whole3)] * 2
        + [w_spec] * 4
        + [pl.BlockSpec((1, 1, chunk), lambda n: (n, 0, 0))],
        out_shape=[jax.ShapeDtypeStruct((frames, rows, D), f32)] * 2
        + [jax.ShapeDtypeStruct(weights[0].shape, bf16)] * 4
        + [jax.ShapeDtypeStruct((steps, 1, chunk), f32)],
        scratch_shapes=[pltpu.VMEM((deep, chunk), bf16), pltpu.VMEM((deep, chunk), bf16)],
        compiler_params=pltpu.CompilerParams(vmem_limit_bytes=60 << 20),
        cost_estimate=pl.CostEstimate(
            flops=12 * frames * rows * D * ff_blocks * local,
            bytes_accessed=8 * D * ff_blocks * local + 16 * frames * rows * D,
            transcendentals=frames * rows * ff_blocks * local,
        ),
        name="feed_forward",
    )(n2, n2t, grads, grads_t, bias.reshape(steps, 1, chunk), *weights)


BLOCK = 128
BLOCKS = D // BLOCK


def permuted(ref, info_ref, first):
    return jnp.concatenate(
        [
            ref[:, pl.ds(pl.multiple_of(info_ref[first + i] * BLOCK, BLOCK), BLOCK)]
            for i in range(BLOCKS)
        ],
        1,
    )


def call(kernel, info, args, grid, in_specs, out_specs, out_shape, name, scratch=(), flops=0, vmem=56):
    moved = sum(a.size * a.dtype.itemsize for a in args)
    moved += sum(o.size * o.dtype.itemsize for o in out_shape)
    return pl.pallas_call(
        kernel,
        grid_spec=pltpu.PrefetchScalarGridSpec(
            num_scalar_prefetch=1,
            grid=grid,
            in_specs=in_specs,
            out_specs=out_specs,
            scratch_shapes=list(scratch),
        ),
        out_shape=out_shape,
        compiler_params=pltpu.CompilerParams(vmem_limit_bytes=vmem << 20),
        cost_estimate=pl.CostEstimate(flops=flops, bytes_accessed=moved, transcendentals=0),
        name=name,
    )(info, *args)


def shaped(dtype, *shape):
    return jax.ShapeDtypeStruct(shape, dtype)


def once(*block, at=None):
    index = at or (0,) * len(block)
    return pl.BlockSpec(block, lambda *_: index, pipeline_mode=pl.Buffered(1))


def kept(*block):
    index = (0,) * len(block)
    return pl.BlockSpec(block, lambda *_: index)


def row_count(frames):
    return -(-frames * ROWS // 128) * 128


def prepare_kernel(info_ref, tokens_ref, cot_ref, x_ref, g_ref, gt_ref, gsum_ref, hold_ref):
    frames = x_ref.shape[0]
    count = tokens_ref.shape[0]
    inside = lax.broadcasted_iota(jnp.int32, (ROWS, BLOCK), 0) < PATCHES
    hold_ref[...] = jnp.zeros_like(hold_ref)

    def padded(ref):
        hold_ref[0:count] = ref[...].astype(f32)
        return [
            jnp.where(inside, hold_ref[pl.ds(f * PATCHES, ROWS)], 0.0) for f in range(frames)
        ]

    for f, rows in enumerate(padded(tokens_ref)):
        x_ref[f] = rows.astype(bf16)
    grads = padded(cot_ref)
    for f, rows in enumerate(grads):
        g_ref[f] = rows.astype(bf16)
    full = pad_rows(jnp.concatenate(grads, 0), gt_ref.shape[1])
    gt_ref[...] = full.T.astype(bf16)
    gsum_ref[...] = jnp.sum(full, 0, keepdims=True)


def prepare(info, tokens, cotangent):
    count = tokens.shape[0]
    frames = count // PATCHES
    deep = row_count(frames)
    taken = pl.BlockSpec((count, BLOCK), lambda r, info_ref: (0, info_ref[r]))
    placed = pl.BlockSpec((frames, ROWS, BLOCK), lambda r, info_ref: (0, 0, r))
    return call(
        prepare_kernel,
        info,
        (tokens, cotangent),
        (BLOCKS,),
        [taken] * 2,
        [
            placed,
            placed,
            pl.BlockSpec((BLOCK, deep), lambda r, info_ref: (r, 0)),
            pl.BlockSpec((1, BLOCK), lambda r, info_ref: (0, r)),
        ],
        [
            shaped(bf16, frames, ROWS, D),
            shaped(bf16, frames, ROWS, D),
            shaped(bf16, D, deep),
            shaped(f32, 1, D),
        ],
        "prepare",
        [pltpu.VMEM((-(-((frames - 1) * PATCHES + ROWS) // 8) * 8, BLOCK), f32)],
    )


def plain_order_kernel(info_ref, in_ref, out_ref):
    out_ref[...] = permuted(in_ref, info_ref, BLOCKS)


def plain_order(info, values):
    return call(
        plain_order_kernel,
        info,
        (values,),
        (1,),
        [kept(*values.shape)],
        [kept(*values.shape)],
        [shaped(f32, *values.shape)],
        "plain_order",
    )[0]


def finish_kernel(info_ref, *refs):
    *in_refs, row_ref, out_ref = refs
    frames = in_refs[0].shape[0]
    for f in range(frames):
        rows = in_refs[0][f]
        for ref in in_refs[1:]:
            rows = rows + ref[f]
        if row_ref.shape[0] == 1:
            rows = rows + row_ref[...]
        else:
            class_row = row_ref[pl.ds(info_ref[2 * BLOCKS] * frames + f, 1)]
            first = lax.broadcasted_iota(jnp.int32, (ROWS, BLOCK), 0) == 0
            rows = rows + jnp.where(first, class_row, 0.0)
        out_ref[pl.ds(f * PATCHES, PATCHES)] = rows[:PATCHES]


def finish(info, parts, row, name):
    frames = parts[0].shape[0]
    taken = pl.BlockSpec((frames, ROWS, BLOCK), lambda d, info_ref: (0, 0, info_ref[BLOCKS + d]))
    row_spec = pl.BlockSpec((row.shape[0], BLOCK), lambda d, info_ref: (0, info_ref[BLOCKS + d]))
    return call(
        finish_kernel,
        info,
        (*parts, row),
        (BLOCKS,),
        [taken] * len(parts) + [row_spec],
        [pl.BlockSpec((frames * PATCHES, BLOCK), lambda d, info_ref: (0, d))],
        [shaped(f32, frames * PATCHES, D)],
        name,
    )[0]


def with_message(x_ref, msg_ref, info_ref, f):
    frames = x_ref.shape[0]
    message = msg_ref[pl.ds(info_ref[2 * BLOCKS] * frames + f, 1)]
    place = lax.broadcasted_iota(jnp.int32, (ROWS, D), 0) == PATCHES
    return jnp.where(place, message, x_ref[f].astype(f32))


def put_transposed(ref, rows):
    for c in range(BLOCKS):
        block = pad_rows(rows[:, c * BLOCK : (c + 1) * BLOCK].astype(f32), ref.shape[1])
        ref[c * BLOCK : (c + 1) * BLOCK] = block.T.astype(bf16)


def halves(own_ref, other_ref, *at):
    return [ref[(slice(None), *at)].reshape(D // 2, ref.shape[-1]) for ref in (own_ref, other_ref)]


def project_kernel(
    info_ref, x_ref, msg_ref, gain_ref, shift_ref, bq_ref, bv_ref, ao_ref, ap_ref, bo_ref, bp_ref,
    q_ref, k_ref, v_ref, ht_ref, h_ref,
):
    frames = x_ref.shape[0]

    @pl.when(pl.program_id(0) == 0)
    def _():
        for f in range(frames):
            rows = with_message(x_ref, msg_ref, info_ref, f)
            normed = norm_rows(rows, gain_ref[...], shift_ref[...])[0]
            h_ref[pl.ds(f * ROWS, ROWS)] = normed.astype(bf16)
        put_transposed(ht_ref, h_ref[...])

    sides = (slice(0, D // 2), slice(D // 2, D))
    for out_ref, weights, bias in (
        (q_ref, halves(ao_ref, ap_ref, 0, 0), bq_ref[...]),
        (k_ref, halves(ao_ref, ap_ref, 0, 1), 0.0),
        (v_ref, halves(bo_ref, bp_ref, 0, 0), bv_ref[...]),
    ):
        for f in range(frames):
            place = pl.ds(f * ROWS, ROWS)
            rows = dot(h_ref[place, sides[0]], weights[0]) + dot(h_ref[place, sides[1]], weights[1])
            out_ref[f] = (rows + bias).astype(bf16)


def project(info, x, message, vec_rel, vectors, attn):
    frames = x.shape[0]
    n, z, _, part, width = attn[0].shape
    deep = row_count(frames)
    bias = pl.BlockSpec((1, width), lambda j, info_ref: (0, j))
    a_spec = pl.BlockSpec((n, 1, 2, part, width), lambda j, info_ref: (0, j, 0, 0, 0))
    b_spec = pl.BlockSpec((n, 1, 1, part, width), lambda j, info_ref: (0, j, 0, 0, 0))
    out = pl.BlockSpec((frames, ROWS, width), lambda j, info_ref: (0, 0, j))
    return call(
        project_kernel,
        info,
        (x, message, vec_rel[0:1], vec_rel[1:2], vectors[10:11], vectors[11:12], *attn),
        (z,),
        [once(frames, ROWS, D), once(FRAMES, D), once(1, D), once(1, D), bias, bias]
        + [a_spec] * 2
        + [b_spec] * 2,
        [out] * 3 + [kept(D, deep)],
        [shaped(bf16, frames, ROWS, D)] * 3 + [shaped(bf16, D, deep)],
        "project",
        [pltpu.VMEM((frames * ROWS, D), bf16)],
        6 * frames * ROWS * D * D,
    )


def combine_kernel(
    info_ref, x_ref, a_ref, bias_ref, gain_ref, shift_ref, bo_ref, bp_ref, mid_ref, n2_ref, n2t_ref, hold_ref
):
    frames = x_ref.shape[0]
    z, width = bo_ref.shape[1], bo_ref.shape[-1]
    for f in range(frames):
        for side, ref in enumerate((bo_ref, bp_ref)):
            half = slice(side * D // 2, (side + 1) * D // 2)
            total = x_ref[f, :, half].astype(f32) + bias_ref[:, half]
            for j in range(z):
                weight = ref[:, j, 0].reshape(D // 2, width)
                total += dot(a_ref[f, :, j * width : (j + 1) * width], weight, NT)
            mid_ref[f, :, half] = total
        low = mid_ref[f].astype(bf16).astype(f32)
        normed = norm_rows(low, gain_ref[...], shift_ref[...])[0].astype(bf16)
        n2_ref[f] = normed
        hold_ref[pl.ds(f * ROWS, ROWS)] = normed
    put_transposed(n2t_ref, hold_ref[...])


def combine(info, x, attended, vec_rel, attn):
    frames = x.shape[0]
    n, z, _, part, width = attn[2].shape
    deep = row_count(frames)
    weight = once(n, z, 1, part, width, at=(0, 0, 1, 0, 0))
    return call(
        combine_kernel,
        info,
        (x, attended, vec_rel[12:13], vec_rel[2:3], vec_rel[3:4], attn[2], attn[3]),
        (1,),
        [once(frames, ROWS, D)] * 2 + [once(1, D)] * 3 + [weight] * 2,
        [once(frames, ROWS, D), once(frames, ROWS, D), once(D, deep)],
        [shaped(f32, frames, ROWS, D), shaped(bf16, frames, ROWS, D), shaped(bf16, D, deep)],
        "combine",
        [pltpu.VMEM((frames * ROWS, D), bf16)],
        2 * frames * ROWS * D * D,
    )


def between_kernel(
    info_ref, ea_ref, eb_ref, mid_ref, g_ref, a_ref, gain_ref, bo_ref, bp_ref,
    dmid_ref, da_ref, keep_ref, send_ref, sums_ref, total_ref, dmt_ref,
):
    f = pl.program_id(0)
    z, width = bo_ref.shape[1], bo_ref.shape[-1]
    n, part = bo_ref.shape[0], bo_ref.shape[3]
    grad = ea_ref[0] + eb_ref[0]
    low = mid_ref[0].astype(bf16).astype(f32)
    _, scaled, inverse = norm_rows(low, 1.0, 0.0)
    back = norm_back(grad, scaled, inverse, gain_ref[...])
    dmid = (g_ref[0].astype(f32) + back).astype(bf16)
    dmid_ref[0] = dmid
    sums = jnp.concatenate(
        [
            jnp.sum(grad * scaled, 0, keepdims=True),
            jnp.sum(grad, 0, keepdims=True),
            jnp.sum(dmid.astype(f32), 0, keepdims=True),
        ],
        0,
    )

    @pl.when(f == 0)
    def _():
        sums_ref[...] = jnp.zeros_like(sums_ref)
        total_ref[...] = jnp.zeros_like(total_ref)

    sums_ref[...] += sums
    for j in range(z):
        weights = halves(bo_ref, bp_ref, j, 0)
        rows = dot(dmid[:, : D // 2], weights[0]) + dot(dmid[:, D // 2 :], weights[1])
        da_ref[0, :, j * width : (j + 1) * width] = rows.astype(bf16)
    put_transposed(dmt_ref, dmid)
    attended = pad_rows(a_ref[0], dmt_ref.shape[1])
    for j in range(z):
        lanes = slice(j * width, (j + 1) * width)
        total_ref[:, lanes] += dot(dmt_ref[...], attended[:, lanes])

    @pl.when(f == pl.num_programs(0) - 1)
    def _():
        for j in range(z):
            lanes = slice(j * width, (j + 1) * width)
            for at, ref in ((0, keep_ref), (D // 2, send_ref)):
                ref[:, j] = total_ref[at : at + D // 2, lanes].astype(bf16).reshape(n, part, width)


def between(info, ea, eb, middle, grads, attended, vec_rel, attn):
    frames = ea.shape[0]
    n, z, _, part, width = attn[2].shape
    frame = pl.BlockSpec((1, ROWS, D), lambda f, info_ref: (f, 0, 0))
    weight = once(n, z, 1, part, width, at=(0, 0, 1, 0, 0))
    return call(
        between_kernel,
        info,
        (ea, eb, middle, grads, attended, vec_rel[2:3], attn[2], attn[3]),
        (frames,),
        [frame] * 5 + [once(1, D)] + [weight] * 2,
        [frame, frame, kept(n, z, part, width), kept(n, z, part, width), kept(3, D)],
        [shaped(bf16, frames, ROWS, D)] * 2
        + [shaped(bf16, n, z, part, width)] * 2
        + [shaped(f32, 3, D)],
        "between",
        [pltpu.VMEM((D, D), f32), pltpu.VMEM((D, row_count(1)), bf16)],
        4 * frames * ROWS * D * D,
    )


def project_grads_kernel(
    info_ref, ht_ref, dq_ref, dk_ref, dv_ref, ak_ref, as_ref, bk_ref, bs_ref, sq_ref, sv_ref
):
    frames = dq_ref.shape[0]
    deep = ht_ref.shape[1]
    n, part, width = bk_ref.shape[0], bk_ref.shape[2], bk_ref.shape[3]
    for w, ref in enumerate((dq_ref, dk_ref, dv_ref)):
        rows = pad_rows(jnp.concatenate([ref[f] for f in range(frames)], 0), deep)
        for at, a_ref, b_ref in ((0, ak_ref, bk_ref), (D // 2, as_ref, bs_ref)):
            grad = dot(ht_ref[at : at + D // 2], rows).astype(bf16).reshape(n, part, width)
            if w < 2:
                a_ref[:, 0, w] = grad
            else:
                b_ref[:, 0] = grad
        if w != 1:
            (sq_ref if w == 0 else sv_ref)[...] = jnp.sum(rows.astype(f32), 0, keepdims=True)


def project_grads(info, normed_t, grads, attn):
    frames = grads[0].shape[0]
    n, z, _, part, width = attn[0].shape
    block = pl.BlockSpec((frames, ROWS, width), lambda j, info_ref: (0, 0, j))
    a_spec = pl.BlockSpec((n, 1, 2, part, width), lambda j, info_ref: (0, j, 0, 0, 0))
    b_spec = pl.BlockSpec((n, 1, part, width), lambda j, info_ref: (0, j, 0, 0))
    row = pl.BlockSpec((1, width), lambda j, info_ref: (0, j))
    return call(
        project_grads_kernel,
        info,
        (normed_t, *grads),
        (z,),
        [once(*normed_t.shape)] + [block] * 3,
        [a_spec] * 2 + [b_spec] * 2 + [row] * 2,
        [shaped(bf16, n, z, 2, part, width)] * 2
        + [shaped(bf16, n, z, part, width)] * 2
        + [shaped(f32, 1, D)] * 2,
        "project_grads",
        (),
        6 * frames * ROWS * D * D,
    )


def project_back_kernel(
    info_ref, x_ref, msg_ref, dmid_ref, gain_ref, dq_ref, dk_ref, dv_ref, ao_ref, ap_ref, bo_ref, bp_ref,
    ing_ref, dmsg_ref, sums_ref, total_ref,
):
    frames = x_ref.shape[0]
    j = pl.program_id(0)

    @pl.when(j == 0)
    def _():
        total_ref[...] = jnp.zeros_like(total_ref)

    for side, (a_ref, b_ref) in enumerate(((ao_ref, bo_ref), (ap_ref, bp_ref))):
        half = slice(side * D // 2, (side + 1) * D // 2)
        width = a_ref.shape[-1]
        weights = [a_ref[:, 0, 0], a_ref[:, 0, 1], b_ref[:, 0, 0]]
        for f in range(frames):
            rows = jnp.zeros((ROWS, D // 2), f32)
            for ref, weight in zip((dq_ref, dk_ref, dv_ref), weights):
                rows += dot(ref[f], weight.reshape(D // 2, width), NT)
            total_ref[f, :, half] += rows

    @pl.when(j == pl.num_programs(0) - 1)
    def _():
        gain_sum, shift_sum = jnp.zeros((1, D), f32), jnp.zeros((1, D), f32)
        for f in range(frames):
            rows = with_message(x_ref, msg_ref, info_ref, f)
            _, scaled, inverse = norm_rows(rows, 1.0, 0.0)
            grad = total_ref[f]
            gain_sum += jnp.sum(grad * scaled, 0, keepdims=True)
            shift_sum += jnp.sum(grad, 0, keepdims=True)
            back = norm_back(grad, scaled, inverse, gain_ref[...])
            ing_ref[f] = dmid_ref[f].astype(f32) + back
            dmsg_ref[f] = back[PATCHES : PATCHES + 1]
        sums_ref[...] = jnp.concatenate([gain_sum, shift_sum], 0)


def project_back(info, x, message, dmid, vec_rel, grads, attn):
    frames = x.shape[0]
    n, z, _, part, width = attn[0].shape
    block = pl.BlockSpec((frames, ROWS, width), lambda j, info_ref: (0, 0, j))
    a_spec = pl.BlockSpec((n, 1, 2, part, width), lambda j, info_ref: (0, j, 0, 0, 0))
    b_spec = pl.BlockSpec((n, 1, 1, part, width), lambda j, info_ref: (0, j, 0, 0, 0))
    return call(
        project_back_kernel,
        info,
        (x, message, dmid, vec_rel[0:1], *grads, *attn),
        (z,),
        [once(frames, ROWS, D), once(FRAMES, D), once(frames, ROWS, D), once(1, D)]
        + [block] * 3
        + [a_spec] * 2
        + [b_spec] * 2,
        [once(frames, ROWS, D), kept(frames, 1, D), kept(2, D)],
        [shaped(f32, frames, ROWS, D), shaped(f32, frames, 1, D), shaped(f32, 2, D)],
        "project_back",
        [pltpu.VMEM((frames, ROWS, D), f32)],
        6 * frames * ROWS * D * D,
    )


def message_times(rows, refs, i):
    own, other = rows[:, : D // 2], rows[:, D // 2 :]
    cols = []
    for own_ref, other_ref in (refs[:2], refs[2:]):
        weights = halves(own_ref, other_ref, i)
        cols.append(dot(own, weights[0]) + dot(other, weights[1]))
    return jnp.concatenate(cols, 1)


def message_times_t(rows, refs, i):
    left, right = rows[:, : D // 2], rows[:, D // 2 :]
    first, second = halves(refs[0], refs[1], i), halves(refs[2], refs[3], i)
    return jnp.concatenate(
        [dot(left, first[s], NT) + dot(right, second[s], NT) for s in range(2)], 1
    )


def by_head(rows):
    full = jnp.concatenate([rows.astype(f32)] * HEADS, 0)
    return jnp.where(head_mask(), full, 0.0).astype(bf16)


def head_mask():
    shape = (HEADS * FRAMES, D)
    head = lax.broadcasted_iota(jnp.int32, shape, 0) // FRAMES
    return head == lax.broadcasted_iota(jnp.int32, shape, 1) // HEAD


def over_heads(rows):
    rows = jnp.where(head_mask(), rows, 0.0)
    return jnp.sum(rows.reshape(HEADS, FRAMES, D), 0)


def message_probability(queries, keys):
    scores = dot(by_head(queries), keys, NT) * HEAD**-0.5
    shifted = jnp.exp(scores - jnp.max(scores, 1, keepdims=True))
    return shifted * (1.0 / jnp.sum(shifted, 1, keepdims=True))


def message_forward_kernel(info_ref, cls_ref, vec_ref, *refs):
    weights, (msg_ref, first_ref, pack_ref, hold_ref) = refs[:4], refs[4:]

    def relative(rows):
        hold_ref[...] = rows
        return permuted(hold_ref, info_ref, 0)

    first = message_times(relative(cls_ref[...]).astype(bf16), weights, 0) + vec_ref[6:7]
    normed = norm_rows(first, vec_ref[4:5], vec_ref[5:6])[0].astype(bf16).astype(f32)
    normed_rel = relative(normed).astype(bf16)
    queries = (message_times(normed_rel, weights, 1) + vec_ref[7:8]).astype(bf16)
    keys = message_times(normed_rel, weights, 2).astype(bf16)
    values = (message_times(normed_rel, weights, 3) + vec_ref[8:9]).astype(bf16)
    probability = message_probability(queries, keys).astype(bf16)
    mixed = over_heads(dot(probability, values)).astype(bf16).astype(f32)
    message = first + message_times(relative(mixed).astype(bf16), weights, 4) + vec_ref[9:10]
    msg_ref[...] = relative(message)
    first_ref[...] = first
    for i, rows in enumerate((normed, mixed, queries, keys, values)):
        pack_ref[i] = rows.astype(f32)


def message_forward(info, class_rows, vectors, weights):
    one = kept(FRAMES, D)
    return call(
        message_forward_kernel,
        info,
        (class_rows, vectors, *weights),
        (1,),
        [one, kept(*vectors.shape)] + [once(*weights[0].shape)] * 4,
        [one, one, kept(5, FRAMES, D)],
        [shaped(f32, FRAMES, D), shaped(f32, FRAMES, D), shaped(f32, 5, FRAMES, D)],
        "message_forward",
        [pltpu.VMEM((FRAMES, D), f32)],
        10 * FRAMES * D * D,
    )


def message_backward_kernel(info_ref, dmsg_ref, first_ref, pack_ref, vec_ref, *refs):
    weights, (class_ref, sent_ref, sums_ref, hold_ref) = refs[:4], refs[4:]
    frames = dmsg_ref.shape[1]
    for i in range(dmsg_ref.shape[0]):
        place = lax.bitwise_xor(info_ref[2 * BLOCKS], i)
        for f in range(frames):
            hold_ref[i * frames + f : i * frames + f + 1] = dmsg_ref[place, f : f + 1]
    dmsg = permuted(hold_ref, info_ref, BLOCKS)

    def plain(rows):
        hold_ref[...] = rows
        return permuted(hold_ref, info_ref, BLOCKS)

    queries, keys, values = (pack_ref[i].astype(bf16) for i in (2, 3, 4))
    grad_mixed = plain(message_times_t(dmsg.astype(bf16), weights, 4)).astype(bf16)
    probability = message_probability(queries, keys)
    grads_big = by_head(grad_mixed)
    grad_prob = dot(grads_big, values, NT)
    inner = jnp.sum(grad_prob * probability, 1, keepdims=True)
    grad_scores = (probability * (grad_prob - inner)).astype(bf16)
    dq = (over_heads(dot(grad_scores, keys)) * HEAD**-0.5).astype(bf16)
    dk = (dot(grad_scores, by_head(queries), TN) * HEAD**-0.5).astype(bf16)
    dv = dot(probability.astype(bf16), grads_big, TN).astype(bf16)
    grad = plain(
        message_times_t(dq, weights, 1)
        + message_times_t(dk, weights, 2)
        + message_times_t(dv, weights, 3)
    )
    _, scaled, inverse = norm_rows(first_ref[...], 1.0, 0.0)
    back = norm_back(grad, scaled, inverse, vec_ref[4:5])
    dfirst = (dmsg + back).astype(bf16)
    class_ref[...] = message_times_t(dfirst, weights, 0)
    sent = [rows.astype(f32) for rows in (dfirst, dq, dk, dv, dmsg)]
    for i, rows in enumerate(sent):
        sent_ref[i] = rows
    sums = [grad * scaled, grad, sent[0], sent[1], sent[3], dmsg]
    sums_ref[...] = jnp.concatenate([jnp.sum(rows, 0, keepdims=True) for rows in sums], 0)


def message_backward(info, dmsg, first, pack, vectors, weights):
    one = kept(FRAMES, D)
    return call(
        message_backward_kernel,
        info,
        (dmsg, first, pack, vectors, *weights),
        (1,),
        [kept(*dmsg.shape), one, kept(*pack.shape), kept(*vectors.shape)]
        + [once(*weights[0].shape)] * 4,
        [one, kept(5, FRAMES, D), kept(6, D)],
        [shaped(f32, FRAMES, D), shaped(f32, 5, FRAMES, D), shaped(f32, 6, D)],
        "message_backward",
        [pltpu.VMEM((FRAMES, D), f32)],
        10 * FRAMES * D * D,
    )


def relative_order():
    return lax.axis_size("dp") * BLOCK == D


def make_info():
    place = lax.iota(jnp.int32, BLOCKS)
    if relative_order():
        mine = lax.axis_index("dp")
        differs = place ^ mine
        places = mine ^ (2 * (place % 4) + place // 4)
        blocks = (differs % 2) * 4 + differs // 2
    else:
        places = blocks = place
    return jnp.concatenate([places, blocks, lax.axis_index("tensor")[None]]).astype(jnp.int32)


def swap(values, axis, bit):
    pairs = [(i, i ^ bit) for i in range(lax.axis_size(axis))]
    return lax.ppermute(values, axis, pairs)


def bits_of(axis):
    size = lax.axis_size(axis)
    return [1 << i for i in range(size.bit_length() - 1)]


def after(values, *earlier):
    return lax.optimization_barrier((values, earlier))[0]


def gather_chips(values, which):
    if not which:
        values = jnp.stack([values, swap(values, "dp", 2)])
        values = jnp.stack([values, swap(values, "dp", 4)])
    else:
        values = jnp.stack([values, swap(values, "dp", 4)])
        values = jnp.stack([values, swap(values, "dp", 2)], 1)
    return values.reshape((4,) + values.shape[2:])


def gather_sides(values, which):
    if relative_order():
        own = gather_chips(values, which)
        return own, swap(own, "dp", 1)
    everything = lax.all_gather(values, "dp", axis=0)
    count = everything.shape[0] // 2
    return everything[:count], everything[count:]


def gather_small(values):
    if relative_order():
        own = gather_chips(values, 0)
        return jnp.concatenate([own, swap(own, "dp", 1)], 0)
    return lax.all_gather(values, "dp", axis=0)


def add_low(left_side, right_side):
    return (left_side.astype(f32) + right_side.astype(f32)).astype(bf16)


class Scatter:
    def __init__(self, keep, send, which):
        self.which, self.place = which, 0
        self.held = keep
        if relative_order():
            self.held = keep.reshape((2, 2) + keep.shape[1:])
            self.arrived = swap(send, "dp", 1).reshape(self.held.shape)
        else:
            self.total = lax.psum_scatter(
                jnp.concatenate([keep, send], 0), "dp", scatter_dimension=0, tiled=False
            )

    def step(self):
        if not relative_order():
            return self.total
        axis, bit = ((0, 4), (0, 2))[self.place] if not self.which else ((1, 2), (0, 4))[self.place]
        take = lambda v, i: lax.index_in_dim(v, i, axis, keepdims=False)
        going = add_low(take(self.held, 1), take(self.arrived, 1))
        self.held = add_low(take(self.held, 0), take(self.arrived, 0))
        self.arrived = swap(going, "dp", bit)
        self.place += 1
        return going

    def result(self):
        if not relative_order():
            return self.total
        return add_low(self.held, self.arrived)


def scatter_videos(values, earlier=None):
    if earlier is not None:
        values = after(values, earlier)
    return lax.psum_scatter(values, "tensor", scatter_dimension=0, tiled=False)


def scatter_videos_swaps(values):
    count = values.shape[0]
    if count != 4:
        return scatter_videos(values)
    mine = lax.axis_index("tensor")
    low, high = mine % 2, mine // 2
    pairs = values.reshape((2, 2) + values.shape[1:])
    take = lambda v, i, axis: lax.dynamic_index_in_dim(v, i, axis, keepdims=False)
    going, held = take(pairs, 1 - low, 1), take(pairs, low, 1)
    held = add_low(held, swap(going, "tensor", 1))
    going, held = take(held, 1 - high, 0), take(held, high, 0)
    return add_low(held, swap(going, "tensor", 2))


def sum_everywhere(values):
    for axis in ("dp", "tensor"):
        for bit in bits_of(axis):
            values = values + swap(values, axis, bit)
    return values


def gather_videos(values):
    values = values[None]
    for bit in bits_of("tensor"):
        values = jnp.concatenate([values, swap(values, "tensor", bit)], 0)
    return values


def adam_step(weight, first_moment, second_moment, gradient, factor, step_rate, decay_rate):
    clipped = gradient * factor
    first_new = beta_one * first_moment + (1.0 - beta_one) * clipped
    second_new = beta_two * second_moment + (1.0 - beta_two) * clipped * clipped
    update = (
        first_new
        / (1.0 - beta_one**STEP)
        / (jnp.sqrt(second_new / (1.0 - beta_two**STEP)) + adam_eps)
    )
    weight_new = weight - step_rate * (update + decay_rate * weight)
    return (first_new, second_new, weight_new)


def on_device(
    tokens,
    cotangent,
    attn_master,
    attn_first,
    attn_second,
    attn_ema,
    mlp_master,
    mlp_first,
    mlp_second,
    mlp_ema,
    msg_master,
    msg_first,
    msg_second,
    msg_ema,
    vec_master,
    vec_first,
    vec_second,
    vec_ema,
):
    z_index = lax.axis_index("tensor")
    z_count = lax.axis_size("tensor")
    dp_index = lax.axis_index("dp")
    part = attn_master.shape[0]
    local_width = attn_master.shape[2]
    local_ff = mlp_master.shape[2]
    frames = tokens.shape[0] // PATCHES
    half_ff = local_ff // 2
    info = make_info()

    attn_z = lax.all_gather(jnp.swapaxes(attn_master, 0, 1).astype(bf16), "tensor", axis=0)
    mlp_z = lax.all_gather(jnp.swapaxes(mlp_master, 0, 1).astype(bf16), "tensor", axis=0)
    class_own = tokens.reshape(frames, PATCHES, D)[:, 0]
    class_rows = gather_videos(class_own)
    order = lax.iota(jnp.int32, z_count) ^ z_index
    class_rows = jnp.take(class_rows, order, axis=0, mode="clip").reshape(FRAMES, D)
    msg_low = jnp.swapaxes(msg_master, 0, 1).astype(bf16)
    msg_w = [
        side
        for i in range(2)
        for side in gather_sides(msg_low[..., i * D // 2 : (i + 1) * D // 2], i)
    ]
    vec_rel = jnp.moveaxis(gather_small(vec_master.astype(bf16).T), 0, 1)
    vec_rel = vec_rel.reshape(-1, D).astype(f32)
    vectors = plain_order(info, vec_rel)
    ff_bias = vectors[14:].reshape(z_count, 2, half_ff)
    attn_w = [side for i in range(2) for side in gather_sides(attn_z[:, 2 * i : 2 * i + 2], i)]
    mlp_w = [
        [
            side
            for i in range(2)
            for side in gather_sides(mlp_z[:, i, :, j * half_ff : (j + 1) * half_ff], i)
        ]
        for j in range(2)
    ]

    x, grads, grads_t, grad_sum = prepare(info, tokens, cotangent)
    message, first_msg, msg_pack = message_forward(
        info, class_rows.astype(f32), vectors, msg_w
    )
    queries, key_rows, value_rows, normed_t = project(info, x, message, vec_rel, vectors, attn_w)
    attended, totals = attend_forward(queries, key_rows, value_rows)
    middle, n2, n2_t = combine(info, x, attended, vec_rel, attn_w)

    def feed(j):
        return feed_forward(n2, n2_t, grads, grads_t, ff_bias[:, j], mlp_w[j])

    def two(grads_of):
        return [Scatter(grads_of[2 * i], grads_of[2 * i + 1], i) for i in range(2)]

    out_0, dn2_0, *dw_0, db_0 = feed(0)
    sums_0 = two(dw_0)
    out_1, dn2_1, *dw_1, db_1 = feed(1)
    sums_1 = two(dw_1)
    going = [s.step() for s in sums_0]
    dmid, grad_attended, *grad_out_w, sums_two = between(
        info, after(dn2_0, *going), dn2_1, middle, grads, attended, vec_rel, attn_w
    )
    going = [s.step() for s in sums_1]
    pairs = HEADS // 2
    back = (queries, key_rows, value_rows, totals)
    grad_qkv = attend_backward(*back, after(grad_attended, *going), 0, pairs // 2)
    going = [s.step() for s in sums_0]
    grad_qkv = attend_backward(
        *back, after(grad_attended, *going), pairs // 2, pairs - pairs // 2, grad_qkv
    )
    mlp_0 = scatter_videos(jnp.stack([s.result() for s in sums_0], 1))
    going = [s.step() for s in sums_1]
    dqk_keep, dqk_send, dv_keep, dv_send, sum_q, sum_v = project_grads(
        info, after(normed_t, *going), grad_qkv, attn_w
    )
    sums_attn = [
        Scatter(dqk_keep, dqk_send, 0),
        Scatter(
            jnp.stack([dv_keep, grad_out_w[0]], 2), jnp.stack([dv_send, grad_out_w[1]], 2), 1
        ),
    ]
    mlp_1 = jnp.stack([s.result() for s in sums_1], 1)
    mlp_1 = scatter_videos(mlp_1, mlp_0)
    going = [s.step() for s in sums_attn]
    ing, dmsg, sums_one = project_back(
        info, after(x, *going), message, dmid, vec_rel, grad_qkv, attn_w
    )
    dmsg = gather_videos(dmsg[:, 0].astype(bf16)).astype(f32)
    going = [s.step() for s in sums_attn]
    grad_class, sent, sums_msg = message_backward(
        info, after(dmsg, *going), first_msg, msg_pack, vectors, msg_w
    )
    input_grad = finish(info, [ing], grad_class, "input_grad")
    block_output = finish(info, [middle, out_0, out_1], vec_rel[13:14], "block_output")
    attn_sum = jnp.concatenate([s.result() for s in sums_attn], 1)
    attn_grad = scatter_videos_swaps(attn_sum)

    sent = jnp.concatenate([class_rows[None], msg_pack[:2].astype(bf16), sent.astype(bf16)], 0)
    everyone = jnp.moveaxis(gather_small(sent), 0, 1).reshape(8, -1, D)
    mine = lax.dynamic_slice_in_dim(everyone[:3], dp_index * part, part, 2)
    msg_grad = jnp.stack(
        [
            dot(mine[0], everyone[3], TN),
            dot(mine[1], everyone[4], TN),
            dot(mine[1], everyone[5], TN),
            dot(mine[1], everyone[6], TN),
            dot(mine[2], everyone[7], TN),
        ],
        1,
    )

    relative = plain_order(info, jnp.concatenate([sums_one, sums_two, grad_sum], 0))
    ff_bias_grad = jnp.stack(
        [db.reshape(z_count, half_ff) for db in (db_0, db_1)], 1
    ).reshape(FF // D, D)
    sums_msg = jnp.where(z_index == 0, sums_msg, 0.0)
    table = sum_everywhere(
        jnp.concatenate([relative[:4], sums_msg, sum_q, sum_v, relative[4:], ff_bias_grad], 0)
    )
    vec_grad = lax.dynamic_slice_in_dim(table, dp_index * part, part, 1).T

    attn_grad = jnp.swapaxes(attn_grad, 0, 1).astype(f32)
    mlp_grad = jnp.swapaxes(jnp.concatenate([mlp_0, mlp_1], 2), 0, 1).astype(f32)

    keep_share = (z_index == 0).astype(f32)
    squares = (
        jnp.sum(attn_grad * attn_grad)
        + jnp.sum(mlp_grad * mlp_grad)
        + keep_share * (jnp.sum(msg_grad * msg_grad) + jnp.sum(vec_grad * vec_grad))
    )
    squares = sum_everywhere(jnp.broadcast_to(squares, (8, 128)))[0, 0]
    grad_norm = jnp.sqrt(squares)
    factor = clip_limit / jnp.maximum(grad_norm, clip_limit)

    def update(master, first, second, ema, grad, rate, decay):
        first_new, second_new, weight = adam_step(master, first, second, grad, factor, rate, decay)
        return grad, first_new, second_new, weight, ema_keep * ema + (1.0 - ema_keep) * weight

    return (
        block_output,
        input_grad,
        grad_norm,
        *update(attn_master, attn_first, attn_second, attn_ema, attn_grad, rate_mat, decay_mat),
        *update(mlp_master, mlp_first, mlp_second, mlp_ema, mlp_grad, rate_mat, decay_mat),
        *update(msg_master, msg_first, msg_second, msg_ema, msg_grad, rate_mat, decay_mat),
        *update(vec_master, vec_first, vec_second, vec_ema, vec_grad, rate_vec, 0.0),
    )


def solution(mesh):
    rows = P(("dp", "tensor"), None)
    split = P("dp", None, "tensor")
    copied = P("dp", None, None)
    table = P("dp", None)
    in_specs = (rows,) * 2 + (split,) * 8 + (copied,) * 4 + (table,) * 4
    out_specs = (rows,) * 2 + (P(),) + (split,) * 10 + (copied,) * 5 + (table,) * 5
    return jax.shard_map(
        on_device, mesh=mesh, in_specs=in_specs, out_specs=out_specs, check_vma=False
    )
```

time: 974 us -> 718 us (0.74)
  local copies, waits for them, and re-layouts: 197 us -> 48.4 us
  Pallas kernels: 160 us -> 287 us
  waiting for transfers between devices: 319 us -> 204 us
  matrix products: 70.4 us -> 1.26 us
  other arithmetic: 131 us -> 96.5 us
    pallas_call x1 -> x14, Pallas kernels: 45.7 us -> 173 us  [the longest x12 125 us: call(): pl.pallas_call(kernel, grid_spec=pltpu.PrefetchScalarGridSpec(num_scalar_...]
    unnamed x8 -> x6, waiting for transfers between devices: 124 us -> 23.9 us
    dot_general x27 -> x5, matrix products: 68.5 us -> 1.26 us  [dot(): lax.dot_general(left_side, right_side, dims, preferred_element_type=f32)]
    unnamed x425 -> x114, local copies, waits for them, and re-layouts: 74.7 us -> 21.7 us
    reshape x22 -> x2, local copies, waits for them, and re-layouts: 43.1 us -> 0.05 us  [gather_chips(): return values.reshape((4,) + values.shape[2:])]
    slice x15 -> x5, local copies, waits for them, and re-layouts: 27.6 us -> 5.42 us  [the longest x1 1.91 us: step(): take = lambda v, i: lax.index_in_dim(v, i, axis, keepdims=False)]
    ppermute x62 -> x64, waiting for transfers between devices: 194 us -> 173 us  [swap(): return lax.ppermute(values, axis, pairs)]
    add x3 -> x0, other arithmetic: 16.3 us -> none  [the longest x1 9.8 us: on_device(): middle + mlp_out + vec_rel[13]]
  transfers between devices with their start and end apart: 67 -> 68, of which waited for: 25 -> 26; matrix products, arithmetic and copies ran while one was open for 31% -> 16% of each run, Pallas kernels for 8% -> 35%
where the time goes in v2:
time: 718 us; the launch traced here: 710 us
  Pallas kernels  287 us (40%)
  waiting for transfers between devices  204 us (28%)
  other arithmetic  96.5 us (13%)
  starting transfers between devices  54.2 us (8%)
  local copies, waits for them, and re-layouts  48.4 us (7%)
  between operations  19.3 us (3%)
    ppermute x64, waiting for transfers between devices, swap(): return lax.ppermute(values, axis, pairs)  173 us
    pallas_call x12, Pallas kernels, call(): pl.pallas_call(kernel, grid_spec=pltpu.PrefetchScalarGridSpec(num_scalar_...  125 us
    pallas_call x2, Pallas kernels, feed_forward(): pl.pallas_call(feed_kernel, grid=(steps,), in_specs=[pl.BlockSpec((frames...  81.4 us
    ppermute x64, starting transfers between devices, swap(): return lax.ppermute(values, axis, pairs)  54 us
    pallas_call x2, Pallas kernels, attend_backward(): pl.pallas_call(attend_backward_kernel, grid=(frames, count), in_specs=[sp...  47.3 us
    pallas_call x1, Pallas kernels, attend_forward(): pl.pallas_call(attend_forward_kernel, grid=(frames, width // 128), in_spe...  32.7 us
    convert_element_type x15, other arithmetic, add_low(): return (left_side.astype(f32) + right_side.astype(f32)).astype(bf16)  28.3 us
    unnamed x6, waiting for transfers between devices  23.9 us
  transfers between devices with their start and end apart: 68, of which 26 were waited for; matrix products, arithmetic and copies ran while one was open for 16% of the time, Pallas kernels for 35%

profile of v2, /device:TPU:0, one launch (start us, length us, event | category | flops | bytes accessed | tf_op | source)
XLA Modules:
  0.0 710.1 jit_solution(2310327927173618724)
XLA Ops:
  9.3 2.3 copy.207
  12.2 3.0 collective-permute-start.5
  15.2 14.7 %collective-permute-done.5 = bf16[5,128,512]{2,1,0:T(8,128)(2,1)S(1)} collective-permute-done((bf16[5,128,512]{2,1,0:T(8,128)(2,1)S(1)}, bf16[5,128,512]{2,1,0:T(8,128)(2,1)S(1)}, u32[]{:S(2)}, u32[]{:S(2)}) %collective-permute-start.5) | collective-permute-done | bytes 655392 | tf_op jit(solution)/shard_map/ppermute | solution.py:848
  33.6 7.3 %all-gather.5.cloned.1.call-done = bf16[16,128,256]{2,1,0:T(8,128)(2,1)} async-done(((bf16[4,128,256]{2,1,0:T(8,128)(2,1)}), bf16[16,128,256]{2,1,0:T(8,128)(2,1)}) %all-gather.5.cloned.1.call-update) | async-done | bytes 1048592 | tf_op jit(solution)/shard_map/all_gather | solution.py:996
  40.8 2.5 slice_bitcast_fusion.25
  44.8 31.2 %collective-permute-done.8 = bf16[5,128,512]{2,1,0:T(8,128)(2,1)} collective-permute-done((bf16[5,128,512]{2,1,0:T(8,128)(2,1)S(1)}, bf16[5,128,512]{2,1,0:T(8,128)(2,1)}, u32[]{:S(2)}, u32[]{:S(2)}) %collective-permute-start.8) | collective-permute-done | bytes 655392 | tf_op jit(solution)/shard_map/ppermute | solution.py:848
  76.0 2.7 fusion.68
  84.5 3.5 reshape.286
  91.1 2.7 fusion.67
  94.5 3.5 collective-permute-done.14
  98.0 2.5 collective-permute-start.1
  100.5 2.5 fusion.66
  103.0 5.3 collective-permute-done.2
  111.0 3.2 slice_bitcast_fusion.6
  114.2 6.0 collective-permute-done.3
  126.1 16.8 %collective-permute-done.23 = bf16[4,128,512]{2,1,0:T(8,128)(2,1)S(1)} collective-permute-done((bf16[4,128,512]{2,1,0:T(8,128)(2,1)S(1)}, bf16[4,128,512]{2,1,0:T(8,128)(2,1)S(1)}, u32[]{:S(2)}, u32[]{:S(2)}) %collective-permute-start.23) | collective-permute-done | bytes 524320 | tf_op jit(solution)/shard_map/ppermute | solution.py:848
  147.3 2.7 fusion.62
  150.1 4.8 collective-permute-done.17
  155.9 2.8 pad_maximum_fusion.2
  158.7 2.8 pad_maximum_fusion.3
  161.6 15.9 %collective-permute-done.20 = bf16[4,128,512]{2,1,0:T(8,128)(2,1)} collective-permute-done((bf16[4,128,512]{2,1,0:T(8,128)(2,1)}, bf16[4,128,512]{2,1,0:T(8,128)(2,1)}, u32[]{:S(2)}, u32[]{:S(2)}) %collective-permute-start.20) | collective-permute-done | bytes 524320 | tf_op jit(solution)/shard_map/ppermute | solution.py:848
  178.0 2.1 fusion.65
  182.3 8.8 %prepare.1 = (bf16[2,592,1024]{2,1,0:T(8,128)(2,1)}, bf16[2,592,1024]{2,1,0:T(8,128)(2,1)}, bf16[1024,1280]{1,0:T(8,128)(2,1)}, f32[1,1024]{1,0:T(1,128)}) custom-call(s32[17]{0:T(128)} %pad_add_fusion.info_ref, bf16[1154,1024]{1,0:T(8,128)(2,1)} %tokens_ref.1, bf16[1154,1024]{1,0:T(8,128)(2,1)} %cot_ref.1), custom_call_target="tpu_custom_call" | custom-call | bytes 12201984 | tf_op jit(solution)/shard_map/prepare/pallas_call | solution.py:290
  193.0 2.2 plain_order.2.vec_ref
  200.0 3.5 pad_maximum_fusion.7
  203.5 2.0 collective-permute-done.18
  207.6 7.8 %message_forward.1 = (f32[8,1024]{1,0:T(8,128)}, f32[8,1024]{1,0:T(8,128)}, f32[5,8,1024]{2,1,0:T(8,128)}) custom-call(s32[17]{0:T(128)} %pad_add_fusion.info_ref, f32[8,1024]{1,0:T(8,128)} %reshape.305.cls_ref, f32[18,1024]{1,0:T(8,128)} %plain_order.2.vec_ref, bf16[4,5,128,512]{3,2,1,0:T(8,128)(2,1)} %bitcast.340, ...), custom_call_target="tpu_custom_call" | custom-call | flops 83886080 | bytes 10821632 | tf_op jit(solution)/shard_map/message_forward/pallas_call | solution.py:290
  215.3 2.8 pad_maximum_fusion.4
  218.1 4.0 collective-permute-done.21
  222.9 15.6 %project.1 = (bf16[2,592,1024]{2,1,0:T(8,128)(2,1)}, bf16[2,592,1024]{2,1,0:T(8,128)(2,1)}, bf16[2,592,1024]{2,1,0:T(8,128)(2,1)}, bf16[1024,1280]{1,0:T(8,128)(2,1)}) custom-call(s32[17]{0:T(128)} %pad_add_fusion.info_ref, bf16[2,592,1024]{2,1,0:T(8,128)(2,1)} %get-tuple-element.125.x_ref, f32[8,1024]{1,0:T(8,128)} %get-tuple-element.84.msg_ref, ...), custom_call_target="tpu_custom_call" | custom-call | flops 7449083904 | bytes 20758528 | tf_op jit(solution)/shard_map/project/pallas_call | solution.py:290
  240.2 32.7 %attend_forward.1 = (bf16[2,592,1024]{2,1,0:T(8,128)(2,1)S(1)}, f32[2,8,2,592]{3,2,1,0:T(2,128)S(1)}) custom-call(bf16[2,592,1024]{2,1,0:T(8,128)(2,1)S(1)} %copy-done.1, bf16[2,592,1024]{2,1,0:T(8,128)(2,1)} %get-tuple-element.86.k_ref, bf16[2,592,1024]{2,1,0:T(8,128)(2,1)} %get-tuple-element.87.v_ref), custom_call_target="tpu_custom_call" | custom-call | flops 5742002176 | bytes 19398656 | tf_op jit(solution)/shard_map/attend_forward/pallas_call | solution.py:139
  274.3 10.9 %combine.1 = (f32[2,592,1024]{2,1,0:T(8,128)}, bf16[2,592,1024]{2,1,0:T(8,128)(2,1)}, bf16[1024,1280]{1,0:T(8,128)(2,1)}) custom-call(s32[17]{0:T(128)} %pad_add_fusion.info_ref, bf16[2,592,1024]{2,1,0:T(8,128)(2,1)} %get-tuple-element.125.x_ref, bf16[2,592,1024]{2,1,0:T(8,128)(2,1)} %copy-done, f32[1,1024]{1,0:T(1,128)} %bitcast.384, f32[1,1024]{1,0:T(1,128)} %bitcast.377, ...), custom_call_target="tpu_custom_call" | custom-call | flops 2483027968 | bytes 18952192 | tf_op jit(solution)/shard_map/combine/pallas_call | solution.py:290
  285.2 40.4 %feed_forward.3 = (f32[2,592,1024]{2,1,0:T(8,128)}, f32[2,592,1024]{2,1,0:T(8,128)}, bf16[4,4,128,512]{3,2,1,0:T(8,128)(2,1)}, bf16[4,4,128,512]{3,2,1,0:T(8,128...) custom-call(bf16[2,592,1024]{2,1,0:T(8,128)(2,1)} %get-tuple-element.90.n2_ref, ...), custom_call_target="tpu_custom_call" | custom-call | flops 29796335616 | bytes 36175872 | tf_op jit(solution)/shard_map/feed_forward/pallas_call | solution.py:245
  326.2 41.0 %feed_forward.2 = (f32[2,592,1024]{2,1,0:T(8,128)}, f32[2,592,1024]{2,1,0:T(8,128)}, bf16[4,4,128,512]{3,2,1,0:T(8,128)(2,1)}, bf16[4,4,128,512]{3,2,1,0:T(8,128...) custom-call(bf16[2,592,1024]{2,1,0:T(8,128)(2,1)} %get-tuple-element.90.n2_ref, ...), custom_call_target="tpu_custom_call" | custom-call | flops 29796335616 | bytes 36175872 | tf_op jit(solution)/shard_map/feed_forward/pallas_call | solution.py:245
  367.8 3.3 add_convert_fusion.11
  371.6 3.3 add_convert_fusion.9
  382.0 18.5 %between.1 = (bf16[2,592,1024]{2,1,0:T(8,128)(2,1)}, bf16[2,592,1024]{2,1,0:T(8,128)(2,1)}, bf16[4,4,128,256]{3,2,1,0:T(8,128)(2,1)}, bf16[4,4,128,256]{3,2,1,0:T(8,128)(2,1)}, f32[3,1024]{1,0:T(4,128)}) custom-call(s32[17]{0:T(128)} %pad_add_fusion.info_ref, f32[2,592,1024]{2,1,0:T(8,128)} %get-tuple-element.108.ea_ref, ...), custom_call_target="tpu_custom_call" | custom-call | flops 4966055936 | bytes 30556160 | tf_op jit(solution)/shard_map/between/pallas_call | solution.py:290
  400.5 23.7 %attend_backward.2 = (bf16[2,592,1024]{2,1,0:T(8,128)(2,1)S(1)}, bf16[2,592,1024]{2,1,0:T(8,128)(2,1)S(1)}, bf16[2,592,1024]{2,1,0:T(8,128)(2,1)}) custom-call(bf16[2,592,1024]{2,1,0:T(8,128)(2,1)} %get-tuple-element.85.q_ref, bf16[2,592,1024]{2,1,0:T(8,128)(2,1)} %get-tuple-element.86.k_ref, bf16[2,592,1024]{2,1,0:T(8,128)(2,1)} %get-tuple-element.87.v_ref, ...), custom_call_target="tpu_custom_call" | custom-call | flops 5742002176 | bytes 19398656 | tf_op jit(solution)/shard_map/attend_backward/pallas_call | solution.py:158
  430.2 23.7 %attend_backward.3 = (bf16[2,592,1024]{2,1,0:T(8,128)(2,1)S(1)}, bf16[2,592,1024]{2,1,0:T(8,128)(2,1)S(1)}, bf16[2,592,1024]{2,1,0:T(8,128)(2,1)}) custom-call(bf16[2,592,1024]{2,1,0:T(8,128)(2,1)} %get-tuple-element.85.q_ref, bf16[2,592,1024]{2,1,0:T(8,128)(2,1)} %get-tuple-element.86.k_ref, ...), custom_call_target="tpu_custom_call", output_to_operand_aliasing={{0}: (5, {}), {1}: (6, {}), {2}: (7, {})} | custom-call | flops 5742002176 | bytes 19398656 | tf_op jit(solution)/shard_map/attend_backward/pallas_call | solution.py:158
  456.8 13.6 %project_grads.1 = (bf16[4,4,2,128,256]{4,3,2,1,0:T(8,128)(2,1)}, bf16[4,4,2,128,256]{4,3,2,1,0:T(8,128)(2,1)}, bf16[4,4,128,256]{3,2,1,0:T(8,128)(2,1)}, bf16[4...) custom-call(s32[17]{0:T(128)} %pad_add_fusion.info_ref, ...), custom_call_target="tpu_custom_call" | custom-call | flops 7449083904 | bytes 16195584 | tf_op jit(solution)/shard_map/project_grads/pallas_call | solution.py:290
  471.1 2.8 pad_maximum_fusion.8
  476.9 8.8 %collective-permute-done.48 = bf16[4,128,512]{2,1,0:T(8,128)(2,1)} collective-permute-done((bf16[4,128,512]{2,1,0:T(8,128)(2,1)}, bf16[4,128,512]{2,1,0:T(8,128)(2,1)}, u32[]{:S(2)}, u32[]{:S(2)}) %collective-permute-start.48) | collective-permute-done | bytes 524320 | tf_op jit(solution)/shard_map/ppermute | solution.py:848
  491.7 4.8 collective-permute-done.50
  502.3 3.2 add_convert_fusion.1
  511.4 19.0 %project_back.1 = (f32[2,592,1024]{2,1,0:T(8,128)}, f32[2,1,1024]{2,1,0:T(1,128)}, f32[2,1024]{1,0:T(2,128)}) custom-call(s32[17]{0:T(128)} %pad_add_fusion.info_ref, bf16[2,592,1024]{2,1,0:T(8,128)(2,1)} %get-tuple-element.125.x_ref, f32[8,1024]{1,0:T(8,128)} %get-tuple-element.84.msg_ref, bf16[2,592,1024]{2,1,0:T(8,128)(2,1)} %get-tuple-element.126.dmid_ref, ...), custom_call_target="tpu_custom_call" | custom-call | flops 7449083904 | bytes 25415680 | tf_op jit(solution)/shard_map/project_back/pallas_call | solution.py:290
  532.7 11.1 %all-reduce.5.cloned.1.call-done = bf16[4,2,128,512]{3,2,0,1:T(8,128)(2,1)} async-done(((bf16[4,2,128,512]{3,2,0,1:T(8,128)(2,1)}), bf16[4,2,128,512]{3,2,0,1:T(8,128)(2,1)}) %all-reduce.5.cloned.1.call-update) | async-done | bytes 1048592
  545.5 2.0 collective-permute-start.40
  548.9 2.0 plain_order.3
  556.2 9.2 %message_backward.1 = (f32[8,1024]{1,0:T(8,128)}, f32[5,8,1024]{2,1,0:T(8,128)}, f32[6,1024]{1,0:T(8,128)}) custom-call(s32[17]{0:T(128)} %pad_add_fusion.info_ref, f32[4,2,1024]{2,1,0:T(2,128)} %maximum_convert_fusion.dmsg_ref, f32[8,1024]{1,0:T(8,128)} %get-tuple-element.130.first_ref, f32[5,8,1024]{2,1,0:T(8,128)} %get-tuple-element.131.pack_ref, ...), custom_call_target="tpu_custom_call" | custom-call | flops 83886080 | bytes 11010048 | tf_op jit(solution)/shard_map/message_backward/pallas_call | solution.py:290
  571.0 3.5 collective-permute-done.55
  576.6 3.6 collective-permute-done.56
  582.0 8.1 %collective-permute-done.57 = f32[18,1024]{1,0:T(8,128)S(1)} collective-permute-done((f32[18,1024]{1,0:T(8,128)S(1)}, f32[18,1024]{1,0:T(8,128)S(1)}, u32[]{:S(2)}, u32[]{:S(2)}) %collective-permute-start.57) | collective-permute-done | bytes 73760 | tf_op jit(solution)/shard_map/ppermute | solution.py:848
  590.2 12.7 %all-reduce.7.cloned.1.call-done = bf16[4,2,128,512]{3,2,0,1:T(8,128)(2,1)} async-done(((bf16[4,2,128,512]{3,2,0,1:T(8,128)(2,1)}), bf16[4,2,128,512]{3,2,0,1:T(8,128)(2,1)}) %all-reduce.7.cloned.1.call-update) | async-done | bytes 1048592
  609.8 8.7 %collective-permute-done.43 = bf16[4,2,128,256]{3,2,1,0:T(8,128)(2,1)S(1)} collective-permute-done((bf16[4,2,128,256]{3,2,1,0:T(8,128)(2,1)}, bf16[4,2,128,256]{3,2,1,0:T(8,128)(2,1)S(1)}, u32[]{:S(2)}, u32[]{:S(2)}) %collective-permute-start.43) | collective-permute-done | bytes 524320 | tf_op jit(solution)/shard_map/ppermute | solution.py:848
  621.6 11.6 %collective-permute-done.45 = bf16[2,4,128,256]{3,1,2,0:T(4,128)(2,1)S(1)} collective-permute-done((bf16[2,4,128,256]{3,1,2,0:T(4,128)(2,1)S(1)}, bf16[2,4,128,256]{3,1,2,0:T(4,128)(2,1)S(1)}, u32[]{:S(2)}, u32[]{:S(2)}) %collective-permute-start.45) | collective-permute-done | bytes 524320 | tf_op jit(solution)/shard_map/ppermute | solution.py:848
  637.7 9.9 %collective-permute-done.46 = bf16[4,128,256]{2,0,1:T(4,128)(2,1)S(1)} collective-permute-done((bf16[4,128,256]{2,0,1:T(4,128)(2,1)}, bf16[4,128,256]{2,0,1:T(4,128)(2,1)S(1)}, u32[]{:S(2)}, u32[]{:S(2)}) %collective-permute-start.46) | collective-permute-done | bytes 262176 | tf_op jit(solution)/shard_map/ppermute | solution.py:848
  647.7 2.5 multiply_reduce_fusion.2
  653.8 2.5 collective-permute-done.60
  657.5 2.5 collective-permute-done.61
  660.0 9.9 %block_output.1 = f32[1154,1024]{1,0:T(8,128)} custom-call(s32[17]{0:T(128)} %pad_add_fusion.info_ref, f32[2,592,1024]{2,1,0:T(8,128)} %get-tuple-element.89.refs_0_.mid_ref, f32[2,592,1024]{2,1,0:T(8,128)} %get-tuple-element.94.refs_1_, f32[2,592,1024]{2,1,0:T(8,128)} %get-tuple-element.95.refs_2_, f32[1,1024]{1,0:T(1,128)} %bitcast.376), custom_call_target="tpu_custom_call" | custom-call | bytes 19279872 | tf_op jit(solution)/shard_map/block_output/pallas_call | solution.py:290
  673.6 7.7 %input_grad.1 = f32[1154,1024]{1,0:T(8,128)} custom-call(s32[17]{0:T(128)} %pad_add_fusion.info_ref, f32[2,592,1024]{2,1,0:T(8,128)} %get-tuple-element.127.refs_0_, f32[8,1024]{1,0:T(8,128)} %get-tuple-element.132.refs_1_), custom_call_target="tpu_custom_call" | custom-call | bytes 9609216 | tf_op jit(solution)/shard_map/input_grad/pallas_call | solution.py:290
  682.5 4.2 fusion.24
  693.9 5.3 multiply_add_fusion
  699.4 2.3 multiply_add_fusion.2
  (321 shorter events, 134.0 us)
Async XLA Ops:
  7.2 33.6 %all-gather.5.cloned.1.call-start = ((), (), s32[]{:S(2)}) async-start(), calls=%async_computation | async-start | bytes 1310720 | tf_op jit(solution)/shard_map/all_gather | solution.py:996
  9.2 101.7 %all-gather.7.cloned.1.call-start = ((), (), s32[]{:S(2)}) async-start(), calls=%async_computation.1 | async-start | bytes 2621440 | tf_op jit(solution)/shard_map/all_gather | solution.py:997
  11.6 532.2 %all-reduce.5.cloned.1.call-start = ((), (), s32[]{:S(2)}) async-start(), calls=%async_computation.2 | async-start | bytes 2097152
  12.2 17.7 %collective-permute-start.5 = (bf16[5,128,512]{2,1,0:T(8,128)(2,1)S(1)}, bf16[5,128,512]{2,1,0:T(8,128)(2,1)S(1)}, u32[]{:S(2)}, u32[]{:S(2)}) collective-permute-start(bf16[5,128,512]{2,1,0:T(8,128)(2,1)S(1)} %get-tuple-element.282), channel_id=1, source_target_pairs={{0,8},{4,12},{8,0},{12,4},{16,24},{20,28},{24,16},{28,20},{1,9},{5... | collective-permute-start | bytes 1966088 | tf_op jit(solution)/shard_map/ppermute | solution.py:848
  31.6 48.6 %collective-permute-start.6 = (bf16[2,5,128,512]{3,2,1,0:T(8,128)(2,1)}, bf16[2,5,128,512]{3,2,1,0:T(8,128)(2,1)S(1)}, u32[]{:S(2)}, u32[]{:S(2)}) collective-permute-start(bf16[2,5,128,512]{3,2,1,0:T(8,128)(2,1)} %get-tuple-element.284), channel_id=1, source_target_pairs={{0,16},{4,20},{8,24},{12,28},{16,0},{20,4},{24,8},{28,12},{1,17},{... | collective-permute-start | bytes 3932168 | tf_op jit(solution)/shard_map/ppermute | solution.py:848
  33.3 42.7 %collective-permute-start.8 = (bf16[5,128,512]{2,1,0:T(8,128)(2,1)S(1)}, bf16[5,128,512]{2,1,0:T(8,128)(2,1)}, u32[]{:S(2)}, u32[]{:S(2)}) collective-permute-start(bf16[5,128,512]{2,1,0:T(8,128)(2,1)S(1)} %get-tuple-element.281), channel_id=1, source_target_pairs={{0,16},{4,20},{8,24},{12,28},{16,0},{20,4},{24,8},{28,12},{1,17},{... | collective-permute-start | bytes 1966088 | tf_op jit(solution)/shard_map/ppermute | solution.py:848
  43.3 47.2 %collective-permute-start.11 = (bf16[4,2,128,256]{3,2,1,0:T(8,128)(2,1)}, bf16[4,2,128,256]{3,2,1,0:T(8,128)(2,1)}, u32[]{:S(2)}, u32[]{:S(2)}) collective-permute-start(bf16[4,2,128,256]{3,2,1,0:T(8,128)(2,1)} %get-tuple-element.300), channel_id=1, source_target_pairs={{0,8},{4,12},{8,0},{12,4},{16,24},{20,28},{24,16},{28,20},{1,9},{5... | collective-permute-start | bytes 1572872 | tf_op jit(solution)/shard_map/ppermute | solution.py:848
  78.7 42.1 %collective-permute-start.9 = (bf16[2,5,128,512]{3,2,1,0:T(8,128)(2,1)}, bf16[2,5,128,512]{3,2,1,0:T(8,128)(2,1)}, u32[]{:S(2)}, u32[]{:S(2)}) collective-permute-start(bf16[2,5,128,512]{3,2,1,0:T(8,128)(2,1)} %get-tuple-element.278), channel_id=1, source_target_pairs={{0,8},{4,12},{8,0},{12,4},{16,24},{20,28},{24,16},{28,20},{1,9},{5... | collective-permute-start | bytes 3932168 | tf_op jit(solution)/shard_map/ppermute | solution.py:848
  82.8 94.7 %collective-permute-start.7 = (bf16[4,5,128,512]{3,2,1,0:T(8,128)(2,1)S(1)}, bf16[4,5,128,512]{3,2,1,0:T(8,128)(2,1)}, u32[]{:S(2)}, u32[]{:S(2)}) collective-permute-start(bf16[4,5,128,512]{3,2,1,0:T(8,128)(2,1)S(1)} %bitcast.339), channel_id=1, source_target_pairs={{0,4},{4,0},{8,12},{12,8},{16,20},{20,16},{24,28},{28,24},{1,5},{5... | collective-permute-start | bytes 7864328 | tf_op jit(solution)/shard_map/ppermute | solution.py:848
  82.9 15.1 %collective-permute-start.14 = (bf16[4,2,128,256]{3,2,1,0:T(8,128)(2,1)}, bf16[4,2,128,256]{3,2,1,0:T(8,128)(2,1)}, u32[]{:S(2)}, u32[]{:S(2)}) collective-permute-start(bf16[4,2,128,256]{3,2,1,0:T(8,128)(2,1)} %get-tuple-element.299), channel_id=1, source_target_pairs={{0,16},{4,20},{8,24},{12,28},{16,0},{20,4},{24,8},{28,12},{1,17},{... | collective-permute-start | bytes 1572872 | tf_op jit(solution)/shard_map/ppermute | solution.py:848
  88.8 4.9 collective-permute-start
  90.5 17.8 %collective-permute-start.2 = (bf16[18,128]{1,0:T(8,128)(2,1)S(1)}, bf16[18,128]{1,0:T(8,128)(2,1)S(1)}, u32[]{:S(2)}, u32[]{:S(2)}) collective-permute-start(bf16[18,128]{1,0:T(8,128)(2,1)S(1)} %get-tuple-element.320), channel_id=1, source_target_pairs={{0,8},{4,12},{8,0},{12,4},{16,24},{20,28},{24,16},{28,20},{1,9},{5... | collective-permute-start | bytes 13832 | tf_op jit(solution)/shard_map/ppermute | solution.py:848
  93.7 30.9 %collective-permute-start.12 = (bf16[2,4,2,128,256]{4,3,2,1,0:T(8,128)(2,1)}, bf16[2,4,2,128,256]{4,3,2,1,0:T(8,128)(2,1)}, u32[]{:S(2)}, u32[]{:S(2)}) collective-permute-start(bf16[2,4,2,128,256]{4,3,2,1,0:T(8,128)(2,1)} %get-tuple-element.302), channel_id=1, source_target_pairs={{0,16},{4,20},{8,24},{12,28},{16,0},{20,4},{24,8},{28,12},{1,17},{... | collective-permute-start | bytes 3145736 | tf_op jit(solution)/shard_map/ppermute | solution.py:848
  98.0 11.4 %collective-permute-start.1 = (bf16[2,2,1024]{2,1,0:T(2,128)(2,1)S(1)}, bf16[2,2,1024]{2,1,0:T(2,128)(2,1)S(1)}, u32[]{:S(2)}, u32[]{:S(2)}) collective-permute-start(bf16[2,2,1024]{2,1,0:T(2,128)(2,1)S(1)} %pad_maximum_fusion.29), channel_id=1, source_target_pairs={{0,2},{1,3},{2,0},{3,1},{4,6},{5,7},{6,4},{7,5},{8,10},{9,11},{10,... | collective-permute-start | bytes 24584 | tf_op jit(solution)/shard_map/ppermute | solution.py:848
  108.3 37.0 %collective-permute-start.15 = (bf16[2,4,2,128,256]{4,3,2,1,0:T(8,128)(2,1)}, bf16[2,4,2,128,256]{4,3,2,1,0:T(8,128)(2,1)}, u32[]{:S(2)}, u32[]{:S(2)}) collective-permute-start(bf16[2,4,2,128,256]{4,3,2,1,0:T(8,128)(2,1)} %get-tuple-element.296), channel_id=1, source_target_pairs={{0,8},{4,12},{8,0},{12,4},{16,24},{20,28},{24,16},{28,20},{1,9},{5... | collective-permute-start | bytes 3145736 | tf_op jit(solution)/shard_map/ppermute | solution.py:848
  109.4 10.8 %collective-permute-start.3 = (bf16[2,18,128]{2,1,0:T(8,128)(2,1)S(1)}, bf16[2,18,128]{2,1,0:T(8,128)(2,1)S(1)}, u32[]{:S(2)}, u32[]{:S(2)}) collective-permute-start(bf16[2,18,128]{2,1,0:T(8,128)(2,1)S(1)} %get-tuple-element.318), channel_id=1, source_target_pairs={{0,16},{4,20},{8,24},{12,28},{16,0},{20,4},{24,8},{28,12},{1,17},{... | collective-permute-start | bytes 27656 | tf_op jit(solution)/shard_map/ppermute | solution.py:848
  120.2 22.7 %collective-permute-start.23 = (bf16[4,128,512]{2,1,0:T(8,128)(2,1)S(1)}, bf16[4,128,512]{2,1,0:T(8,128)(2,1)S(1)}, u32[]{:S(2)}, u32[]{:S(2)}) collective-permute-start(bf16[4,128,512]{2,1,0:T(8,128)(2,1)S(1)} %get-tuple-element.273), channel_id=1, source_target_pairs={{0,8},{4,12},{8,0},{12,4},{16,24},{20,28},{24,16},{28,20},{1,9},{5... | collective-permute-start | bytes 1572872 | tf_op jit(solution)/shard_map/ppermute | solution.py:848
  124.1 79.4 %collective-permute-start.10 = (bf16[4,5,128,512]{3,2,1,0:T(8,128)(2,1)}, bf16[4,5,128,512]{3,2,1,0:T(8,128)(2,1)}, u32[]{:S(2)}, u32[]{:S(2)}) collective-permute-start(bf16[4,5,128,512]{3,2,1,0:T(8,128)(2,1)} %bitcast.19.refs_2_), channel_id=1, source_target_pairs={{0,4},{4,0},{8,12},{12,8},{16,20},{20,16},{24,28},{28,24},{1,5},{5... | collective-permute-start | bytes 7864328 | tf_op jit(solution)/shard_map/ppermute | solution.py:848
  124.6 22.2 %collective-permute-start.26 = (bf16[4,128,512]{2,1,0:T(8,128)(2,1)}, bf16[4,128,512]{2,1,0:T(8,128)(2,1)}, u32[]{:S(2)}, u32[]{:S(2)}) collective-permute-start(bf16[4,128,512]{2,1,0:T(8,128)(2,1)} %get-tuple-element.276), channel_id=1, source_target_pairs={{0,16},{4,20},{8,24},{12,28},{16,0},{20,4},{24,8},{28,12},{1,17},{... | collective-permute-start | bytes 1572872 | tf_op jit(solution)/shard_map/ppermute | solution.py:848
  142.8 12.1 %collective-permute-start.17 = (bf16[4,128,512]{2,1,0:T(8,128)(2,1)}, bf16[4,128,512]{2,1,0:T(8,128)(2,1)}, u32[]{:S(2)}, u32[]{:S(2)}) collective-permute-start(bf16[4,128,512]{2,1,0:T(8,128)(2,1)} %get-tuple-element.275), channel_id=1, source_target_pairs={{0,8},{4,12},{8,0},{12,4},{16,24},{20,28},{24,16},{28,20},{1,9},{5... | collective-permute-start | bytes 1572872 | tf_op jit(solution)/shard_map/ppermute | solution.py:848
  145.3 34.8 %collective-permute-start.24 = (bf16[2,4,128,512]{3,2,1,0:T(8,128)(2,1)}, bf16[2,4,128,512]{3,2,1,0:T(8,128)(2,1)}, u32[]{:S(2)}, u32[]{:S(2)}) collective-permute-start(bf16[2,4,128,512]{3,2,1,0:T(8,128)(2,1)} %get-tuple-element.290), channel_id=1, source_target_pairs={{0,16},{4,20},{8,24},{12,28},{16,0},{20,4},{24,8},{28,12},{1,17},{... | collective-permute-start | bytes 3145736 | tf_op jit(solution)/shard_map/ppermute | solution.py:848
  146.8 30.6 %collective-permute-start.20 = (bf16[4,128,512]{2,1,0:T(8,128)(2,1)}, bf16[4,128,512]{2,1,0:T(8,128)(2,1)}, u32[]{:S(2)}, u32[]{:S(2)}) collective-permute-start(bf16[4,128,512]{2,1,0:T(8,128)(2,1)} %get-tuple-element.274), channel_id=1, source_target_pairs={{0,16},{4,20},{8,24},{12,28},{16,0},{20,4},{24,8},{28,12},{1,17},{... | collective-permute-start | bytes 1572872 | tf_op jit(solution)/shard_map/ppermute | solution.py:848
  154.9 42.3 %collective-permute-start.27 = (bf16[2,4,128,512]{3,2,1,0:T(8,128)(2,1)}, bf16[2,4,128,512]{3,2,1,0:T(8,128)(2,1)}, u32[]{:S(2)}, u32[]{:S(2)}) collective-permute-start(bf16[2,4,128,512]{3,2,1,0:T(8,128)(2,1)} %get-tuple-element.288), channel_id=1, source_target_pairs={{0,8},{4,12},{8,0},{12,4},{16,24},{20,28},{24,16},{28,20},{1,9},{5... | collective-permute-start | bytes 3145736 | tf_op jit(solution)/shard_map/ppermute | solution.py:848
  177.5 44.9 %collective-permute-start.13 = (bf16[4,4,2,128,256]{4,3,2,1,0:T(8,128)(2,1)}, bf16[4,4,2,128,256]{4,3,2,1,0:T(8,128)(2,1)}, u32[]{:S(2)}, u32[]{:S(2)}) collective-permute-start(bf16[4,4,2,128,256]{4,3,2,1,0:T(8,128)(2,1)} %bitcast.28.ao_ref), channel_id=1, source_target_pairs={{0,4},{4,0},{8,12},{12,8},{16,20},{20,16},{24,28},{28,24},{1,5},{5... | collective-permute-start | bytes 6291464 | tf_op jit(solution)/shard_map/ppermute | solution.py:848
  177.5 45.4 %collective-permute-start.16 = (bf16[4,4,2,128,256]{4,3,2,1,0:T(8,128)(2,1)}, bf16[4,4,2,128,256]{4,3,2,1,0:T(8,128)(2,1)}, u32[]{:S(2)}, u32[]{:S(2)}) collective-permute-start(bf16[4,4,2,128,256]{4,3,2,1,0:T(8,128)(2,1)} %bitcast.34.bo_ref), channel_id=1, source_target_pairs={{0,4},{4,0},{8,12},{12,8},{16,20},{20,16},{24,28},{28,24},{1,5},{5... | collective-permute-start | bytes 6291464 | tf_op jit(solution)/shard_map/ppermute | solution.py:848
  180.1 25.4 %collective-permute-start.18 = (bf16[2,4,128,512]{3,2,1,0:T(8,128)(2,1)}, bf16[2,4,128,512]{3,2,1,0:T(8,128)(2,1)}, u32[]{:S(2)}, u32[]{:S(2)}) collective-permute-start(bf16[2,4,128,512]{3,2,1,0:T(8,128)(2,1)} %get-tuple-element.294), channel_id=1, source_target_pairs={{0,16},{4,20},{8,24},{12,28},{16,0},{20,4},{24,8},{28,12},{1,17},{... | collective-permute-start | bytes 3145736 | tf_op jit(solution)/shard_map/ppermute | solution.py:848
  197.2 24.9 %collective-permute-start.21 = (bf16[2,4,128,512]{3,2,1,0:T(8,128)(2,1)S(1)}, bf16[2,4,128,512]{3,2,1,0:T(8,128)(2,1)S(1)}, u32[]{:S(2)}, u32[]{:S(2)}) collective-permute-start(bf16[2,4,128,512]{3,2,1,0:T(8,128)(2,1)S(1)} %get-tuple-element.292), channel_id=1, source_target_pairs={{0,8},{4,12},{8,0},{12,4},{16,24},{20,28},{24,16},{28,20},{1,9},{5... | collective-permute-start | bytes 3145736 | tf_op jit(solution)/shard_map/ppermute | solution.py:848
  203.5 81.7 %collective-permute-start.25 = (bf16[4,4,128,512]{3,2,1,0:T(8,128)(2,1)S(1)}, bf16[4,4,128,512]{3,2,1,0:T(8,128)(2,1)}, u32[]{:S(2)}, u32[]{:S(2)}) collective-permute-start(bf16[4,4,128,512]{3,2,1,0:T(8,128)(2,1)S(1)} %bitcast.349), channel_id=1, source_target_pairs={{0,4},{4,0},{8,12},{12,8},{16,20},{20,16},{24,28},{28,24},{1,5},{5... | collective-permute-start | bytes 6291464 | tf_op jit(solution)/shard_map/ppermute | solution.py:848
  205.5 79.7 %collective-permute-start.28 = (bf16[4,4,128,512]{3,2,1,0:T(8,128)(2,1)}, bf16[4,4,128,512]{3,2,1,0:T(8,128)(2,1)}, u32[]{:S(2)}, u32[]{:S(2)}) collective-permute-start(bf16[4,4,128,512]{3,2,1,0:T(8,128)(2,1)} %bitcast.65.down_own_ref), channel_id=1, source_target_pairs={{0,4},{4,0},{8,12},{12,8},{16,20},{20,16},{24,28},{28,24},{1,5},{5... | collective-permute-start | bytes 6291464 | tf_op jit(solution)/shard_map/ppermute | solution.py:848
  222.1 104.1 %collective-permute-start.19 = (bf16[4,4,128,512]{3,2,1,0:T(8,128)(2,1)}, bf16[4,4,128,512]{3,2,1,0:T(8,128)(2,1)}, u32[]{:S(2)}, u32[]{:S(2)}) collective-permute-start(bf16[4,4,128,512]{3,2,1,0:T(8,128)(2,1)} %bitcast.45.up_own_ref), channel_id=1, source_target_pairs={{0,4},{4,0},{8,12},{12,8},{16,20},{20,16},{24,28},{28,24},{1,5},{5... | collective-permute-start | bytes 6291464 | tf_op jit(solution)/shard_map/ppermute | solution.py:848
  222.3 103.9 %collective-permute-start.22 = (bf16[4,4,128,512]{3,2,1,0:T(8,128)(2,1)S(1)}, bf16[4,4,128,512]{3,2,1,0:T(8,128)(2,1)}, u32[]{:S(2)}, u32[]{:S(2)}) collective-permute-start(bf16[4,4,128,512]{3,2,1,0:T(8,128)(2,1)S(1)} %bitcast.351), channel_id=1, source_target_pairs={{0,4},{4,0},{8,12},{12,8},{16,20},{20,16},{24,28},{28,24},{1,5},{5... | collective-permute-start | bytes 6291464 | tf_op jit(solution)/shard_map/ppermute | solution.py:848
  325.7 42.2 %collective-permute-start.29 = (bf16[4,4,128,512]{3,2,1,0:T(8,128)(2,1)}, bf16[4,4,128,512]{3,2,1,0:T(8,128)(2,1)}, u32[]{:S(2)}, u32[]{:S(2)}) collective-permute-start(bf16[4,4,128,512]{3,2,1,0:T(8,128)(2,1)} %get-tuple-element.98), channel_id=1, source_target_pairs={{0,4},{4,0},{8,12},{12,8},{16,20},{20,16},{24,28},{28,24},{1,5},{5... | collective-permute-start | bytes 6291464 | tf_op jit(solution)/shard_map/ppermute | solution.py:848
  325.8 45.9 %collective-permute-start.31 = (bf16[4,4,128,512]{3,2,1,0:T(8,128)(2,1)}, bf16[4,4,128,512]{3,2,1,0:T(8,128)(2,1)}, u32[]{:S(2)}, u32[]{:S(2)}) collective-permute-start(bf16[4,4,128,512]{3,2,1,0:T(8,128)(2,1)} %get-tuple-element.100), channel_id=1, source_target_pairs={{0,4},{4,0},{8,12},{12,8},{16,20},{20,16},{24,28},{28,24},{1,5},{5... | collective-permute-start | bytes 6291464 | tf_op jit(solution)/shard_map/ppermute | solution.py:848
  367.2 9.2 %collective-permute-start.33 = (bf16[4,4,128,512]{3,2,1,0:T(8,128)(2,1)}, bf16[4,4,128,512]{3,2,1,0:T(8,128)(2,1)S(1)}, u32[]{:S(2)}, u32[]{:S(2)}) collective-permute-start(bf16[4,4,128,512]{3,2,1,0:T(8,128)(2,1)} %get-tuple-element.105), channel_id=1, source_target_pairs={{0,4},{4,0},{8,12},{12,8},{16,20},{20,16},{24,28},{28,24},{1,5},{5... | collective-permute-start | bytes 6291464 | tf_op jit(solution)/shard_map/ppermute | solution.py:848
  367.4 11.5 %collective-permute-start.34 = (bf16[4,4,128,512]{3,2,1,0:T(8,128)(2,1)}, bf16[4,4,128,512]{3,2,1,0:T(8,128)(2,1)S(1)}, u32[]{:S(2)}, u32[]{:S(2)}) collective-permute-start(bf16[4,4,128,512]{3,2,1,0:T(8,128)(2,1)} %get-tuple-element.107), channel_id=1, source_target_pairs={{0,4},{4,0},{8,12},{12,8},{16,20},{20,16},{24,28},{28,24},{1,5},{5... | collective-permute-start | bytes 6291464 | tf_op jit(solution)/shard_map/ppermute | solution.py:848
  371.1 53.0 %collective-permute-start.30 = (bf16[2,4,128,512]{3,2,1,0:T(8,128)(2,1)}, bf16[2,4,128,512]{3,2,1,0:T(8,128)(2,1)S(1)}, u32[]{:S(2)}, u32[]{:S(2)}) collective-permute-start(bf16[2,4,128,512]{3,2,1,0:T(8,128)(2,1)} %get-tuple-element.264), channel_id=1, source_target_pairs={{0,16},{4,20},{8,24},{12,28},{16,0},{20,4},{24,8},{28,12},{1,17},{... | collective-permute-start | bytes 3145736 | tf_op jit(solution)/shard_map/ppermute | solution.py:848
  375.0 50.3 %collective-permute-start.32 = (bf16[2,4,128,512]{3,2,1,0:T(8,128)(2,1)}, bf16[2,4,128,512]{3,2,1,0:T(8,128)(2,1)}, u32[]{:S(2)}, u32[]{:S(2)}) collective-permute-start(bf16[2,4,128,512]{3,2,1,0:T(8,128)(2,1)} %get-tuple-element.262), channel_id=1, source_target_pairs={{0,8},{4,12},{8,0},{12,4},{16,24},{20,28},{24,16},{28,20},{1,9},{5... | collective-permute-start | bytes 3145736 | tf_op jit(solution)/shard_map/ppermute | solution.py:848
  378.2 49.0 %collective-permute-start.35 = (bf16[2,4,128,512]{3,2,1,0:T(8,128)(2,1)}, bf16[2,4,128,512]{3,2,1,0:T(8,128)(2,1)}, u32[]{:S(2)}, u32[]{:S(2)}) collective-permute-start(bf16[2,4,128,512]{3,2,1,0:T(8,128)(2,1)} %get-tuple-element.260), channel_id=1, source_target_pairs={{0,16},{4,20},{8,24},{12,28},{16,0},{20,4},{24,8},{28,12},{1,17},{... | collective-permute-start | bytes 3145736 | tf_op jit(solution)/shard_map/ppermute | solution.py:848
  380.5 48.7 %collective-permute-start.36 = (bf16[2,4,128,512]{3,2,1,0:T(8,128)(2,1)}, bf16[2,4,128,512]{3,2,1,0:T(8,128)(2,1)S(1)}, u32[]{:S(2)}, u32[]{:S(2)}) collective-permute-start(bf16[2,4,128,512]{3,2,1,0:T(8,128)(2,1)} %get-tuple-element.258), channel_id=1, source_target_pairs={{0,8},{4,12},{8,0},{12,4},{16,24},{20,28},{24,16},{28,20},{1,9},{5... | collective-permute-start | bytes 3145736 | tf_op jit(solution)/shard_map/ppermute | solution.py:848
  470.5 31.8 %collective-permute-start.37 = (bf16[4,4,2,128,256]{4,3,2,1,0:T(8,128)(2,1)}, bf16[4,4,2,128,256]{4,3,2,1,0:T(8,128)(2,1)}, u32[]{:S(2)}, u32[]{:S(2)}) collective-permute-start(bf16[4,4,2,128,256]{4,3,2,1,0:T(8,128)(2,1)} %get-tuple-element.120), channel_id=1, source_target_pairs={{0,4},{4,0},{8,12},{12,8},{16,20},{20,16},{24,28},{28,24},{1,5},{5... | collective-permute-start | bytes 6291464 | tf_op jit(solution)/shard_map/ppermute | solution.py:848
  470.6 15.1 %collective-permute-start.48 = (bf16[4,128,512]{2,1,0:T(8,128)(2,1)}, bf16[4,128,512]{2,1,0:T(8,128)(2,1)}, u32[]{:S(2)}, u32[]{:S(2)}) collective-permute-start(bf16[4,128,512]{2,1,0:T(8,128)(2,1)} %fusion.35), channel_id=1, source_target_pairs={{0,16},{4,20},{8,24},{12,28},{16,0},{20,4},{24,8},{28,12},{1,17},{... | collective-permute-start | bytes 1572872 | tf_op jit(solution)/shard_map/ppermute | solution.py:848
  473.9 31.6 %collective-permute-start.38 = (bf16[4,4,2,128,256]{4,3,1,0,2:T(8,128)(2,1)}, bf16[4,4,2,128,256]{4,3,1,0,2:T(8,128)(2,1)}, u32[]{:S(2)}, u32[]{:S(2)}) collective-permute-start(bf16[4,4,2,128,256]{4,3,1,0,2:T(8,128)(2,1)} %pad_maximum_fusion.8), channel_id=1, source_target_pairs={{0,4},{4,0},{8,12},{12,8},{16,20},{20,16},{24,28},{28,24},{1,5},{5... | collective-permute-start | bytes 6291464 | tf_op jit(solution)/shard_map/ppermute | solution.py:848
  474.1 15.1 %collective-permute-start.47 = (bf16[4,128,512]{2,1,0:T(8,128)(2,1)}, bf16[4,128,512]{2,1,0:T(8,128)(2,1)}, u32[]{:S(2)}, u32[]{:S(2)}) collective-permute-start(bf16[4,128,512]{2,1,0:T(8,128)(2,1)} %fusion.29), channel_id=1, source_target_pairs={{0,8},{4,12},{8,0},{12,4},{16,24},{20,28},{24,16},{28,20},{1,9},{5... | collective-permute-start | bytes 1572872 | tf_op jit(solution)/shard_map/ppermute | solution.py:848
  476.2 20.2 %collective-permute-start.50 = (bf16[4,128,512]{2,1,0:T(8,128)(2,1)}, bf16[4,128,512]{2,1,0:T(8,128)(2,1)}, u32[]{:S(2)}, u32[]{:S(2)}) collective-permute-start(bf16[4,128,512]{2,1,0:T(8,128)(2,1)} %fusion.34), channel_id=1, source_target_pairs={{0,16},{4,20},{8,24},{12,28},{16,0},{20,4},{24,8},{28,12},{1,17},{... | collective-permute-start | bytes 1572872 | tf_op jit(solution)/shard_map/ppermute | solution.py:848
  485.7 14.1 %collective-permute-start.49 = (bf16[4,128,512]{2,1,0:T(8,128)(2,1)}, bf16[4,128,512]{2,1,0:T(8,128)(2,1)}, u32[]{:S(2)}, u32[]{:S(2)}) collective-permute-start(bf16[4,128,512]{2,1,0:T(8,128)(2,1)} %fusion.28), channel_id=1, source_target_pairs={{0,8},{4,12},{8,0},{12,4},{16,24},{20,28},{24,16},{28,20},{1,9},{5... | collective-permute-start | bytes 1572872 | tf_op jit(solution)/shard_map/ppermute | solution.py:848
  491.6 111.3 %all-reduce.7.cloned.1.call-start = ((), (), s32[]{:S(2)}) async-start(), calls=%async_computation.3 | async-start | bytes 2097152
  507.5 44.9 %collective-permute-start.41 = (bf16[2,4,2,128,256]{4,3,2,1,0:T(8,128)(2,1)}, bf16[2,4,2,128,256]{4,3,2,1,0:T(8,128)(2,1)}, u32[]{:S(2)}, u32[]{:S(2)}) collective-permute-start(bf16[2,4,2,128,256]{4,3,2,1,0:T(8,128)(2,1)} %get-tuple-element.256), channel_id=1, source_target_pairs={{0,16},{4,20},{8,24},{12,28},{16,0},{20,4},{24,8},{28,12},{1,17},{... | collective-permute-start | bytes 3145736 | tf_op jit(solution)/shard_map/ppermute | solution.py:848
  510.9 43.4 %collective-permute-start.42 = (bf16[2,4,2,128,256]{4,3,2,1,0:T(8,128)(2,1)}, bf16[2,4,2,128,256]{4,3,2,1,0:T(8,128)(2,1)}, u32[]{:S(2)}, u32[]{:S(2)}) collective-permute-start(bf16[2,4,2,128,256]{4,3,2,1,0:T(8,128)(2,1)} %get-tuple-element.266), channel_id=1, source_target_pairs={{0,8},{4,12},{8,0},{12,4},{16,24},{20,28},{24,16},{28,20},{1,9},{5... | collective-permute-start | bytes 3145736 | tf_op jit(solution)/shard_map/ppermute | solution.py:848
  531.2 14.3 %collective-permute-start.39 = (bf16[1,2,1024]{2,1,0:T(2,128)(2,1)S(1)}, bf16[1,2,1024]{2,1,0:T(2,128)(2,1)S(1)}, u32[]{:S(2)}, u32[]{:S(2)}) collective-permute-start(bf16[1,2,1024]{2,1,0:T(2,128)(2,1)S(1)} %bitcast.370), channel_id=1, source_target_pairs={{0,1},{1,0},{2,3},{3,2},{4,5},{5,4},{6,7},{7,6},{8,9},{9,8},{10,11... | collective-permute-start | bytes 12296 | tf_op jit(solution)/shard_map/ppermute | solution.py:848
  545.5 6.2 collective-permute-start.40
  568.8 5.7 collective-permute-start.55
  570.4 9.9 %collective-permute-start.51 = (bf16[8,8,1024]{2,1,0:T(8,128)(2,1)S(1)}, bf16[8,8,1024]{2,1,0:T(8,128)(2,1)S(1)}, u32[]{:S(2)}, u32[]{:S(2)}) collective-permute-start(bf16[8,8,1024]{2,1,0:T(8,128)(2,1)S(1)} %get-tuple-element.306), channel_id=1, source_target_pairs={{0,8},{4,12},{8,0},{12,4},{16,24},{20,28},{24,16},{28,20},{1,9},{5... | collective-permute-start | bytes 393224 | tf_op jit(solution)/shard_map/ppermute | solution.py:848
  574.5 5.7 collective-permute-start.56
  576.0 32.4 %collective-permute-start.44 = (bf16[4,2,128,256]{3,2,1,0:T(8,128)(2,1)}, bf16[4,2,128,256]{3,2,1,0:T(8,128)(2,1)}, u32[]{:S(2)}, u32[]{:S(2)}) collective-permute-start(bf16[4,2,128,256]{3,2,1,0:T(8,128)(2,1)} %fusion.36), channel_id=1, source_target_pairs={{0,16},{4,20},{8,24},{12,28},{16,0},{20,4},{24,8},{28,12},{1,17},{... | collective-permute-start | bytes 1572872 | tf_op jit(solution)/shard_map/ppermute | solution.py:848
  580.3 9.8 %collective-permute-start.57 = (f32[18,1024]{1,0:T(8,128)S(1)}, f32[18,1024]{1,0:T(8,128)S(1)}, u32[]{:S(2)}, u32[]{:S(2)}) collective-permute-start(f32[18,1024]{1,0:T(8,128)S(1)} %add.317), channel_id=1, source_target_pairs={{0,1},{1,0},{2,3},{3,2},{4,5},{5,4},{6,7},{7,6},{8,9},{9,8},{10,11... | collective-permute-start | bytes 221192 | tf_op jit(solution)/shard_map/ppermute | solution.py:848
  580.4 27.8 %collective-permute-start.52 = (bf16[2,8,8,1024]{3,2,1,0:T(8,128)(2,1)S(1)}, bf16[2,8,8,1024]{3,2,1,0:T(8,128)(2,1)S(1)}, u32[]{:S(2)}, u32[]{:S(2)}) collective-permute-start(bf16[2,8,8,1024]{3,2,1,0:T(8,128)(2,1)S(1)} %get-tuple-element.304), channel_id=1, source_target_pairs={{0,16},{4,20},{8,24},{12,28},{16,0},{20,4},{24,8},{28,12},{1,17},{... | collective-permute-start | bytes 786440 | tf_op jit(solution)/shard_map/ppermute | solution.py:848
  590.1 16.8 %collective-permute-start.58 = (f32[18,1024]{1,0:T(8,128)S(1)}, f32[18,1024]{1,0:T(8,128)}, u32[]{:S(2)}, u32[]{:S(2)}) collective-permute-start(f32[18,1024]{1,0:T(8,128)S(1)} %add.318), channel_id=1, source_target_pairs={{0,2},{1,3},{2,0},{3,1},{4,6},{5,7},{6,4},{7,5},{8,10},{9,11},{10,... | collective-permute-start | bytes 221192 | tf_op jit(solution)/shard_map/ppermute | solution.py:848
  604.5 14.0 %collective-permute-start.43 = (bf16[4,2,128,256]{3,2,1,0:T(8,128)(2,1)}, bf16[4,2,128,256]{3,2,1,0:T(8,128)(2,1)S(1)}, u32[]{:S(2)}, u32[]{:S(2)}) collective-permute-start(bf16[4,2,128,256]{3,2,1,0:T(8,128)(2,1)} %fusion.30), channel_id=1, source_target_pairs={{0,8},{4,12},{8,0},{12,4},{16,24},{20,28},{24,16},{28,20},{1,9},{5... | collective-permute-start | bytes 1572872 | tf_op jit(solution)/shard_map/ppermute | solution.py:848
  608.3 12.1 %collective-permute-start.53 = (bf16[4,8,8,1024]{3,2,0,1:T(8,128)(2,1)S(1)}, bf16[4,8,8,1024]{3,2,0,1:T(8,128)(2,1)S(1)}, u32[]{:S(2)}, u32[]{:S(2)}) collective-permute-start(bf16[4,8,8,1024]{3,2,0,1:T(8,128)(2,1)S(1)} %copy.151), channel_id=1, source_target_pairs={{0,4},{4,0},{8,12},{12,8},{16,20},{20,16},{24,28},{28,24},{1,5},{5... | collective-permute-start | bytes 1572872 | tf_op jit(solution)/shard_map/ppermute | solution.py:848
  620.3 12.9 %collective-permute-start.45 = (bf16[2,4,128,256]{3,1,2,0:T(4,128)(2,1)S(1)}, bf16[2,4,128,256]{3,1,2,0:T(4,128)(2,1)S(1)}, u32[]{:S(2)}, u32[]{:S(2)}) collective-permute-start(bf16[2,4,128,256]{3,1,2,0:T(4,128)(2,1)S(1)} %bitcast.362), channel_id=1, source_target_pairs={{0,1},{1,0},{2,3},{3,2},{4,5},{5,4},{6,7},{7,6},{8,9},{9,8},{10,11... | collective-permute-start | bytes 1572872 | tf_op jit(solution)/shard_map/ppermute | solution.py:848
  634.6 13.0 %collective-permute-start.46 = (bf16[4,128,256]{2,0,1:T(4,128)(2,1)}, bf16[4,128,256]{2,0,1:T(4,128)(2,1)S(1)}, u32[]{:S(2)}, u32[]{:S(2)}) collective-permute-start(bf16[4,128,256]{2,0,1:T(4,128)(2,1)} %dynamic-slice_bitcast_fusion.2), channel_id=1, source_target_pairs={{0,2},{1,3},{2,0},{3,1},{4,6},{5,7},{6,4},{7,5},{8,10},{9,11},{10,... | collective-permute-start | bytes 786440 | tf_op jit(solution)/shard_map/ppermute | solution.py:848
  652.7 3.6 collective-permute-start.60
  660.0 9.9 %collective-permute-start.62 = (f32[8,128]{1,0:T(8,128)S(1)}, f32[8,128]{1,0:T(8,128)S(1)}, u32[]{:S(2)}, u32[]{:S(2)}) collective-permute-start(f32[8,128]{1,0:T(8,128)S(1)} %add.324), channel_id=1, source_target_pairs={{0,1},{1,0},{2,3},{3,2},{4,5},{5,4},{6,7},{7,6},{8,9},{9,8},{10,11... | collective-permute-start | bytes 12296 | tf_op jit(solution)/shard_map/ppermute | solution.py:848
  669.9 11.4 %collective-permute-start.63 = (f32[8,128]{1,0:T(8,128)S(1)}, f32[8,128]{1,0:T(8,128)S(1)}, u32[]{:S(2)}, u32[]{:S(2)}) collective-permute-start(f32[8,128]{1,0:T(8,128)S(1)} %add.325), channel_id=1, source_target_pairs={{0,2},{1,3},{2,0},{3,1},{4,6},{5,7},{6,4},{7,5},{8,10},{9,11},{10,... | collective-permute-start | bytes 12296 | tf_op jit(solution)/shard_map/ppermute | solution.py:848
  (56 other events, 631.7 us)
Sparse Core Ops, SparseCore 0:
  10.2 30.6 all-gather.4
  43.0 45.4 all-gather.6
  491.8 52.0 all-reduce.4
  546.7 56.1 all-reduce.6
